TPU v7x, 32 devices: a whole 2x2x4 slice. The times are simulated.
32 devices in a mesh: replica: 8 (over z, x), group: 4 (over y, core).
Axes of the slice: x: 2, y: 2, z: 4, core: 2. Of those that a mesh axis runs over, the one named last changes fastest.
Arguments:
- hidden_in: bfloat16 [16, 1024, 1024], P('replica', 'group'), may hold values from -6 to 6
- segments: int32 [16, 1024], P('replica', 'group'), may hold values from 0 to 63, as said below
- positions: int32 [16, 1024], P('replica', 'group'), may hold values from 0 to 2047, as said below
- out_grad: bfloat16 [16, 1024, 1024], P('replica', 'group'), may hold values from -6 to 6
- attn_gain: bfloat16 [1024], P('group'), may hold values from 0.099609375 to 1.8984375
- w_query: bfloat16 [1024, 1024], P('group'), may hold values from -0.1875 to 0.1875
- w_key: bfloat16 [1024, 512], P('group'), may hold values from -0.1875 to 0.1875
- w_value: bfloat16 [1024, 512], P('group'), may hold values from -0.1875 to 0.1875
- query_gain: bfloat16 [64], replicated, may hold values from 0.099609375 to 1.8984375
- key_gain: bfloat16 [64], replicated, may hold values from 0.099609375 to 1.8984375
- w_out: bfloat16 [1024, 1024], P('group'), may hold values from -0.75 to 0.75
- ffn_gain: bfloat16 [1024], P('group'), may hold values from 0.099609375 to 1.8984375
- w_gate: bfloat16 [1024, 4608], P('group'), may hold values from -0.1875 to 0.1875
- w_up: bfloat16 [1024, 4608], P('group'), may hold values from -0.1875 to 0.1875
- w_down: bfloat16 [4608, 1024], P('group'), may hold values from -0.09375 to 0.09375
Outputs:
- block_out: bfloat16 [16, 1024, 1024], P('replica', 'group')
- input_grad: float32 [16, 1024, 1024], P('replica', 'group')
- attn_gain_grad: float32 [1024], P('group')
- w_query_grad: float32 [1024, 1024], P('group')
- w_key_grad: float32 [1024, 512], P('group')
- w_value_grad: float32 [1024, 512], P('group')
- query_gain_grad: float32 [64], replicated
- key_gain_grad: float32 [64], replicated
- w_out_grad: float32 [1024, 1024], P('group')
- ffn_gain_grad: float32 [1024], P('group')
- w_gate_grad: float32 [1024, 4608], P('group')
- w_up_grad: float32 [1024, 4608], P('group')
- w_down_grad: float32 [4608, 1024], P('group')
Inputs may be any that keep to these rules, and one draw needn't show every extreme that they name: `segments`: within a sequence the document numbers start at 0, never fall and grow by at most one from token to token, so that each document is a run of consecutive tokens; some sequence reaches the most. Within a document the positions rise by one from token to token; later documents of a sequence start at 0, the first one may continue a document of an earlier pack.
All inputs are finite; a program needn't handle non-finite values.
Results may differ from a plain program's by a relative error of at most 0.015.
Values may be sent and summed in bfloat16 or wider, within the bound.
No kernel may reach another device: no remote copies, remote signals or barrier semaphores. Data moves between devices by JAX's collectives and lax.ppermute only.
A program may use at most 256 MiB of HBM per device.

v0:
```python
import jax
import jax.numpy as jnp
from jax import lax
from jax.sharding import PartitionSpec as P

HQ = 16
KV = 8
HD = 64


EPS = 1e-05
THETA = 1000000.0
NEG = -1e30


def norm_rows(inputs):
    inv_scale = lax.rsqrt(jnp.mean(inputs * inputs, -1, keepdims=True) + EPS)
    return (inputs * inv_scale, inv_scale)


def norm_back(grad_normed, normed, inv_scale):
    return inv_scale * (grad_normed - normed * jnp.mean(grad_normed * normed, -1, keepdims=True))


def rope_tables(places, head_size):
    half_size = head_size // 2
    freq_table = THETA ** (-(jnp.arange(half_size, dtype=jnp.float32) * 2.0 / head_size))
    angle = places.astype(jnp.float32)[..., None] * freq_table
    return (jnp.cos(angle), jnp.sin(angle))


def rotate(heads, cosine, sine_table):
    half_size = heads.shape[-1] // 2
    first_half = heads[..., :half_size]
    second_half = heads[..., half_size:]
    cos_col = cosine[..., None, :]
    sin_col = sine_table[..., None, :]
    return jnp.concatenate(
        [
            first_half * cos_col - second_half * sin_col,
            second_half * cos_col + first_half * sin_col,
        ],
        -1,
    )


def unrotate(grads, cosine, sine_table):
    half_size = grads.shape[-1] // 2
    first_half = grads[..., :half_size]
    second_half = grads[..., half_size:]
    cos_col = cosine[..., None, :]
    sin_col = sine_table[..., None, :]
    return jnp.concatenate(
        [
            first_half * cos_col + second_half * sin_col,
            second_half * cos_col - first_half * sin_col,
        ],
        -1,
    )


def scores_of(queries, key_all, seg_query, seg_key, first_row):
    query_count = queries.shape[0]
    length = key_all.shape[0]
    grouped = queries.reshape(query_count, KV, HQ // KV, HD)
    key_heads = key_all.reshape(length, KV, HD)
    raw_scores = jnp.einsum(
        "tkgd,jkd->kgtj", grouped, key_heads, preferred_element_type=jnp.float32
    ) * HD ** (-0.5)
    query_place = first_row + jnp.arange(query_count)
    visible = (seg_query[:, None] == seg_key[None, :]) & (
        jnp.arange(length)[None, :] <= query_place[:, None]
    )
    return (grouped, key_heads, raw_scores, visible)


def attend(queries, key_all, value_all, seg_query, seg_key, first_row):
    grouped, key_heads, raw_scores, visible = scores_of(
        queries, key_all, seg_query, seg_key, first_row
    )
    value_heads = value_all.reshape(key_all.shape[0], KV, HD)
    masked = jnp.where(visible, raw_scores, NEG)
    row_max = jnp.max(masked, -1, keepdims=True)
    weights = jnp.exp(masked - row_max)
    total = jnp.sum(weights, -1, keepdims=True)
    prob_low = (weights / total).astype(jnp.bfloat16)
    mixed_heads = jnp.einsum(
        "kgtj,jkd->tkgd", prob_low, value_heads, preferred_element_type=jnp.float32
    )
    return (mixed_heads.reshape(queries.shape[0], HQ * HD), row_max + jnp.log(total))


def attend_back(queries, key_all, value_all, seg_query, seg_key, first_row, log_total, grad_mixed):
    grouped, key_heads, raw_scores, visible = scores_of(
        queries, key_all, seg_query, seg_key, first_row
    )
    length = key_all.shape[0]
    value_heads = value_all.reshape(length, KV, HD)
    probs = jnp.where(visible, jnp.exp(raw_scores - log_total), 0.0)
    grad_heads = grad_mixed.reshape(queries.shape[0], KV, HQ // KV, HD)
    grad_probs = jnp.einsum(
        "tkgd,jkd->kgtj", grad_heads, value_heads, preferred_element_type=jnp.float32
    )
    row_inner = jnp.sum(probs * grad_probs, -1, keepdims=True)
    grad_scores = (probs * (grad_probs - row_inner)).astype(jnp.bfloat16)
    grad_query = jnp.einsum(
        "kgtj,jkd->tkgd", grad_scores, key_heads, preferred_element_type=jnp.float32
    ) * HD ** (-0.5)
    grad_key = jnp.einsum(
        "kgtj,tkgd->jkd", grad_scores, grouped, preferred_element_type=jnp.float32
    ) * HD ** (-0.5)
    grad_value = jnp.einsum(
        "kgtj,tkgd->jkd", probs.astype(jnp.bfloat16), grad_heads, preferred_element_type=jnp.float32
    )
    return (
        grad_query.reshape(queries.shape[0], HQ, HD),
        grad_key.reshape(length, KV * HD),
        grad_value.reshape(length, KV * HD),
    )


def spread_columns(values, groups, copies):
    row_count, columns = values.shape
    return (
        values.reshape(row_count, groups, copies, columns // (groups * copies))
        .transpose(0, 2, 1, 3)
        .reshape(row_count, columns)
    )


def outer_sum(left, right):
    return lax.dot_general(
        left, right, (((0,), (0,)), ((), ())), preferred_element_type=jnp.float32
    )


def per_device(
    hidden_in,
    segments,
    positions,
    out_grad,
    attn_gain,
    w_query,
    w_key,
    w_value,
    query_gain,
    key_gain,
    w_out,
    ffn_gain,
    w_gate,
    w_up,
    w_down,
):
    groups = lax.axis_size("group")
    copies = lax.axis_size("replica")
    member = lax.axis_index("group")
    seq_count, span_rows, model_width = hidden_in.shape
    token_count = seq_count * span_rows
    first_row = member * span_rows
    full_query, full_key, full_value, full_out, full_gain = (
        lax.all_gather(w_query, "group", axis=0, tiled=True),
        lax.all_gather(w_key, "group", axis=0, tiled=True),
        lax.all_gather(w_value, "group", axis=0, tiled=True),
        lax.all_gather(w_out, "group", axis=0, tiled=True),
        lax.all_gather(attn_gain, "group", axis=0, tiled=True),
    )
    inputs = hidden_in.reshape(token_count, model_width).astype(jnp.float32)
    normed_one, inv_one = norm_rows(inputs)
    gain_one = full_gain.astype(jnp.float32)
    hidden_one = (normed_one * gain_one).astype(jnp.bfloat16)
    query_raw = jnp.dot(hidden_one, full_query, preferred_element_type=jnp.float32)
    key_raw = jnp.dot(hidden_one, full_key, preferred_element_type=jnp.float32)
    value_low = jnp.dot(hidden_one, full_value, preferred_element_type=jnp.float32).astype(
        jnp.bfloat16
    )
    cosine, sine_table = rope_tables(positions.reshape(token_count), HD)
    query_scale = query_gain.astype(jnp.float32)
    key_scale = key_gain.astype(jnp.float32)
    query_normed, query_inv = norm_rows(query_raw.reshape(token_count, HQ, HD))
    key_normed, key_inv = norm_rows(key_raw.reshape(token_count, KV, HD))
    query_rot = rotate(query_normed * query_scale, cosine, sine_table).astype(jnp.bfloat16)
    key_rot = rotate(key_normed * key_scale, cosine, sine_table).astype(jnp.bfloat16)
    key_all, value_all = (
        lax.all_gather(key_rot.reshape(seq_count, span_rows, KV * HD), "group", axis=1, tiled=True),
        lax.all_gather(
            value_low.reshape(seq_count, span_rows, KV * HD), "group", axis=1, tiled=True
        ),
    )
    seg_all = lax.all_gather(segments, "group", axis=1, tiled=True)
    query_seqs = query_rot.reshape(seq_count, span_rows, HQ, HD)

    def forward_one(sequence):
        queries, keys_seq, values_seq, seg_query, seg_key = sequence
        return attend(
            queries.reshape(span_rows, HQ * HD), keys_seq, values_seq, seg_query, seg_key, first_row
        )

    mixed_heads, log_total = lax.map(
        forward_one, (query_seqs, key_all, value_all, segments, seg_all)
    )
    mixed_low = mixed_heads.reshape(token_count, HQ * HD).astype(jnp.bfloat16)
    middle = inputs + jnp.dot(mixed_low, full_out, preferred_element_type=jnp.float32)
    normed_two, inv_two = norm_rows(middle)
    full_gate, full_up, full_down, full_ffn_gain = (
        lax.all_gather(w_gate, "group", axis=0, tiled=True),
        lax.all_gather(w_up, "group", axis=0, tiled=True),
        lax.all_gather(w_down, "group", axis=0, tiled=True),
        lax.all_gather(ffn_gain, "group", axis=0, tiled=True),
    )
    gain_two = full_ffn_gain.astype(jnp.float32)
    hidden_two = (normed_two * gain_two).astype(jnp.bfloat16)
    gate_raw = jnp.dot(hidden_two, full_gate, preferred_element_type=jnp.float32)
    upward = jnp.dot(hidden_two, full_up, preferred_element_type=jnp.float32)
    act_low = (jax.nn.silu(gate_raw) * upward).astype(jnp.bfloat16)
    result = middle + jnp.dot(act_low, full_down, preferred_element_type=jnp.float32)
    block_out = result.astype(jnp.bfloat16).reshape(seq_count, span_rows, model_width)
    grad_out = out_grad.reshape(token_count, model_width)
    grad_act = jnp.dot(grad_out, full_down.T, preferred_element_type=jnp.float32)
    sig_gate = jax.nn.sigmoid(gate_raw)
    grad_gate = (grad_act * upward * sig_gate * (1.0 + gate_raw * (1.0 - sig_gate))).astype(
        jnp.bfloat16
    )
    grad_up = (grad_act * gate_raw * sig_gate).astype(jnp.bfloat16)
    grad_hidden_two = jnp.dot(grad_gate, full_gate.T, preferred_element_type=jnp.float32) + jnp.dot(
        grad_up, full_up.T, preferred_element_type=jnp.float32
    )
    gain_two_grad = jnp.sum(grad_hidden_two * normed_two, 0)
    grad_middle = grad_out.astype(jnp.float32) + norm_back(
        grad_hidden_two * gain_two, normed_two, inv_two
    )
    grad_branch = grad_middle.astype(jnp.bfloat16)
    grad_mixed = jnp.dot(grad_branch, full_out.T, preferred_element_type=jnp.float32).astype(
        jnp.bfloat16
    )

    def backward_one(sequence):
        queries, keys_seq, values_seq, seg_query, seg_key, log_seq, grad_seq = sequence
        return attend_back(
            queries.reshape(span_rows, HQ * HD),
            keys_seq,
            values_seq,
            seg_query,
            seg_key,
            first_row,
            log_seq,
            grad_seq,
        )

    grad_query, key_part, value_part = lax.map(
        backward_one,
        (
            query_seqs,
            key_all,
            value_all,
            segments,
            seg_all,
            log_total,
            grad_mixed.reshape(seq_count, span_rows, HQ * HD),
        ),
    )
    grad_key_own, grad_value_own = (
        lax.psum_scatter(
            key_part.astype(jnp.bfloat16), "group", scatter_dimension=1, tiled=True
        ).astype(jnp.float32),
        lax.psum_scatter(
            value_part.astype(jnp.bfloat16), "group", scatter_dimension=1, tiled=True
        ).astype(jnp.float32),
    )
    grad_query_norm = unrotate(grad_query.reshape(token_count, HQ, HD), cosine, sine_table)
    query_gain_part = jnp.sum(grad_query_norm * query_normed, (0, 1))
    grad_query_raw = (
        norm_back(grad_query_norm * query_scale, query_normed, query_inv)
        .reshape(token_count, HQ * HD)
        .astype(jnp.bfloat16)
    )
    grad_key_norm = unrotate(grad_key_own.reshape(token_count, KV, HD), cosine, sine_table)
    key_gain_part = jnp.sum(grad_key_norm * key_normed, (0, 1))
    grad_key_raw = (
        norm_back(grad_key_norm * key_scale, key_normed, key_inv)
        .reshape(token_count, KV * HD)
        .astype(jnp.bfloat16)
    )
    grad_value_low = grad_value_own.reshape(token_count, KV * HD).astype(jnp.bfloat16)
    grad_hidden_one = jnp.dot(grad_query_raw, full_query.T, preferred_element_type=jnp.float32)
    grad_hidden_one = grad_hidden_one + jnp.dot(
        grad_key_raw, full_key.T, preferred_element_type=jnp.float32
    )
    grad_hidden_one = grad_hidden_one + jnp.dot(
        grad_value_low, full_value.T, preferred_element_type=jnp.float32
    )
    gain_one_grad = jnp.sum(grad_hidden_one * normed_one, 0)
    grad_input = grad_middle + norm_back(grad_hidden_one * gain_one, normed_one, inv_one)
    input_grad = grad_input.reshape(seq_count, span_rows, model_width)
    query_gain_grad, key_gain_grad = lax.psum(
        (query_gain_part, key_gain_part), ("replica", "group")
    )
    left_one = spread_columns(hidden_one, groups, copies)
    left_mix = spread_columns(mixed_low, groups, copies)
    left_two = spread_columns(hidden_two, groups, copies)
    left_act = spread_columns(act_low, groups, copies)
    gain_one_vec = spread_columns(gain_one_grad[None, :], groups, copies)[0]
    gain_two_vec = spread_columns(gain_two_grad[None, :], groups, copies)[0]
    partials = (
        gain_one_vec,
        outer_sum(left_one, grad_query_raw),
        outer_sum(left_one, grad_key_raw),
        outer_sum(left_one, grad_value_low),
        outer_sum(left_mix, grad_branch),
        gain_two_vec,
        outer_sum(left_two, grad_gate),
        outer_sum(left_two, grad_up),
        outer_sum(left_act, grad_out),
    )
    shares = (
        lax.psum_scatter(partials[0], ("replica", "group"), scatter_dimension=0, tiled=True),
        lax.psum_scatter(partials[1], ("replica", "group"), scatter_dimension=0, tiled=True),
        lax.psum_scatter(partials[2], ("replica", "group"), scatter_dimension=0, tiled=True),
        lax.psum_scatter(partials[3], ("replica", "group"), scatter_dimension=0, tiled=True),
        lax.psum_scatter(partials[4], ("replica", "group"), scatter_dimension=0, tiled=True),
        lax.psum_scatter(partials[5], ("replica", "group"), scatter_dimension=0, tiled=True),
        lax.psum_scatter(partials[6], ("replica", "group"), scatter_dimension=0, tiled=True),
        lax.psum_scatter(partials[7], ("replica", "group"), scatter_dimension=0, tiled=True),
        lax.psum_scatter(partials[8], ("replica", "group"), scatter_dimension=0, tiled=True),
    )
    totals = (
        lax.all_gather(shares[0].astype(jnp.bfloat16), "replica", axis=0, tiled=True).astype(
            jnp.float32
        ),
        lax.all_gather(shares[1].astype(jnp.bfloat16), "replica", axis=0, tiled=True).astype(
            jnp.float32
        ),
        lax.all_gather(shares[2].astype(jnp.bfloat16), "replica", axis=0, tiled=True).astype(
            jnp.float32
        ),
        lax.all_gather(shares[3].astype(jnp.bfloat16), "replica", axis=0, tiled=True).astype(
            jnp.float32
        ),
        lax.all_gather(shares[4].astype(jnp.bfloat16), "replica", axis=0, tiled=True).astype(
            jnp.float32
        ),
        lax.all_gather(shares[5].astype(jnp.bfloat16), "replica", axis=0, tiled=True).astype(
            jnp.float32
        ),
        lax.all_gather(shares[6].astype(jnp.bfloat16), "replica", axis=0, tiled=True).astype(
            jnp.float32
        ),
        lax.all_gather(shares[7].astype(jnp.bfloat16), "replica", axis=0, tiled=True).astype(
            jnp.float32
        ),
        lax.all_gather(shares[8].astype(jnp.bfloat16), "replica", axis=0, tiled=True).astype(
            jnp.float32
        ),
    )
    (
        attn_gain_grad,
        w_query_grad,
        w_key_grad,
        w_value_grad,
        w_out_grad,
        ffn_gain_grad,
        w_gate_grad,
        w_up_grad,
        w_down_grad,
    ) = totals
    return (
        block_out,
        input_grad,
        attn_gain_grad,
        w_query_grad,
        w_key_grad,
        w_value_grad,
        query_gain_grad,
        key_gain_grad,
        w_out_grad,
        ffn_gain_grad,
        w_gate_grad,
        w_up_grad,
        w_down_grad,
    )


def solution(mesh):
    placed = (
        P("replica", "group", None),
        P("replica", "group"),
        P("replica", "group"),
        P("replica", "group", None),
        P("group"),
        P("group", None),
        P("group", None),
        P("group", None),
        P(),
        P(),
        P("group", None),
        P("group"),
        P("group", None),
        P("group", None),
        P("group", None),
    )
    return jax.shard_map(
        per_device,
        mesh=mesh,
        in_specs=placed,
        out_specs=(
            P("replica", "group", None),
            P("replica", "group", None),
            P("group"),
            P("group", None),
            P("group", None),
            P("group", None),
            P(),
            P(),
            P("group", None),
            P("group"),
            P("group", None),
            P("group", None),
            P("group", None),
        ),
        check_vma=False,
    )
```

profile of v0, /device:TPU:0, one launch (start us, length us, event | category | flops | bytes accessed | tf_op | source)
XLA Modules:
  0.0 1943.8 jit_solution(17396402424499055007)
XLA Ops:
  18.2 10.8 all-gather.15.cloned.1.call-done
  32.8 14.6 all-gather.19.cloned.1.call-done
  79.2 17.3 all-gather.17.cloned.1.call-done
  96.5 24.8 %all-gather.21.cloned.1.call-done = bf16[2,1024,512]{1,2,0:T(8,128)(2,1)} async-done(((bf16[2,256,512]{1,2,0:T(8,128)(2,1)}), bf16[2,1024,512]{1,2,0:T(8,128)(2,1)}) %all-gather.21.cloned.1.call-update) | async-done | bytes 2097168 | tf_op jit(solution)/shard_map/all_gather | solution.py:184
  121.3 59.3 %while.26 = (s32[]{:T(128)}, bf16[2,256,1024]{2,1,0:T(8,128)(2,1)S(1)}, f32[2,8,2,256,1]{3,2,1,4,0:T(2,128)}, bf16[2,1024,512]{1,2,0:T(8,128)(2,1)}, s32[2,256]{...) while((s32[]{:T(128)}, ...), condition=%wide.region_6.7_spmd, body=%wide.region_3.6_spmd.sunk | while | flops 1124856064 | bytes 62014600 | solution.py:198
  124.5 7.5 fusion.122
  132.0 9.2 fusion.123
  141.2 8.1 fusion.124
  153.4 8.9 fusion.122
  162.3 9.2 fusion.123
  171.5 8.2 fusion.124
  185.5 25.7 %all-gather.27.cloned.1.call-done = bf16[1024,4608]{1,0:T(8,128)(2,1)} async-done(((bf16[256,4608]{1,0:T(8,128)(2,1)}), bf16[1024,4608]{1,0:T(8,128)(2,1)}) %all-gather.27.cloned.1.call-update) | async-done | bytes 9437200 | tf_op jit(solution)/shard_map/all_gather | solution.py:205
  211.2 11.8 fusion.33
  222.9 54.1 %all-gather.29.cloned.1.call-done = bf16[1024,4608]{1,0:T(8,128)(2,1)} async-done(((bf16[256,4608]{1,0:T(8,128)(2,1)}), bf16[1024,4608]{1,0:T(8,128)(2,1)}) %all-gather.29.cloned.1.call-update) | async-done | bytes 9437200 | tf_op jit(solution)/shard_map/all_gather | solution.py:206
  277.0 11.3 fusion.34
  288.3 54.5 %all-gather.31.cloned.1.call-done = bf16[4608,1024]{1,0:T(8,128)(2,1)} async-done(((bf16[1152,1024]{1,0:T(8,128)(2,1)}), bf16[4608,1024]{1,0:T(8,128)(2,1)}) %all-gather.31.cloned.1.call-update) | async-done | bytes 9437200 | tf_op jit(solution)/shard_map/all_gather | solution.py:207
  342.9 20.4 %multiply_convert_fusion = (bf16[512,4608]{1,0:T(8,128)(2,1)}, bf16[512,4608]{1,0:T(8,128)(2,1)}, bf16[512,4608]{1,0:T(8,128)(2,1)}) fusion(f32[512,4608]{1,0:T(8,128)} %fusion.33, f32[512,4608]{1,0:T(8,128)} %fusion.34, bf16[512,1024]{1,0:T(8,128)(2,1)S(1)} %bitcast.314, bf16[4608,1024]{1,0:T(8,128)(2,1)} %all-gather.31.cloned.1.call-done), kind=kOutput, calls=%fused_computation.42 | convolution fusion | flops 4869586944 | bytes 43515904 | tf_op jit(solution)/shard_map/dot_general | solution.py:218
  363.3 9.2 fusion.35
  372.5 8.6 multiply_reduce_fusion
  384.9 134.0 %while.27 = (s32[]{:T(128)}, f32[2,256,16,64]{1,0,3,2:T(2,128)}, bf16[2,1024,512]{1,2,0:T(8,128)(2,1)}, bf16[2,1024,512]{2,1,0:T(8,128)(2,1)}, bf16[2,1024,512]{...) while((s32[]{:T(128)}, f32[2,256,16,64]{1,0,3,2:T(2,128)}, ...), condition=%wide.region_11.12_spmd, body=%wide.region_9.11_spmd.sunk | while | flops 2724196608 | bytes 207324480 | solution.py:249
  391.0 9.2 fusion.137
  400.1 7.8 fusion.138
  412.4 21.9 %dynamic_update_slice.32 = f32[2,256,16,64]{1,0,3,2:T(2,128)} dynamic-update-slice(f32[2,256,16,64]{1,0,3,2:T(2,128)} %get-tuple-element.454, f32[1,256,16,64]{1,0,3,2:T(1,128)S(1)} %copy.155, s32[]{:T(128)S(6)} %copy.176, s32[]{:T(128)} %constant.63.clone.1..sunk, s32[]{:T(128)} %constant.63.clone.1..sunk, s32[]{:T(128)} %constant.63.clone.1..sunk) | dynamic-update-slice | bytes 2097156 | tf_op jit(solution)/shard_map/while/body/jit(dynamic_update_index_in_dim)/dynamic_update_slice | solution.py:249
  441.9 8.4 fusion.139
  457.9 9.2 fusion.137
  467.1 7.8 fusion.138
  479.3 21.9 %dynamic_update_slice.32 = f32[2,256,16,64]{1,0,3,2:T(2,128)} dynamic-update-slice(f32[2,256,16,64]{1,0,3,2:T(2,128)} %get-tuple-element.454, f32[1,256,16,64]{1,0,3,2:T(1,128)S(1)} %copy.155, s32[]{:T(128)S(6)} %copy.176, s32[]{:T(128)} %constant.63.clone.1..sunk, s32[]{:T(128)} %constant.63.clone.1..sunk, s32[]{:T(128)} %constant.63.clone.1..sunk) | dynamic-update-slice | bytes 2097156 | tf_op jit(solution)/shard_map/while/body/jit(dynamic_update_index_in_dim)/dynamic_update_slice | solution.py:249
  508.8 8.4 fusion.139
  521.0 11.5 fusion.41
  532.6 11.5 fusion.42
  553.5 9.8 fusion.43
  605.1 192.5 %reduce-scatter.22.cloned.1.call-done = f32[32,4608]{1,0:T(8,128)} async-done(((f32[1024,4608]{1,0:T(8,128)}), f32[32,4608]{1,0:T(8,128)}) %reduce-scatter.22.cloned.1.call-update) | async-done | bytes 589840 | tf_op jit(solution)/shard_map/reduce_scatter | solution.py:321
  799.6 210.2 %reduce-scatter.24.cloned.1.call-done = f32[32,4608]{1,0:T(8,128)} async-done(((f32[1024,4608]{1,0:T(8,128)}), f32[32,4608]{1,0:T(8,128)}) %reduce-scatter.24.cloned.1.call-update) | async-done | bytes 589840 | tf_op jit(solution)/shard_map/reduce_scatter | solution.py:322
  1011.6 210.1 %reduce-scatter.26.cloned.1.call-done = f32[144,1024]{1,0:T(8,128)} async-done(((f32[4608,1024]{1,0:T(8,128)}), f32[144,1024]{1,0:T(8,128)}) %reduce-scatter.26.cloned.1.call-update) | async-done | bytes 589840 | tf_op jit(solution)/shard_map/reduce_scatter | solution.py:323
  1228.5 10.1 add_convert_fusion
  1242.6 39.7 %all-reduce.4 = (bf16[1024]{0:T(1024)(128)(2,1)S(1)}, f32[64]{0:T(128)}, f32[64]{0:T(128)}, bf16[1024]{0:T(1024)(128)(2,1)S(1)}) all-reduce(f32[1024]{0:T(1024)S(1)} %squeeze_reshape.6, f32[64]{0:T(128)S(1)} %get-tuple-element.178, f32[64]{0:T(128)S(1)} %get-tuple-element.184, ...), channel_id=4, replica_groups=mesh['replica'=8,'group'=4] {'replica','group'}, use_global_device_ids=true, to_apply=%region_18.19.clone | all-reduce | flops 2176 | bytes 13312
  1282.9 20.5 %all-reduce.5 = (bf16[256]{0:T(256)(128)(2,1)S(1)}, bf16[256]{0:T(256)(128)(2,1)S(1)}) all-reduce(bf16[256]{0:T(256)(128)(2,1)S(1)} %dynamic-update-slice, bf16[256]{0:T(256)(128)(2,1)S(1)} %dynamic-update-slice.1), channel_id=1, replica_groups=mesh['replica'=8,'group'=4] {'replica'}, use_global_device_ids=true, to_apply=%add | all-reduce | flops 512 | bytes 2048
  1307.9 56.8 %reduce-scatter.14.cloned.1.call-done = f32[32,1024]{1,0:T(8,128)} async-done(((f32[1024,1024]{1,0:T(8,128)}), f32[32,1024]{1,0:T(8,128)}) %reduce-scatter.14.cloned.1.call-update) | async-done | bytes 131088 | tf_op jit(solution)/shard_map/reduce_scatter | solution.py:316
  1365.6 31.4 %all_gather.76 = bf16[256,1024]{1,0:T(8,128)(2,1)S(1)} all-gather(bf16[32,1024]{1,0:T(8,128)(2,1)S(1)} %convert_element_type.221), channel_id=1, replica_groups=mesh['replica'=8,'group'=4] {'replica'}, dimensions={0}, use_global_device_ids=true | all-gather | bytes 589824 | tf_op jit(solution)/shard_map/all_gather | solution.py:329
  1398.2 101.8 %reduce-scatter.16.cloned.1.call-done = f32[32,512]{1,0:T(8,128)} async-done(((f32[1024,512]{1,0:T(8,128)}), f32[32,512]{1,0:T(8,128)}) %reduce-scatter.16.cloned.1.call-update) | async-done | bytes 65552 | tf_op jit(solution)/shard_map/reduce_scatter | solution.py:317
  1500.8 30.7 %all_gather.77 = bf16[256,512]{1,0:T(8,128)(2,1)S(1)} all-gather(bf16[32,512]{1,0:T(8,128)(2,1)S(1)} %convert_element_type.223), channel_id=1, replica_groups=mesh['replica'=8,'group'=4] {'replica'}, dimensions={0}, use_global_device_ids=true | all-gather | bytes 294912 | tf_op jit(solution)/shard_map/all_gather | solution.py:332
  1532.4 102.7 %reduce-scatter.18.cloned.1.call-done = f32[32,512]{1,0:T(8,128)} async-done(((f32[1024,512]{1,0:T(8,128)}), f32[32,512]{1,0:T(8,128)}) %reduce-scatter.18.cloned.1.call-update) | async-done | bytes 65552 | tf_op jit(solution)/shard_map/reduce_scatter | solution.py:318
  1635.9 30.7 %all_gather.78 = bf16[256,512]{1,0:T(8,128)(2,1)S(1)} all-gather(bf16[32,512]{1,0:T(8,128)(2,1)S(1)} %convert_element_type.225), channel_id=1, replica_groups=mesh['replica'=8,'group'=4] {'replica'}, dimensions={0}, use_global_device_ids=true | all-gather | bytes 294912 | tf_op jit(solution)/shard_map/all_gather | solution.py:335
  1667.5 107.6 %reduce-scatter.20.cloned.1.call-done = f32[32,1024]{1,0:T(8,128)} async-done(((f32[1024,1024]{1,0:T(8,128)}), f32[32,1024]{1,0:T(8,128)}) %reduce-scatter.20.cloned.1.call-update) | async-done | bytes 131088 | tf_op jit(solution)/shard_map/reduce_scatter | solution.py:319
  1776.0 32.2 %all_gather.79 = bf16[256,1024]{1,0:T(8,128)(2,1)S(1)} all-gather(bf16[32,1024]{1,0:T(8,128)(2,1)S(1)} %convert_element_type.228), channel_id=1, replica_groups=mesh['replica'=8,'group'=4] {'replica'}, dimensions={0}, use_global_device_ids=true | all-gather | bytes 589824 | tf_op jit(solution)/shard_map/all_gather | solution.py:338
  1809.3 17.4 all-gather.33.cloned.1.call-done
  1831.2 48.4 %all-gather.35.cloned.1.call-done = bf16[256,4608]{1,0:T(8,128)(2,1)} async-done(((bf16[32,4608]{1,0:T(8,128)(2,1)}), bf16[256,4608]{1,0:T(8,128)(2,1)}) %all-gather.35.cloned.1.call-update) | async-done | bytes 2359312 | tf_op jit(solution)/shard_map/all_gather | solution.py:347
  1884.0 48.4 %all-gather.37.cloned.1.call-done = bf16[1152,1024]{1,0:T(8,128)(2,1)} async-done(((bf16[144,1024]{1,0:T(8,128)(2,1)}), bf16[1152,1024]{1,0:T(8,128)(2,1)}) %all-gather.37.cloned.1.call-update) | async-done | bytes 2359312 | tf_op jit(solution)/shard_map/all_gather | solution.py:350
  (330 shorter events, 194.2 us)
Async XLA Ops:
  7.2 10.5 copy-start.1
  7.2 21.9 %all-gather.15.cloned.1.call-start = ((), (), s32[]{:S(2)}) async-start(), calls=%async_computation.9 | async-start | bytes 1310720 | tf_op jit(solution)/shard_map/all_gather | solution.py:163
  7.9 39.4 %all-gather.19.cloned.1.call-start = ((), (), s32[]{:S(2)}) async-start(), calls=%async_computation.11 | async-start | bytes 1310720 | tf_op jit(solution)/shard_map/all_gather | solution.py:162
  8.7 62.9 %all-gather.23.cloned.1.call-start = ((), (), s32[]{:S(2)}) async-start(), calls=%async_computation.13 | async-start | bytes 2621440 | tf_op jit(solution)/shard_map/all_gather | solution.py:161
  9.4 87.0 %all-gather.17.cloned.1.call-start = ((), (), s32[]{:S(2)}) async-start(), calls=%async_computation.10 | async-start | bytes 2621440 | tf_op jit(solution)/shard_map/all_gather | solution.py:185
  16.1 16.4 copy-start.38
  18.2 13.8 copy-start.53
  18.2 13.9 copy-start.51
  32.0 89.3 %all-gather.21.cloned.1.call-start = ((), (), s32[]{:S(2)}) async-start(), calls=%async_computation.12 | async-start | bytes 2621440 | tf_op jit(solution)/shard_map/all_gather | solution.py:184
  32.1 17.6 copy-start.48
  32.5 43.8 %copy-start.22 = (f32[512,32]{0,1:T(8,128)}, f32[512,32]{0,1:T(8,128)S(1)}, u32[]{:S(2)}) copy-start(f32[512,32]{0,1:T(8,128)S(1)} %get-tuple-element.253) | copy-start | bytes 196612
  32.5 43.8 %copy-start.24 = (f32[512,32]{0,1:T(8,128)}, f32[512,32]{0,1:T(8,128)S(1)}, u32[]{:S(2)}) copy-start(f32[512,32]{0,1:T(8,128)S(1)} %get-tuple-element.254) | copy-start | bytes 196612
  52.1 128.5 %all-gather.25.cloned.1.call-start = ((), (), s32[]{:S(2)}) async-start(), calls=%async_computation.14 | async-start | bytes 2621440 | tf_op jit(solution)/shard_map/all_gather | solution.py:164
  52.7 158.5 %all-gather.27.cloned.1.call-start = ((), (), s32[]{:S(2)}) async-start(), calls=%async_computation.15 | async-start | bytes 11796480 | tf_op jit(solution)/shard_map/all_gather | solution.py:205
  53.5 6.8 copy-start.54
  53.5 6.8 copy-start.55
  53.5 223.5 %all-gather.29.cloned.1.call-start = ((), (), s32[]{:S(2)}) async-start(), calls=%async_computation.16 | async-start | bytes 11796480 | tf_op jit(solution)/shard_map/all_gather | solution.py:206
  54.2 288.6 %all-gather.31.cloned.1.call-start = ((), (), s32[]{:S(2)}) async-start(), calls=%async_computation.17 | async-start | bytes 11796480 | tf_op jit(solution)/shard_map/all_gather | solution.py:207
  55.0 526.6 %reduce-scatter.10.cloned.1.call-start = ((), (), s32[]{:S(2)}) async-start(), calls=%async_computation.18 | async-start | bytes 2621440 | tf_op jit(solution)/shard_map/reduce_scatter | solution.py:262
  60.3 15.5 copy-start.46
  77.1 44.2 %copy-start.27 = (bf16[2,256,1024]{2,1,0:T(8,128)(2,1)S(1)}, bf16[2,256,1024]{2,1,0:T(8,128)(2,1)}, u32[]{:S(2)}) copy-start(bf16[2,256,1024]{2,1,0:T(8,128)(2,1)} %custom-call.1) | copy-start | bytes 3145732
  121.3 59.3 %copy-start.2 = (bf16[2,256,1024]{2,1,0:T(8,128)(2,1)S(1)}, bf16[2,256,1024]{2,1,0:T(8,128)(2,1)}, u32[]{:S(2)}) copy-start(bf16[2,256,1024]{2,1,0:T(8,128)(2,1)} %param.19) | copy-start | bytes 3145732
  180.6 4.7 copy-start.43
  185.5 91.5 %copy-start.17 = (bf16[512,1024]{1,0:T(8,128)(2,1)}, bf16[512,1024]{1,0:T(8,128)(2,1)S(1)}, u32[]{:S(2)}) copy-start(bf16[512,1024]{1,0:T(8,128)(2,1)S(1)} %multiply_convert_fusion.5) | copy-start | bytes 3145732
  222.9 119.9 %copy-start.30 = (bf16[2,256,1024]{2,1,0:T(8,128)(2,1)S(1)}, bf16[2,256,1024]{2,1,0:T(8,128)(2,1)}, u32[]{:S(2)}) copy-start(bf16[2,256,1024]{2,1,0:T(8,128)(2,1)} %param.22) | copy-start | bytes 3145732
  363.2 9.2 copy-start.11
  363.2 9.2 copy-start.57
  434.3 6.2 copy-start.20
  501.2 6.2 copy-start.20
  518.9 73.5 %reduce-scatter.12.cloned.1.call-start = ((), (), s32[]{:S(2)}) async-start(), calls=%async_computation.19 | async-start | bytes 2621440 | tf_op jit(solution)/shard_map/reduce_scatter | solution.py:265
  519.7 278.0 %reduce-scatter.22.cloned.1.call-start = ((), (), s32[]{:S(2)}) async-start(), calls=%async_computation.24 | async-start | bytes 19464192 | tf_op jit(solution)/shard_map/reduce_scatter | solution.py:321
  532.5 477.2 %reduce-scatter.24.cloned.1.call-start = ((), (), s32[]{:S(2)}) async-start(), calls=%async_computation.26 | async-start | bytes 19464192 | tf_op jit(solution)/shard_map/reduce_scatter | solution.py:322
  544.1 677.7 %reduce-scatter.26.cloned.1.call-start = ((), (), s32[]{:S(2)}) async-start(), calls=%async_computation.28 | async-start | bytes 19464192 | tf_op jit(solution)/shard_map/reduce_scatter | solution.py:323
  563.4 801.4 %reduce-scatter.14.cloned.1.call-start = ((), (), s32[]{:S(2)}) async-start(), calls=%async_computation.20 | async-start | bytes 4325376 | tf_op jit(solution)/shard_map/reduce_scatter | solution.py:316
  581.5 918.4 %reduce-scatter.16.cloned.1.call-start = ((), (), s32[]{:S(2)}) async-start(), calls=%async_computation.21 | async-start | bytes 2162688 | tf_op jit(solution)/shard_map/reduce_scatter | solution.py:317
  584.2 4.5 copy-start.9
  584.2 4.5 copy-start.36
  584.2 4.5 copy-start.49
  592.3 1042.7 %reduce-scatter.18.cloned.1.call-start = ((), (), s32[]{:S(2)}) async-start(), calls=%async_computation.22 | async-start | bytes 2162688 | tf_op jit(solution)/shard_map/reduce_scatter | solution.py:318
  595.6 1179.5 %reduce-scatter.20.cloned.1.call-start = ((), (), s32[]{:S(2)}) async-start(), calls=%async_computation.23 | async-start | bytes 4325376 | tf_op jit(solution)/shard_map/reduce_scatter | solution.py:319
  597.7 4.1 copy-start.7
  605.0 618.6 %copy-start.56 = (u32[32]{0:T(128)S(1)}, u32[32]{0:T(128)}, u32[]{:S(2)}) copy-start(u32[32]{0:T(128)} %constant.99) | copy-start | bytes 388
  605.1 619.8 %copy-start.50 = (f32[1024]{0:T(1024)S(1)}, f32[1024]{0:T(1024)}, u32[]{:S(2)}) copy-start(f32[1024]{0:T(1024)} %get-tuple-element.180) | copy-start | bytes 12292
  605.1 1221.7 %all-gather.33.cloned.1.call-start = ((), (), s32[]{:S(2)}) async-start(), calls=%async_computation.25 | async-start | bytes 2654208 | tf_op jit(solution)/shard_map/all_gather | solution.py:344
  799.5 1080.1 %all-gather.35.cloned.1.call-start = ((), (), s32[]{:S(2)}) async-start(), calls=%async_computation.27 | async-start | bytes 2654208 | tf_op jit(solution)/shard_map/all_gather | solution.py:347
  1011.6 920.8 %all-gather.37.cloned.1.call-start = ((), (), s32[]{:S(2)}) async-start(), calls=%async_computation.29 | async-start | bytes 2654208 | tf_op jit(solution)/shard_map/all_gather | solution.py:350
  1228.4 10.2 copy-start.15
  1228.4 10.2 copy-start.16
  (36 other events, 75.5 us)
Sparse Core Ops, SparseCore 0:
  9.6 19.4 all-gather.14
  30.6 16.7 all-gather.18
  48.9 22.6 all-gather.22
  73.6 22.8 all-gather.16
  98.4 22.8 all-gather.20
  122.7 22.5 all-gather.24
  146.9 64.2 all-gather.26
  212.7 64.2 all-gather.28
  278.6 64.2 all-gather.30
  519.1 31.4 reduce-scatter.9
  553.2 31.3 reduce-scatter.11
  590.9 206.6 reduce-scatter.21
  804.1 205.6 reduce-scatter.23
  1016.0 205.7 reduce-scatter.25
  1224.5 140.2 reduce-scatter.13
  1366.8 133.0 reduce-scatter.15
  1502.1 132.8 reduce-scatter.17
  1637.7 137.3 reduce-scatter.19
  1777.3 49.4 all-gather.32
  1828.8 50.7 all-gather.34
  1881.8 50.5 all-gather.36
where the time goes:
time: 1950 us; the launch traced here: 1940 us
  waiting for transfers between devices  1310 us (67%)
  matrix products  220 us (11%)
  blocking collectives  202 us (10%)
  local copies, waits for them, and re-layouts  118 us (6%)
  other arithmetic  77.9 us (4%)
    reduce_scatter x1, waiting for transfers between devices, per_device(): lax.psum_scatter(partials[7], ('replica', 'group'), scatter_dimension=0,...  210 us
    reduce_scatter x1, waiting for transfers between devices, per_device(): lax.psum_scatter(partials[8], ('replica', 'group'), scatter_dimension=0,...  210 us
    reduce_scatter x1, waiting for transfers between devices, per_device(): lax.psum_scatter(partials[6], ('replica', 'group'), scatter_dimension=0,...  193 us
    reduce_scatter x1, waiting for transfers between devices, per_device(): lax.psum_scatter(partials[4], ('replica', 'group'), scatter_dimension=0,...  108 us
    reduce_scatter x1, waiting for transfers between devices, per_device(): lax.psum_scatter(partials[3], ('replica', 'group'), scatter_dimension=0,...  103 us
    reduce_scatter x1, waiting for transfers between devices, per_device(): lax.psum_scatter(partials[2], ('replica', 'group'), scatter_dimension=0,...  102 us
    unnamed x2, blocking collectives  60.2 us
    reduce_scatter x1, waiting for transfers between devices, per_device(): lax.psum_scatter(partials[1], ('replica', 'group'), scatter_dimension=0,...  56.8 us
  transfers between devices with their start and end apart: 21, of which 18 were waited for; matrix products, arithmetic and copies ran while one was open for 12% of the time, Pallas kernels for 0%

commit v1 on v0

v1 whole, which is shorter than its diff:
```python
import functools

import jax
import jax.numpy as jnp
from jax import lax
from jax.experimental import pallas as pl
from jax.experimental.pallas import tpu as pltpu
from jax.sharding import PartitionSpec as P

HEADS = 8
PAIRS = 4
HD = 64
HALF = 32
SPAN = 256

EPS = 1e-05
THETA = 1000000.0
NEG = -1e30

BF = jnp.bfloat16
F32 = jnp.float32

Y_SWAP = [(0, 2), (2, 0), (1, 3), (3, 1)]
CORE_SWAP = [(0, 1), (1, 0), (2, 3), (3, 2)]


def contract(left, right, left_dim, right_dim):
    return lax.dot_general(
        left, right, (((left_dim,), (right_dim,)), ((), ())), preferred_element_type=F32
    )


def visible_block(seg_col, seg_row, block):
    end = (block + 1) * SPAN
    key_at = lax.broadcasted_iota(jnp.int32, (end, SPAN), 0)
    query_at = lax.broadcasted_iota(jnp.int32, (end, SPAN), 1) + block * SPAN
    return (seg_col[0:end, :] == seg_row[:, block * SPAN : end]) & (key_at <= query_at)


def forward_kernel(
    hidden_ref,
    weight_ref,
    cos_ref,
    sin_ref,
    seg_row_ref,
    seg_col_ref,
    gain_ref,
    mixed_ref,
    rot_ref,
    key_ref,
    value_ref,
    value_t_ref,
    normed_ref,
    inv_ref,
    log_ref,
):
    blocks = hidden_ref.shape[0] // SPAN
    heads = HEADS + PAIRS
    for block in range(blocks):
        span = slice(block * SPAN, (block + 1) * SPAN)
        raw = jnp.dot(hidden_ref[span, :], weight_ref[...], preferred_element_type=F32)
        value_ref[span, :] = raw[:, heads * HD :].astype(BF)
        raw_t = raw.T
        value_t_ref[:, span] = raw_t[heads * HD :, :].astype(BF)
        cosine = cos_ref[:, span]
        sine = sin_ref[:, span]
        for head in range(heads):
            rows = slice(head * HD, (head + 1) * HD)
            part = raw_t[rows, :]
            inv = lax.rsqrt(jnp.mean(part * part, 0, keepdims=True) + EPS)
            normed = part * inv
            normed_ref[rows, span] = normed
            inv_ref[head : head + 1, span] = inv
            kind = 0 if head < HEADS else 1
            scaled = normed * gain_ref[:, kind : kind + 1]
            first = scaled[:HALF, :]
            second = scaled[HALF:, :]
            turned = jnp.concatenate(
                [first * cosine - second * sine, second * cosine + first * sine], 0
            )
            if head < HEADS:
                rot_ref[rows, span] = turned.astype(BF) * BF(HD**-0.5)
            else:
                rot_ref[rows, span] = turned.astype(BF)
    for pair in range(PAIRS):
        rows = slice((HEADS + pair) * HD, (HEADS + pair + 1) * HD)
        key_ref[pair] = rot_ref[rows, :].astype(F32).T.astype(BF)
    for block in range(blocks):
        end = (block + 1) * SPAN
        span = slice(block * SPAN, end)
        visible = visible_block(seg_col_ref[...], seg_row_ref[...], block)

        def one_pair(pair, carry, end=end, span=span, visible=visible):
            keys = key_ref[pair, 0:end, :]
            values_t = value_t_ref[pl.ds(pl.multiple_of(pair * HD, HD), HD), 0:end]
            outs = []
            for side in range(2):
                head = pair * 2 + side
                rows = pl.ds(pl.multiple_of(head * HD, HD), HD)
                score = jnp.dot(keys, rot_ref[rows, span], preferred_element_type=F32)
                score = jnp.where(visible, score, NEG)
                top = jnp.max(score, 0, keepdims=True)
                weight = jnp.exp(score - top)
                total = jnp.sum(weight, 0, keepdims=True)
                log_ref[pl.ds(head, 1), span] = top + jnp.log(total)
                prob = (weight * (1.0 / total)).astype(BF)
                outs.append(jnp.dot(values_t, prob, preferred_element_type=F32))
            both = jnp.concatenate(outs, 0).T
            cols = pl.ds(pl.multiple_of(pair * 2 * HD, 2 * HD), 2 * HD)
            mixed_ref[span, cols] = both.astype(BF)
            return carry

        lax.fori_loop(0, PAIRS, one_pair, 0)


def backward_kernel(
    grad_ref,
    rot_ref,
    key_ref,
    value_ref,
    normed_ref,
    inv_ref,
    log_ref,
    cos_ref,
    sin_ref,
    seg_row_ref,
    seg_col_ref,
    gain_ref,
    out_ref,
    gain_grad_ref,
    grad_t,
    query_grad,
    value_one,
    key_sum,
    value_sum,
    out_t,
):
    length = grad_ref.shape[0]
    blocks = length // SPAN
    heads = HEADS + PAIRS
    for part in range(HEADS // 2):
        cols = slice(part * 2 * HD, (part + 1) * 2 * HD)
        grad_t[cols, :] = grad_ref[:, cols].astype(F32).T.astype(BF)
    values_t = value_ref[...].astype(F32).T
    for pair in range(PAIRS):
        value_one[pair] = values_t[pair * HD : (pair + 1) * HD, :].T.astype(BF)
    left_lane = lax.broadcasted_iota(jnp.int32, (SPAN, 2 * HD), 1) < HD
    zero = jnp.zeros((SPAN, 2 * HD), BF)

    def one_pair(pair, carry):
        key_sum[...] = jnp.zeros_like(key_sum)
        value_sum[...] = jnp.zeros_like(value_sum)
        keys_t = rot_ref[pl.ds(pl.multiple_of((HEADS + pair) * HD, HD), HD), :]
        both = pl.ds(pl.multiple_of(pair * 2 * HD, 2 * HD), 2 * HD)
        for block in range(blocks):
            end = (block + 1) * SPAN
            span = slice(block * SPAN, end)
            visible = visible_block(seg_col_ref[...], seg_row_ref[...], block)
            queries = rot_ref[both, span].astype(F32).T.astype(BF)
            grads = grad_ref[span, both]
            for side in range(2):
                head = pair * 2 + side
                rows = pl.ds(pl.multiple_of(head * HD, HD), HD)
                score = jnp.dot(
                    key_ref[pair, 0:end, :], rot_ref[rows, span], preferred_element_type=F32
                )
                prob = jnp.where(visible, jnp.exp(score - log_ref[pl.ds(head, 1), span]), 0.0)
                grad_prob = jnp.dot(
                    value_one[pair, 0:end, :], grad_t[rows, span], preferred_element_type=F32
                )
                inner = jnp.sum(prob * grad_prob, 0, keepdims=True)
                grad_score = (prob * (grad_prob - inner)).astype(BF)
                mine = left_lane if side == 0 else jnp.logical_not(left_lane)
                value_sum[0:end, :] += jnp.dot(
                    prob.astype(BF), jnp.where(mine, grads, zero), preferred_element_type=F32
                )
                key_sum[0:end, :] += jnp.dot(
                    grad_score, jnp.where(mine, queries, zero), preferred_element_type=F32
                )
                query_grad[rows, span] = jnp.dot(
                    keys_t[:, 0:end], grad_score, preferred_element_type=F32
                ) * (HD**-0.5)
        key_t = key_sum[...].T
        value_t = value_sum[...].T
        key_rows = pl.ds(pl.multiple_of((HEADS + pair) * HD, HD), HD)
        query_grad[key_rows, :] = key_t[:HD, :] + key_t[HD:, :]
        value_rows = pl.ds(pl.multiple_of((heads + pair) * HD, HD), HD)
        out_t[value_rows, :] = value_t[:HD, :] + value_t[HD:, :]
        return carry

    lax.fori_loop(0, PAIRS, one_pair, 0)

    cosine = cos_ref[...]
    sine = sin_ref[...]
    gain_sums = [jnp.zeros((HD, length), F32), jnp.zeros((HD, length), F32)]
    for head in range(heads):
        rows = slice(head * HD, (head + 1) * HD)
        kind = 0 if head < HEADS else 1
        part = query_grad[rows, :]
        first = part[:HALF, :]
        second = part[HALF:, :]
        turned = jnp.concatenate(
            [first * cosine + second * sine, second * cosine - first * sine], 0
        )
        normed = normed_ref[rows, :]
        gain_sums[kind] = gain_sums[kind] + turned * normed
        scaled = turned * gain_ref[:, kind : kind + 1]
        mean = jnp.mean(scaled * normed, 0, keepdims=True)
        out_t[rows, :] = inv_ref[head : head + 1, :] * (scaled - normed * mean)
    for kind in range(2):
        gain_grad_ref[:, kind : kind + 1] = jnp.sum(gain_sums[kind], 1, keepdims=True)
    width = out_t.shape[0]
    for part in range(width // (2 * HD)):
        cols = slice(part * 2 * HD, (part + 1) * 2 * HD)
        out_ref[:, cols] = out_t[cols, :].T.astype(BF)


def whole_refs(count):
    return [pl.BlockSpec(memory_space=pltpu.VMEM)] * count


def attention_forward(hidden, weight, cosine, sine, seg_row, seg_col, gains):
    length = hidden.shape[0]
    rows = (HEADS + PAIRS) * HD
    outs = [
        ((length, HEADS * HD), BF),
        ((rows, length), BF),
        ((PAIRS, length, HD), BF),
        ((length, PAIRS * HD), BF),
        ((PAIRS * HD, length), BF),
        ((rows, length), F32),
        ((16, length), F32),
        ((HEADS, length), F32),
    ]
    return pl.pallas_call(
        forward_kernel,
        out_shape=[jax.ShapeDtypeStruct(shape, kind) for shape, kind in outs],
        in_specs=whole_refs(7),
        out_specs=whole_refs(len(outs)),
        compiler_params=pltpu.CompilerParams(vmem_limit_bytes=48 * 1024 * 1024),
        cost_estimate=pl.CostEstimate(
            flops=12 * 10**9, bytes_accessed=16 * 2**20, transcendentals=6 * 10**6
        ),
        name="attention_forward",
    )(hidden, weight, cosine, sine, seg_row, seg_col, gains)


def attention_backward(grad, rot, key, value, normed, inv, log, cosine, sine, seg_row, seg_col, gains):
    length = grad.shape[0]
    rows = (HEADS + PAIRS) * HD
    width = rows + PAIRS * HD
    return pl.pallas_call(
        backward_kernel,
        out_shape=[
            jax.ShapeDtypeStruct((length, width), BF),
            jax.ShapeDtypeStruct((HD, 2), F32),
        ],
        in_specs=whole_refs(12),
        out_specs=whole_refs(2),
        scratch_shapes=[
            pltpu.VMEM((HEADS * HD, length), BF),
            pltpu.VMEM((rows, length), F32),
            pltpu.VMEM((PAIRS, length, HD), BF),
            pltpu.VMEM((length, 2 * HD), F32),
            pltpu.VMEM((length, 2 * HD), F32),
            pltpu.VMEM((width, length), F32),
        ],
        compiler_params=pltpu.CompilerParams(vmem_limit_bytes=56 * 1024 * 1024),
        cost_estimate=pl.CostEstimate(
            flops=25 * 10**9, bytes_accessed=16 * 2**20, transcendentals=6 * 10**6
        ),
        name="attention_backward",
    )(grad, rot, key, value, normed, inv, log, cosine, sine, seg_row, seg_col, gains)


def norm_rows(inputs):
    inv = lax.rsqrt(jnp.mean(inputs * inputs, -1, keepdims=True) + EPS)
    return (inputs * inv, inv)


def norm_back(grad, normed, inv):
    return inv * (grad - normed * jnp.mean(grad * normed, -1, keepdims=True))


def swap_y(value):
    return lax.ppermute(value, "group", Y_SWAP)


def swap_core(value):
    return lax.ppermute(value, "group", CORE_SWAP)


def cycle_of(count):
    return list(range(0, count, 2)) + list(range(count - 1, 0, -2))


class Ring:
    def __init__(self, way):
        count = lax.axis_size("replica")
        cycle = cycle_of(count)
        if way < 0:
            cycle = cycle[::-1]
        places = [cycle.index(member) for member in range(count)]
        self.count = count
        self.cycle = jnp.array(cycle, jnp.int32)
        self.place = jnp.array(places, jnp.int32)[lax.axis_index("replica")]
        self.hops = [(cycle[at], cycle[(at + 1) % count]) for at in range(count)]

    def chunk_at(self, back):
        return self.cycle[lax.rem(self.place - back + 2 * self.count, self.count)]

    def send(self, value):
        return lax.ppermute(value, "replica", self.hops)

    def reduce(self, pick):
        moving = pick(self.chunk_at(1)).astype(BF)
        for step in range(self.count - 1):
            arrived = self.send(moving)
            moving = (pick(self.chunk_at(step + 2)) + arrived.astype(F32)).astype(BF)
        return moving

    def gather(self, chunk, place):
        moving = chunk
        place(self.chunk_at(0), moving)
        for step in range(self.count - 1):
            moving = self.send(moving)
            place(self.chunk_at(step + 1), moving)


def pick_rows(whole, dim):
    def pick(index):
        return lax.dynamic_index_in_dim(whole, index, dim, keepdims=False).astype(F32)

    return pick


def gather_rows(ring, chunk, count):
    rows, columns = chunk.shape
    store = [jnp.zeros((count * rows, columns), F32)]

    def place(index, value):
        store[0] = lax.dynamic_update_slice(store[0], value.astype(F32), (index * rows, 0))

    ring.gather(chunk, place)
    return store[0]


def per_device(
    hidden_in,
    segments,
    positions,
    out_grad,
    attn_gain,
    w_query,
    w_key,
    w_value,
    query_gain,
    key_gain,
    w_out,
    ffn_gain,
    w_gate,
    w_up,
    w_down,
):
    copies = lax.axis_size("replica")
    member = lax.axis_index("group")
    y_at = member // 2
    core = lax.rem(member, 2)
    on_low_y = y_at == 0
    on_low_core = core == 0
    span, width = hidden_in.shape[1:]
    hidden_units = w_down.shape[0]

    def by_y(mine, other):
        return jnp.where(on_low_y, mine, other), jnp.where(on_low_y, other, mine)

    def by_core(mine, other):
        return jnp.where(on_low_core, mine, other), jnp.where(on_low_core, other, mine)

    def at_y(pair_low, pair_high):
        return jnp.where(on_low_y, pair_low, pair_high), jnp.where(on_low_y, pair_high, pair_low)

    def at_core(low, high):
        return jnp.where(on_low_core, low, high), jnp.where(on_low_core, high, low)

    small = jnp.concatenate(
        [
            attn_gain.astype(F32)[None],
            ffn_gain.astype(F32)[None],
            segments.astype(F32),
            positions.astype(F32),
        ],
        0,
    )
    small_low, small_high = by_y(small, swap_y(small))
    small_two = jnp.stack([small_low, small_high])
    small_even, small_odd = by_core(small_two, swap_core(small_two))
    small_all = jnp.stack([small_even, small_odd], 1).reshape(4, 6, span)
    small_rows = small_all.transpose(1, 0, 2).reshape(6, 4 * span)
    gain_one = small_rows[0]
    gain_two = small_rows[1]
    seg = jnp.where(on_low_y, small_rows[2], small_rows[3])
    place = jnp.where(on_low_y, small_rows[4], small_rows[5])

    seq_mine, seq_other = at_y(hidden_in[0], hidden_in[1])
    own_low, own_high = by_y(seq_mine, swap_y(seq_other))
    own_in = jnp.stack([own_low, own_high])
    all_even, all_odd = by_core(own_in, swap_core(own_in))
    all_in = jnp.stack([all_even, all_odd], 1).reshape(4 * span, width)

    def head_columns(weight):
        rows = weight.shape[0]
        parts = weight.reshape(rows, 2, 2, -1)
        mine, other = at_core(parts[:, :, 0], parts[:, :, 1])
        return mine.reshape(rows, -1), other.reshape(rows, -1)

    columns = [head_columns(weight) for weight in (w_query, w_key, w_value)]
    mine_cols = jnp.concatenate([mine for mine, other in columns], 1)
    other_cols = jnp.concatenate([other for mine, other in columns], 1)
    two_rows = jnp.concatenate(by_core(mine_cols, swap_core(other_cols)), 0)
    w_attn = jnp.concatenate(by_y(two_rows, swap_y(two_rows)), 0)
    w_mix = jnp.concatenate(by_y(w_out, swap_y(w_out)), 0)

    def unit_columns(weight):
        rows = weight.shape[0]
        parts = weight.reshape(rows, 2, 2, -1)
        return at_core(parts[:, :, 0], parts[:, :, 1])

    gate_mine, gate_other = unit_columns(w_gate)
    up_mine, up_other = unit_columns(w_up)
    ffn_mine = jnp.concatenate([gate_mine, up_mine], -1)
    ffn_other = jnp.concatenate([gate_other, up_other], -1)
    ffn_rows = jnp.concatenate(by_core(ffn_mine, swap_core(ffn_other)), 0)
    ffn_here, ffn_there = at_y(ffn_rows[:, 0], ffn_rows[:, 1])
    w_ffn = jnp.concatenate(by_y(ffn_here, swap_y(ffn_there)), 0)

    dy_mine, dy_other = at_y(out_grad[0], out_grad[1])
    dy_y = swap_y(out_grad)
    dy_y_mine, dy_y_other = at_y(dy_y[0], dy_y[1])
    dy_own = jnp.concatenate(by_y(dy_mine, dy_y_mine), 0)
    dy_next = jnp.concatenate(by_y(dy_other, dy_y_other), 0)
    dy_sib = swap_core(dy_own)
    dy_diag = swap_core(dy_next)
    dy_near = jnp.concatenate([dy_own, dy_sib], 0)
    dy_far = jnp.concatenate([dy_next, dy_diag], 0)

    normed_all, _ = norm_rows(all_in.astype(F32))
    hidden_one = (normed_all * gain_one).astype(BF)
    freq = THETA ** (-(jnp.arange(HALF, dtype=F32) * 2.0 / HD))
    angle = freq[:, None] * place[None, :]
    cosine, sine = jnp.cos(angle), jnp.sin(angle)
    gains = jnp.stack([query_gain, key_gain], 1).astype(F32)
    seg_row = seg[None, :]
    seg_col = seg[:, None]
    mixed, rot, key_rot, value_low, _, head_normed, head_inv, log_total = attention_forward(
        hidden_one, w_attn, cosine, sine, seg_row, seg_col, gains
    )

    def own_and_other(rows):
        parts = rows.reshape(2, 2, span, rows.shape[-1])
        mine, other = at_core(parts[:, 0], parts[:, 1])
        return mine.reshape(2 * span, -1), other.reshape(2 * span, -1)

    mix_part = jnp.dot(mixed, w_mix, preferred_element_type=F32)
    mix_mine, mix_other = own_and_other(mix_part)
    inputs = own_in.reshape(2 * span, width).astype(F32)
    middle = inputs + mix_mine + swap_core(mix_other.astype(BF)).astype(F32)
    normed_two, inv_two = norm_rows(middle)
    hidden_two = (normed_two * gain_two).astype(BF)

    h2_next = swap_y(hidden_two)
    h2_sib = swap_core(hidden_two)
    h2_diag = swap_core(h2_next)
    h2_near = jnp.concatenate([hidden_two, h2_sib], 0)
    h2_far = jnp.concatenate([h2_next, h2_diag], 0)
    units = hidden_units

    def ffn(h2, dy):
        both = contract(h2, w_ffn, 1, 0)
        gate, up = both[:, :units], both[:, units:]
        sig = jax.nn.sigmoid(gate)
        act = (gate * sig * up).astype(BF)
        grad_act = contract(dy, w_down, 1, 1)
        grad_gate = (grad_act * up * sig * (1.0 + gate * (1.0 - sig))).astype(BF)
        grad_up = (grad_act * gate * sig).astype(BF)
        return act, jnp.concatenate([grad_gate, grad_up], 1)

    act_near, grad_near = ffn(h2_near, dy_near)
    act_far, grad_far = ffn(h2_far, dy_far)
    down_grad = (contract(act_near, dy_near, 0, 0) + contract(act_far, dy_far, 0, 0)).astype(BF)
    back_far = contract(grad_far, w_ffn, 1, 1)
    back_near = contract(grad_near, w_ffn, 1, 1)
    rows_own = 2 * span
    dh2_far = back_far[:rows_own] + swap_core(back_far[rows_own:].astype(BF)).astype(F32)
    dh2_near = back_near[:rows_own] + swap_core(back_near[rows_own:].astype(BF)).astype(F32)
    grad_hidden_two = dh2_near + swap_y(dh2_far.astype(BF)).astype(F32)
    ffn_grad = (contract(h2_near, grad_near, 0, 0) + contract(h2_far, grad_far, 0, 0)).astype(BF)

    out_near = contract(act_near, w_down, 1, 0)
    out_far = contract(act_far, w_down, 1, 0)
    out_own = middle + out_near[:rows_own] + swap_core(out_near[rows_own:].astype(BF)).astype(F32)
    out_next = out_far[:rows_own] + swap_core(out_far[rows_own:].astype(BF)).astype(F32)

    def chunk_pair(rows):
        parts = rows.reshape(2, span, width)
        return at_y(parts[0], parts[1])

    own_here, own_there = chunk_pair(out_own)
    next_here, next_there = chunk_pair(out_next)
    out_back = swap_y(jnp.stack([own_there, next_there]).astype(BF)).astype(F32)
    block_out = jnp.stack(by_y(own_here + out_back[1], next_here + out_back[0])).astype(BF)

    ffn_gain_part = jnp.sum(grad_hidden_two * normed_two, 0)
    grad_middle = dy_own.astype(F32) + norm_back(grad_hidden_two * gain_two, normed_two, inv_two)
    grad_branch = grad_middle.astype(BF).reshape(2, span, width)
    branch_even, branch_odd = by_core(grad_branch, swap_core(grad_branch))
    branch_all = jnp.stack([branch_even, branch_odd], 1).reshape(4 * span, width)
    grad_mixed = contract(branch_all, w_mix, 1, 1).astype(BF)
    mix_grad = contract(mixed, branch_all, 0, 0)
    grad_heads, head_gain_part = attention_backward(
        grad_mixed,
        rot,
        key_rot,
        value_low,
        head_normed,
        head_inv,
        log_total,
        cosine,
        sine,
        seg_row,
        seg_col,
        gains,
    )
    back_one = contract(grad_heads, w_attn, 1, 1)
    one_mine, one_other = own_and_other(back_one)
    grad_hidden_one = one_mine + swap_core(one_other.astype(BF)).astype(F32)
    normed_one, inv_one = norm_rows(inputs)
    attn_gain_part = jnp.sum(grad_hidden_one * normed_one, 0)
    grad_input = grad_middle + norm_back(grad_hidden_one * gain_one, normed_one, inv_one)
    input_here, input_there = chunk_pair(grad_input)
    input_back = swap_y(input_there.astype(BF)).astype(F32)
    input_grad = jnp.stack(by_y(input_here, input_back))

    attn_grad = contract(hidden_one, grad_heads, 0, 0).reshape(2, 2 * span, -1)
    rows_here, rows_there = at_y(attn_grad[0], attn_grad[1])
    attn_grad_y = rows_here + swap_y(rows_there.astype(BF)).astype(F32)
    mix_here, mix_there = at_y(mix_grad[:span], mix_grad[span:])
    mix_grad_y = mix_here + swap_y(mix_there.astype(BF)).astype(F32)

    sums = jnp.concatenate([attn_gain_part, ffn_gain_part, head_gain_part.T.reshape(-1)])
    sums = sums.reshape(-1, 128)
    sums = sums + swap_core(sums)
    sums = sums + swap_y(sums)
    step = 1
    while step < copies:
        sums = sums + lax.ppermute(sums, "replica", [(at, at ^ step) for at in range(copies)])
        step *= 2
    sums = sums.reshape(-1)
    attn_gain_grad = lax.dynamic_slice(sums, (member * span,), (span,))
    ffn_gain_grad = lax.dynamic_slice(sums, (width + member * span,), (span,))
    query_gain_grad = sums[2 * width : 2 * width + HD]
    key_gain_grad = sums[2 * width + HD : 2 * width + 2 * HD]

    right, left = Ring(1), Ring(-1)
    half = width // 2
    down_rows = hidden_units // copies
    down_view = down_grad.reshape(copies, down_rows, width)
    down_right = right.reduce(pick_rows(down_view[:, :, :half], 0))
    down_left = left.reduce(pick_rows(down_view[:, :, half:], 0))
    w_down_grad = jnp.concatenate(
        [gather_rows(right, down_right, copies), gather_rows(left, down_left, copies)], 1
    )

    rows = span // copies
    ffn_view = ffn_grad.reshape(4, copies, rows, 2 * units)
    gate_part = right.reduce(pick_rows(ffn_view[..., :units], 1))
    up_part = left.reduce(pick_rows(ffn_view[..., units:], 1))

    def own_rows(part):
        parts = part.reshape(2, 2, rows, units)
        mine, other = at_core(parts[:, 0], parts[:, 1])
        both_cores = jnp.stack(by_core(mine, swap_core(other)), 1)
        here, there = at_y(both_cores[0], both_cores[1])
        all_units = jnp.stack(by_y(here, swap_y(there)))
        return all_units.transpose(2, 0, 1, 3).reshape(rows, 4 * units)

    w_gate_grad = gather_rows(right, own_rows(gate_part), copies)
    w_up_grad = gather_rows(left, own_rows(up_part), copies)

    query_width = 2 * span
    attn_view = attn_grad_y.reshape(2, copies, rows, -1)
    query_part = right.reduce(pick_rows(attn_view[..., :query_width], 1))
    rest_part = left.reduce(pick_rows(attn_view[..., query_width:], 1))
    mix_view = mix_grad_y.reshape(copies, rows, width)
    mix_right = right.reduce(pick_rows(mix_view[..., :half], 0))
    mix_left = left.reduce(pick_rows(mix_view[..., half:], 0))

    def all_heads(part, kinds):
        mine, other = at_core(part[0], part[1])
        even, odd = by_core(mine, swap_core(other))
        shape = (rows, kinds, 2, 1, part.shape[-1] // (2 * kinds))
        return jnp.concatenate([even.reshape(shape), odd.reshape(shape)], 3).reshape(rows, -1)

    query_all = gather_rows(right, all_heads(query_part, 1), copies)
    rest_all = gather_rows(left, all_heads(rest_part, 2), copies)
    w_out_grad = jnp.concatenate(
        [gather_rows(right, mix_right, copies), gather_rows(left, mix_left, copies)], 1
    )
    w_query_grad = query_all
    w_key_grad = rest_all[:, : 2 * span]
    w_value_grad = rest_all[:, 2 * span :]

    return (
        block_out,
        input_grad,
        attn_gain_grad,
        w_query_grad,
        w_key_grad,
        w_value_grad,
        query_gain_grad,
        key_gain_grad,
        w_out_grad,
        ffn_gain_grad,
        w_gate_grad,
        w_up_grad,
        w_down_grad,
    )


def solution(mesh):
    rows = P("group", None)
    tokens = P("replica", "group", None)
    placed = (
        tokens,
        P("replica", "group"),
        P("replica", "group"),
        tokens,
        P("group"),
        rows,
        rows,
        rows,
        P(),
        P(),
        rows,
        P("group"),
        rows,
        rows,
        rows,
    )
    return jax.shard_map(
        per_device,
        mesh=mesh,
        in_specs=placed,
        out_specs=(
            tokens,
            tokens,
            P("group"),
            rows,
            rows,
            rows,
            P(),
            P(),
            rows,
            P("group"),
            rows,
            rows,
            rows,
        ),
        check_vma=False,
    )
```

time: 1950 us -> 815 us (0.42)
  waiting for transfers between devices: 1310 us -> 314 us
  blocking collectives: 202 us -> 0 us
  starting transfers between devices: 0.84 us -> 149 us
  matrix products: 220 us -> 88.5 us
  local copies, waits for them, and re-layouts: 118 us -> 46.3 us
  Pallas kernels: 0 us -> 53.4 us
  between operations: 16 us -> 66.1 us
    reduce_scatter x9 -> x0, waiting for transfers between devices: 982 us -> none  [the longest x1 210 us: per_device(): lax.psum_scatter(partials[7], ('replica', 'group'), scatter_dimension=0,...]
    all_gather x12 -> x0, waiting for transfers between devices: 321 us -> none  [the longest x1 54.5 us: per_device(): lax.all_gather(w_down, 'group', axis=0, tiled=True)]
    ppermute x0 -> x150, waiting for transfers between devices: none -> 314 us  [the longest x112 224 us: send(): return lax.ppermute(value, 'replica', self.hops)]
    ppermute x0 -> x150, starting transfers between devices: none -> 149 us  [the longest x112 127 us: send(): return lax.ppermute(value, 'replica', self.hops)]
    all_gather x7 -> x0, blocking collectives: 142 us -> none  [the longest x1 32.2 us: per_device(): lax.all_gather(shares[4].astype(jnp.bfloat16), 'replica', axis=0, tiled=T...]
    dot_general x35 -> x17, matrix products: 220 us -> 88.5 us  [the longest x16 87.3 us: contract(): lax.dot_general(left, right, (((left_dim,), (right_dim,)), ((), ())), pre...]
    unnamed x2 -> x0, blocking collectives: 60.2 us -> none
    pallas_call x0 -> x2, Pallas kernels: none -> 53.4 us  [the longest x1 26.8 us: attention_forward(): pl.pallas_call(forward_kernel, out_shape=[jax.ShapeDtypeStruct(shape, kin...]
  transfers between devices with their start and end apart: 21 -> 150, of which waited for: 18 -> 83; matrix products, arithmetic and copies ran while one was open for 12% -> 22% of each run, Pallas kernels for 0% -> 7%
where the time goes in v1:
time: 815 us; the launch traced here: 805 us
  waiting for transfers between devices  314 us (39%)
  starting transfers between devices  149 us (18%)
  matrix products  88.5 us (11%)
  other arithmetic  86.7 us (11%)
  between operations  66.1 us (8%)
  Pallas kernels  53.4 us (7%)
  local copies, waits for them, and re-layouts  46.3 us (6%)
    ppermute x112, waiting for transfers between devices, send(): return lax.ppermute(value, 'replica', self.hops)  224 us
    ppermute x112, starting transfers between devices, send(): return lax.ppermute(value, 'replica', self.hops)  127 us
    dot_general x16, matrix products, contract(): lax.dot_general(left, right, (((left_dim,), (right_dim,)), ((), ())), pre...  87.3 us
    ppermute x15, waiting for transfers between devices, swap_y(): return lax.ppermute(value, 'group', Y_SWAP)  79.7 us
    pallas_call x1, Pallas kernels, attention_forward(): pl.pallas_call(forward_kernel, out_shape=[jax.ShapeDtypeStruct(shape, kin...  26.8 us
    pallas_call x1, Pallas kernels, attention_backward(): pl.pallas_call(backward_kernel, out_shape=[jax.ShapeDtypeStruct((length,...  26.6 us
    unnamed x194, local copies, waits for them, and re-layouts  23.1 us
    dynamic_update_slice x64, other arithmetic, place(): lax.dynamic_update_slice(store[0], value.astype(F32), (index * rows, 0))  18.3 us
  transfers between devices with their start and end apart: 150, of which 83 were waited for; matrix products, arithmetic and copies ran while one was open for 22% of the time, Pallas kernels for 7%

profile of v1, /device:TPU:0, one launch (start us, length us, event | category | flops | bytes accessed | tf_op | source)
XLA Modules:
  0.0 804.5 jit_solution(8566776878726177173)
XLA Ops:
  0.7 4.4 copy.225
  5.1 4.3 copy.222
  32.7 8.0 collective-permute-done.2
  55.4 40.8 %collective-permute-done.5 = bf16[512,1024]{1,0:T(8,128)(2,1)S(1)} collective-permute-done((bf16[512,1024]{1,0:T(8,128)(2,1)S(1)}, bf16[512,1024]{1,0:T(8,128)(2,1)S(1)}, u32[]{:S(2)}, u32[]{:S(2)}) %collective-permute-start.5) | collective-permute-done | bytes 1048608 | tf_op jit(solution)/shard_map/ppermute | solution.py:286
  101.5 26.8 %attention_forward.1 = (bf16[1024,512]{1,0:T(8,128)(2,1)S(1)}, bf16[768,1024]{1,0:T(8,128)(2,1)S(1)}, bf16[4,1024,64]{2,1,0:T(8,128)(2,1)S(1)}, bf16[1024,256]{1...) custom-call(bf16[1024,1024]{1,0:T(8,128)(2,1)} %fusion.1.hidden_ref,, ...), custom_call_target="tpu_custom_call" | custom-call | flops 12000000000 | bytes 16777216 | tf_op jit(solution)/shard_map/attention_forward/pallas_call | solution.py:235
  218.3 8.9 %fusion.19 = f32[1024,2304]{1,0:T(8,128)} fusion(bf16[512,1024]{1,0:T(8,128)(2,1)S(1)} %collective-permute-done.8, bf16[512,1024]{1,0:T(8,128)(2,1)} %multiply_convert_fusion.6, bf16[512,2304]{0,1:T(8,128)(2,1)S(1)} %get-tuple-element.54, bf16[512,2304]{0,1:T(8,128)(2,1)S(1)} %get-tuple-element.53), kind=kOutput, calls=%fused_computation.78 | convolution fusion | flops 4845469696 | bytes 16252928 | tf_op jit(solution)/shard_map/dot_general | solution.py:28
  227.2 9.9 %multiply_convert_fusion.3 = (bf16[1024,1152]{1,0:T(8,128)(2,1)}, bf16[1024,1152]{1,0:T(8,128)(2,1)}, bf16[1024,1152]{1,0:T(8,128)(2,1)S(1)}) fusion(f32[1024,2304]{1,0:T(8,128)} %fusion.19, bf16[1152,1024]{1,0:T(8,128)(2,1)S(1)} %copy-done, bf16[512,1024]{1,0:T(8,128)(2,1)S(1)} %collective-permute-done.17, bf16[256,1024]{1,0:T(8,128)(2,1)S(1)} %get-tuple-element.73, ...), kind=kOutput, calls=%fused_computation.11 | convolution fusion | flops 2441084928 | bytes 20971520 | tf_op jit(solution)/shard_map/dot_general | solution.py:28
  237.1 4.4 fusion.140
  241.6 7.5 fusion.120
  249.1 8.3 %multiply_convert_fusion.1 = (bf16[1024,1152]{1,0:T(8,128)(2,1)S(1)}, bf16[1024,1152]{1,0:T(8,128)(2,1)S(1)}, bf16[1024,1152]{1,0:T(8,128)(2,1)S(1)}) fusion(f32[1024,2304]{1,0:T(8,128)} %fusion.120, bf16[1152,1024]{1,0:T(8,128)(2,1)S(1)} %copy-done, bf16[512,1024]{1,0:T(8,128)(2,1)S(1)} %collective-permute-done.19, ...), kind=kOutput, calls=%fused_computation.9 | convolution fusion | flops 2441084928 | bytes 20971520 | tf_op jit(solution)/shard_map/dot_general | solution.py:28
  257.4 4.4 fusion.141
  271.1 5.0 fusion.4
  276.2 7.0 fusion.2
  283.2 6.7 fusion.3
  290.0 7.6 add_convert_fusion
  308.4 3.6 collective-permute-done.123
  313.6 3.7 collective-permute-done.137
  319.7 4.0 collective-permute-done.124
  326.3 4.1 collective-permute-done.125
  338.3 5.9 collective-permute-done.91
  351.6 4.0 collective-permute-done.127
  356.8 3.9 collective-permute-done.141
  362.1 8.1 %collective-permute-done.92 = bf16[4,32,1152]{2,1,0:T(8,128)(2,1)S(1)} collective-permute-done((bf16[4,32,1152]{2,1,0:T(8,128)(2,1)S(1)}, bf16[4,32,1152]{2,1,0:T(8,128)(2,1)S(1)}, u32[]{:S(2)}, u32[]{:S(2)}) %collective-permute-start.92) | collective-permute-done | bytes 294944 | tf_op jit(solution)/shard_map/ppermute | solution.py:313
  371.6 4.2 collective-permute-done.128
  385.9 7.6 collective-permute-done.129
  394.9 3.7 collective-permute-done.143
  408.4 4.5 collective-permute-done.131
  419.7 7.4 collective-permute-done.94
  432.3 6.7 collective-permute-done.133
  440.7 4.9 collective-permute-done.147
  447.0 5.4 collective-permute-done.95
  458.2 4.5 collective-permute-done.135
  484.9 25.9 %collective-permute-done.114 = bf16[2,32,1152]{2,1,0:T(8,128)(2,1)S(1)} collective-permute-done((bf16[2,32,1152]{2,1,0:T(8,128)(2,1)S(1)}, bf16[2,32,1152]{2,1,0:T(8,128)(2,1)S(1)}, u32[]{:S(2)}, u32[]{:S(2)}) %collective-permute-start.114) | collective-permute-done | bytes 147488 | tf_op jit(solution)/shard_map/ppermute | solution.py:286
  525.4 4.5 collective-permute-done.116
  542.9 26.6 %attention_backward.1 = (bf16[1024,1024]{1,0:T(8,128)(2,1)}, f32[64,2]{1,0:T(8,128)}) custom-call(bf16[1024,512]{1,0:T(8,128)(2,1)} %convolution_convert_fusion.grad_ref, bf16[768,1024]{1,0:T(8,128)(2,1)} %copy-done.7, bf16[4,1024,64]{2,1,0:T(8,128)(2,1)} %copy-done.8, bf16[1024,256]{1,0:T(8,128)(2,1)} %copy-done.9, ...), custom_call_target="tpu_custom_call" | custom-call | flops 24999999488 | bytes 16777216 | tf_op jit(solution)/shard_map/attention_backward/pallas_call | solution.py:252
  569.5 4.0 fusion.142
  578.1 4.0 fusion.121
  618.0 3.5 collective-permute-done.64
  633.8 3.7 collective-permute-done.66
  647.9 6.4 collective-permute-done.68
  658.7 3.5 collective-permute-done.69
  666.4 3.7 collective-permute-done.70
  674.4 3.6 collective-permute-done.71
  682.4 3.6 collective-permute-done.72
  690.7 3.6 collective-permute-done.73
  698.5 3.6 collective-permute-done.74
  706.3 3.6 collective-permute-done.75
  735.9 4.4 collective-permute-done.29
  (734 shorter events, 389.7 us)
Async XLA Ops:
  14.0 116.2 %collective-permute-start.9 = (bf16[256,2,2304]{0,2,1:T(8,128)(2,1)}, bf16[256,2,2304]{0,2,1:T(8,128)(2,1)}, u32[]{:S(2)}, u32[]{:S(2)}) collective-permute-start(bf16[256,2,2304]{0,2,1:T(8,128)(2,1)} %pad_maximum_fusion.10), channel_id=1, source_target_pairs={{0,1},{1,0},{2,3},{3,2},{4,5},{5,4},{6,7},{7,6},{8,9},{9,8},{10,11... | collective-permute-start | bytes 7077896 | tf_op jit(solution)/shard_map/ppermute | solution.py:290
  23.7 24.1 %collective-permute-start.4 = (bf16[256,1024]{1,0:T(8,128)(2,1)}, bf16[256,1024]{1,0:T(8,128)(2,1)}, u32[]{:S(2)}, u32[]{:S(2)}) collective-permute-start(bf16[256,1024]{1,0:T(8,128)(2,1)} %pad_maximum_fusion.33), channel_id=1, source_target_pairs={{0,1},{1,0},{2,3},{3,2},{4,5},{5,4},{6,7},{7,6},{8,9},{9,8},{10,11... | collective-permute-start | bytes 1572872 | tf_op jit(solution)/shard_map/ppermute | solution.py:290
  24.6 19.5 %collective-permute-start = (bf16[256,1024]{1,0:T(8,128)(2,1)}, bf16[256,1024]{1,0:T(8,128)(2,1)}, u32[]{:S(2)}, u32[]{:S(2)}) collective-permute-start(bf16[256,1024]{1,0:T(8,128)(2,1)} %select_bitcast_fusion.11), channel_id=1, source_target_pairs={{0,2},{2,0},{1,3},{3,1},{4,6},{6,4},{5,7},{7,5},{8,10},{10,8},{9,1... | collective-permute-start | bytes 1572872 | tf_op jit(solution)/shard_map/ppermute | solution.py:286
  27.7 13.0 %collective-permute-start.2 = (f32[6,256]{1,0:T(8,128)S(1)}, f32[6,256]{1,0:T(8,128)S(1)}, u32[]{:S(2)}, u32[]{:S(2)}) collective-permute-start(f32[6,256]{1,0:T(8,128)S(1)} %pad_maximum_fusion.40), channel_id=1, source_target_pairs={{0,2},{2,0},{1,3},{3,1},{4,6},{6,4},{5,7},{7,5},{8,10},{10,8},{9,1... | collective-permute-start | bytes 18440 | tf_op jit(solution)/shard_map/ppermute | solution.py:286
  27.8 24.3 %collective-permute-start.6 = (bf16[256,1024]{1,0:T(8,128)(2,1)}, bf16[256,1024]{1,0:T(8,128)(2,1)}, u32[]{:S(2)}, u32[]{:S(2)}) collective-permute-start(bf16[256,1024]{1,0:T(8,128)(2,1)} %param.29), channel_id=1, source_target_pairs={{0,2},{2,0},{1,3},{3,1},{4,6},{6,4},{5,7},{7,5},{8,10},{10,8},{9,1... | collective-permute-start | bytes 1572872 | tf_op jit(solution)/shard_map/ppermute | solution.py:286
  42.0 168.4 %collective-permute-start.16 = (bf16[2,256,1024]{2,1,0:T(8,128)(2,1)}, bf16[2,256,1024]{2,1,0:T(8,128)(2,1)}, u32[]{:S(2)}, u32[]{:S(2)}) collective-permute-start(bf16[2,256,1024]{2,1,0:T(8,128)(2,1)} %param.22), channel_id=1, source_target_pairs={{0,2},{2,0},{1,3},{3,1},{4,6},{6,4},{5,7},{7,5},{8,10},{10,8},{9,1... | collective-permute-start | bytes 3145736 | tf_op jit(solution)/shard_map/ppermute | solution.py:286
  49.3 47.0 %collective-permute-start.5 = (bf16[512,1024]{1,0:T(8,128)(2,1)S(1)}, bf16[512,1024]{1,0:T(8,128)(2,1)S(1)}, u32[]{:S(2)}, u32[]{:S(2)}) collective-permute-start(bf16[512,1024]{1,0:T(8,128)(2,1)S(1)} %pad_maximum_fusion.20), channel_id=1, source_target_pairs={{0,2},{2,0},{1,3},{3,1},{4,6},{6,4},{5,7},{7,5},{8,10},{10,8},{9,1... | collective-permute-start | bytes 3145736 | tf_op jit(solution)/shard_map/ppermute | solution.py:286
  137.0 78.1 %collective-permute-start.10 = (bf16[512,2304]{0,1:T(8,128)(2,1)}, bf16[512,2304]{0,1:T(8,128)(2,1)}, u32[]{:S(2)}, u32[]{:S(2)}) collective-permute-start(bf16[512,2304]{0,1:T(8,128)(2,1)} %select_bitcast_fusion), channel_id=1, source_target_pairs={{0,2},{2,0},{1,3},{3,1},{4,6},{6,4},{5,7},{7,5},{8,10},{10,8},{9,1... | collective-permute-start | bytes 7077896 | tf_op jit(solution)/shard_map/ppermute | solution.py:286
  142.3 70.7 %collective-permute-start.12 = (bf16[512,1024]{1,0:T(8,128)(2,1)}, bf16[512,1024]{1,0:T(8,128)(2,1)}, u32[]{:S(2)}, u32[]{:S(2)}) collective-permute-start(bf16[512,1024]{1,0:T(8,128)(2,1)} %multiply_convert_fusion.6), channel_id=1, source_target_pairs={{0,2},{2,0},{1,3},{3,1},{4,6},{6,4},{5,7},{7,5},{8,10},{10,8},{9,1... | collective-permute-start | bytes 3145736 | tf_op jit(solution)/shard_map/ppermute | solution.py:286
  212.2 15.0 %collective-permute-start.17 = (bf16[512,1024]{1,0:T(8,128)(2,1)S(1)}, bf16[512,1024]{1,0:T(8,128)(2,1)S(1)}, u32[]{:S(2)}, u32[]{:S(2)}) collective-permute-start(bf16[512,1024]{1,0:T(8,128)(2,1)S(1)} %pad_maximum_fusion.24), channel_id=1, source_target_pairs={{0,1},{1,0},{2,3},{3,2},{4,5},{5,4},{6,7},{7,6},{8,9},{9,8},{10,11... | collective-permute-start | bytes 3145736 | tf_op jit(solution)/shard_map/ppermute | solution.py:290
  212.3 36.8 %collective-permute-start.19 = (bf16[512,1024]{1,0:T(8,128)(2,1)S(1)}, bf16[512,1024]{1,0:T(8,128)(2,1)S(1)}, u32[]{:S(2)}, u32[]{:S(2)}) collective-permute-start(bf16[512,1024]{1,0:T(8,128)(2,1)S(1)} %pad_maximum_fusion.25), channel_id=1, source_target_pairs={{0,1},{1,0},{2,3},{3,2},{4,5},{5,4},{6,7},{7,6},{8,9},{9,8},{10,11... | collective-permute-start | bytes 3145736 | tf_op jit(solution)/shard_map/ppermute | solution.py:290
  215.1 26.4 %collective-permute-start.13 = (bf16[512,1024]{1,0:T(8,128)(2,1)}, bf16[512,1024]{1,0:T(8,128)(2,1)S(1)}, u32[]{:S(2)}, u32[]{:S(2)}) collective-permute-start(bf16[512,1024]{1,0:T(8,128)(2,1)} %collective-permute-done.12), channel_id=1, source_target_pairs={{0,1},{1,0},{2,3},{3,2},{4,5},{5,4},{6,7},{7,6},{8,9},{9,8},{10,11... | collective-permute-start | bytes 3145736 | tf_op jit(solution)/shard_map/ppermute | solution.py:290
  268.2 36.6 %collective-permute-start.122 = (bf16[144,512]{1,0:T(8,128)(2,1)S(1)}, bf16[144,512]{1,0:T(8,128)(2,1)}, u32[]{:S(2)}, u32[]{:S(2)}) collective-permute-start(bf16[144,512]{1,0:T(8,128)(2,1)S(1)} %dynamic-slice_bitcast_fusion.3), channel_id=1, source_target_pairs={{0,8},{8,16},{16,24},{24,28},{28,20},{20,12},{12,4},{4,0},{1,9},{9... | collective-permute-start | bytes 442376 | tf_op jit(solution)/shard_map/ppermute | solution.py:313
  269.8 36.1 %collective-permute-start.136 = (bf16[144,512]{1,0:T(8,128)(2,1)S(1)}, bf16[144,512]{1,0:T(8,128)(2,1)}, u32[]{:S(2)}, u32[]{:S(2)}) collective-permute-start(bf16[144,512]{1,0:T(8,128)(2,1)S(1)} %dynamic-slice_bitcast_fusion.2), channel_id=1, source_target_pairs={{4,12},{12,20},{20,28},{28,24},{24,16},{16,8},{8,0},{0,4},{5,13},{... | collective-permute-start | bytes 442376 | tf_op jit(solution)/shard_map/ppermute | solution.py:313
  298.1 19.3 %collective-permute-start.106 = (bf16[4,32,1152]{2,1,0:T(8,128)(2,1)S(1)}, bf16[4,32,1152]{2,1,0:T(8,128)(2,1)S(1)}, u32[]{:S(2)}, u32[]{:S(2)}) collective-permute-start(bf16[4,32,1152]{2,1,0:T(8,128)(2,1)S(1)} %dynamic-slice_bitcast_fusion), channel_id=1, source_target_pairs={{4,12},{12,20},{20,28},{28,24},{24,16},{16,8},{8,0},{0,4},{5,13},{... | collective-permute-start | bytes 884744 | tf_op jit(solution)/shard_map/ppermute | solution.py:313
  299.7 18.9 %collective-permute-start.90 = (bf16[4,32,1152]{2,1,0:T(8,128)(2,1)S(1)}, bf16[4,32,1152]{2,1,0:T(8,128)(2,1)S(1)}, u32[]{:S(2)}, u32[]{:S(2)}) collective-permute-start(bf16[4,32,1152]{2,1,0:T(8,128)(2,1)S(1)} %dynamic-slice_bitcast_fusion.1), channel_id=1, source_target_pairs={{0,8},{8,16},{16,24},{24,28},{28,20},{20,12},{12,4},{4,0},{1,9},{9... | collective-permute-start | bytes 884744 | tf_op jit(solution)/shard_map/ppermute | solution.py:313
  300.4 174.7 %collective-permute-start.18 = (bf16[512,1024]{1,0:T(8,128)(2,1)S(1)}, bf16[512,1024]{1,0:T(8,128)(2,1)S(1)}, u32[]{:S(2)}, u32[]{:S(2)}) collective-permute-start(bf16[512,1024]{1,0:T(8,128)(2,1)S(1)} %slice.683), channel_id=1, source_target_pairs={{0,1},{1,0},{2,3},{3,2},{4,5},{5,4},{6,7},{7,6},{8,9},{9,8},{10,11... | collective-permute-start | bytes 3145736 | tf_op jit(solution)/shard_map/ppermute | solution.py:290
  304.7 78.6 %collective-permute-start.20 = (bf16[512,1024]{1,0:T(8,128)(2,1)S(1)}, bf16[512,1024]{1,0:T(8,128)(2,1)S(1)}, u32[]{:S(2)}, u32[]{:S(2)}) collective-permute-start(bf16[512,1024]{1,0:T(8,128)(2,1)S(1)} %slice.682), channel_id=1, source_target_pairs={{0,1},{1,0},{2,3},{3,2},{4,5},{5,4},{6,7},{7,6},{8,9},{9,8},{10,11... | collective-permute-start | bytes 3145736 | tf_op jit(solution)/shard_map/ppermute | solution.py:290
  317.3 158.7 %collective-permute-start.11 = (bf16[512,1024]{1,0:T(8,128)(2,1)S(1)}, bf16[512,1024]{1,0:T(8,128)(2,1)S(1)}, u32[]{:S(2)}, u32[]{:S(2)}) collective-permute-start(bf16[512,1024]{1,0:T(8,128)(2,1)S(1)} %slice.685), channel_id=1, source_target_pairs={{0,1},{1,0},{2,3},{3,2},{4,5},{5,4},{6,7},{7,6},{8,9},{9,8},{10,11... | collective-permute-start | bytes 3145736 | tf_op jit(solution)/shard_map/ppermute | solution.py:290
  323.7 12.9 %collective-permute-start.107 = (bf16[4,32,1152]{2,1,0:T(8,128)(2,1)S(1)}, bf16[4,32,1152]{2,1,0:T(8,128)(2,1)S(1)}, u32[]{:S(2)}, u32[]{:S(2)}) collective-permute-start(bf16[4,32,1152]{2,1,0:T(8,128)(2,1)S(1)} %fusion.30), channel_id=1, source_target_pairs={{4,12},{12,20},{20,28},{28,24},{24,16},{16,8},{8,0},{0,4},{5,13},{... | collective-permute-start | bytes 884744 | tf_op jit(solution)/shard_map/ppermute | solution.py:313
  345.8 15.0 %collective-permute-start.108 = (bf16[4,32,1152]{2,1,0:T(8,128)(2,1)S(1)}, bf16[4,32,1152]{2,1,0:T(8,128)(2,1)S(1)}, u32[]{:S(2)}, u32[]{:S(2)}) collective-permute-start(bf16[4,32,1152]{2,1,0:T(8,128)(2,1)S(1)} %fusion.31), channel_id=1, source_target_pairs={{4,12},{12,20},{20,28},{28,24},{24,16},{16,8},{8,0},{0,4},{5,13},{... | collective-permute-start | bytes 884744 | tf_op jit(solution)/shard_map/ppermute | solution.py:313
  360.7 23.0 %collective-permute-start.14 = (bf16[512,1024]{1,0:T(8,128)(2,1)S(1)}, bf16[512,1024]{1,0:T(8,128)(2,1)S(1)}, u32[]{:S(2)}, u32[]{:S(2)}) collective-permute-start(bf16[512,1024]{1,0:T(8,128)(2,1)S(1)} %slice.684), channel_id=1, source_target_pairs={{0,1},{1,0},{2,3},{3,2},{4,5},{5,4},{6,7},{7,6},{8,9},{9,8},{10,11... | collective-permute-start | bytes 3145736 | tf_op jit(solution)/shard_map/ppermute | solution.py:290
  380.9 19.5 %collective-permute-start.109 = (bf16[4,32,1152]{2,1,0:T(8,128)(2,1)S(1)}, bf16[4,32,1152]{2,1,0:T(8,128)(2,1)S(1)}, u32[]{:S(2)}, u32[]{:S(2)}) collective-permute-start(bf16[4,32,1152]{2,1,0:T(8,128)(2,1)S(1)} %fusion.32), channel_id=1, source_target_pairs={{4,12},{12,20},{20,28},{28,24},{24,16},{16,8},{8,0},{0,4},{5,13},{... | collective-permute-start | bytes 884744 | tf_op jit(solution)/shard_map/ppermute | solution.py:313
  383.3 17.3 %collective-permute-start.93 = (bf16[4,32,1152]{2,1,0:T(8,128)(2,1)S(1)}, bf16[4,32,1152]{2,1,0:T(8,128)(2,1)S(1)}, u32[]{:S(2)}, u32[]{:S(2)}) collective-permute-start(bf16[4,32,1152]{2,1,0:T(8,128)(2,1)S(1)} %fusion.39), channel_id=1, source_target_pairs={{0,8},{8,16},{16,24},{24,28},{28,20},{20,12},{12,4},{4,0},{1,9},{9... | collective-permute-start | bytes 884744 | tf_op jit(solution)/shard_map/ppermute | solution.py:313
  398.6 76.6 %collective-permute-start.21 = (bf16[512,1024]{1,0:T(8,128)(2,1)S(1)}, bf16[512,1024]{1,0:T(8,128)(2,1)S(1)}, u32[]{:S(2)}, u32[]{:S(2)}) collective-permute-start(bf16[512,1024]{1,0:T(8,128)(2,1)S(1)} %fusion.6), channel_id=1, source_target_pairs={{0,2},{2,0},{1,3},{3,1},{4,6},{6,4},{5,7},{7,5},{8,10},{10,8},{9,1... | collective-permute-start | bytes 3145736 | tf_op jit(solution)/shard_map/ppermute | solution.py:286
  406.2 12.4 %collective-permute-start.110 = (bf16[4,32,1152]{2,1,0:T(8,128)(2,1)S(1)}, bf16[4,32,1152]{2,1,0:T(8,128)(2,1)S(1)}, u32[]{:S(2)}, u32[]{:S(2)}) collective-permute-start(bf16[4,32,1152]{2,1,0:T(8,128)(2,1)S(1)} %fusion.33), channel_id=1, source_target_pairs={{4,12},{12,20},{20,28},{28,24},{24,16},{16,8},{8,0},{0,4},{5,13},{... | collective-permute-start | bytes 884744 | tf_op jit(solution)/shard_map/ppermute | solution.py:313
  418.6 10.6 %collective-permute-start.132 = (bf16[144,512]{1,0:T(8,128)(2,1)S(1)}, bf16[144,512]{1,0:T(8,128)(2,1)S(1)}, u32[]{:S(2)}, u32[]{:S(2)}) collective-permute-start(bf16[144,512]{1,0:T(8,128)(2,1)S(1)} %collective-permute-done.131), channel_id=1, source_target_pairs={{0,8},{8,16},{16,24},{24,28},{28,20},{20,12},{12,4},{4,0},{1,9},{9... | collective-permute-start | bytes 442376 | tf_op jit(solution)/shard_map/ppermute | solution.py:313
  429.2 16.5 %collective-permute-start.111 = (bf16[4,32,1152]{2,1,0:T(8,128)(2,1)S(1)}, bf16[4,32,1152]{2,1,0:T(8,128)(2,1)S(1)}, u32[]{:S(2)}, u32[]{:S(2)}) collective-permute-start(bf16[4,32,1152]{2,1,0:T(8,128)(2,1)S(1)} %fusion.34), channel_id=1, source_target_pairs={{4,12},{12,20},{20,28},{28,24},{24,16},{16,8},{8,0},{0,4},{5,13},{... | collective-permute-start | bytes 884744 | tf_op jit(solution)/shard_map/ppermute | solution.py:313
  454.3 17.1 %collective-permute-start.112 = (bf16[4,32,1152]{2,1,0:T(8,128)(2,1)S(1)}, bf16[4,32,1152]{2,1,0:T(8,128)(2,1)S(1)}, u32[]{:S(2)}, u32[]{:S(2)}) collective-permute-start(bf16[4,32,1152]{2,1,0:T(8,128)(2,1)S(1)} %fusion.35), channel_id=1, source_target_pairs={{4,12},{12,20},{20,28},{28,24},{24,16},{16,8},{8,0},{0,4},{5,13},{... | collective-permute-start | bytes 884744 | tf_op jit(solution)/shard_map/ppermute | solution.py:313
  471.5 11.0 %collective-permute-start.113 = (bf16[2,32,1152]{2,1,0:T(8,128)(2,1)S(1)}, bf16[2,32,1152]{2,1,0:T(8,128)(2,1)S(1)}, u32[]{:S(2)}, u32[]{:S(2)}) collective-permute-start(bf16[2,32,1152]{2,1,0:T(8,128)(2,1)S(1)} %select_bitcast_fusion.13), channel_id=1, source_target_pairs={{0,1},{1,0},{2,3},{3,2},{4,5},{5,4},{6,7},{7,6},{8,9},{9,8},{10,11... | collective-permute-start | bytes 442376 | tf_op jit(solution)/shard_map/ppermute | solution.py:290
  479.7 55.8 %collective-permute-start.22 = (bf16[2,256,1024]{2,1,0:T(8,128)(2,1)}, bf16[2,256,1024]{2,1,0:T(8,128)(2,1)}, u32[]{:S(2)}, u32[]{:S(2)}) collective-permute-start(bf16[2,256,1024]{2,1,0:T(8,128)(2,1)} %bitcast.41), channel_id=1, source_target_pairs={{0,1},{1,0},{2,3},{3,2},{4,5},{5,4},{6,7},{7,6},{8,9},{9,8},{10,11... | collective-permute-start | bytes 3145736 | tf_op jit(solution)/shard_map/ppermute | solution.py:290
  481.4 100.9 %collective-permute-start.15 = (bf16[2,256,1024]{2,1,0:T(8,128)(2,1)}, bf16[2,256,1024]{2,1,0:T(8,128)(2,1)}, u32[]{:S(2)}, u32[]{:S(2)}) collective-permute-start(bf16[2,256,1024]{2,1,0:T(8,128)(2,1)} %pad_maximum_fusion.22), channel_id=1, source_target_pairs={{0,2},{2,0},{1,3},{3,1},{4,6},{6,4},{5,7},{7,5},{8,10},{10,8},{9,1... | collective-permute-start | bytes 3145736 | tf_op jit(solution)/shard_map/ppermute | solution.py:286
  482.6 28.1 %collective-permute-start.114 = (bf16[2,32,1152]{2,1,0:T(8,128)(2,1)S(1)}, bf16[2,32,1152]{2,1,0:T(8,128)(2,1)S(1)}, u32[]{:S(2)}, u32[]{:S(2)}) collective-permute-start(bf16[2,32,1152]{2,1,0:T(8,128)(2,1)S(1)} %select_bitcast_fusion.12), channel_id=1, source_target_pairs={{0,2},{2,0},{1,3},{3,1},{4,6},{6,4},{5,7},{7,5},{8,10},{10,8},{9,1... | collective-permute-start | bytes 442376 | tf_op jit(solution)/shard_map/ppermute | solution.py:286
  483.7 29.6 %collective-permute-start.98 = (bf16[2,32,1152]{2,1,0:T(8,128)(2,1)S(1)}, bf16[2,32,1152]{2,1,0:T(8,128)(2,1)S(1)}, u32[]{:S(2)}, u32[]{:S(2)}) collective-permute-start(bf16[2,32,1152]{2,1,0:T(8,128)(2,1)S(1)} %fusion.65), channel_id=1, source_target_pairs={{0,2},{2,0},{1,3},{3,1},{4,6},{6,4},{5,7},{7,5},{8,10},{10,8},{9,1... | collective-permute-start | bytes 442376 | tf_op jit(solution)/shard_map/ppermute | solution.py:286
  529.9 57.0 %collective-permute-start.117 = (bf16[32,4608]{1,0:T(8,128)(2,1)}, bf16[32,4608]{1,0:T(8,128)(2,1)}, u32[]{:S(2)}, u32[]{:S(2)}) collective-permute-start(bf16[32,4608]{1,0:T(8,128)(2,1)} %collective-permute-done.116), channel_id=1, source_target_pairs={{4,12},{12,20},{20,28},{28,24},{24,16},{16,8},{8,0},{0,4},{5,13},{... | collective-permute-start | bytes 884744 | tf_op jit(solution)/shard_map/ppermute | solution.py:313
  531.4 57.1 %collective-permute-start.101 = (bf16[32,4608]{1,0:T(8,128)(2,1)}, bf16[32,4608]{1,0:T(8,128)(2,1)}, u32[]{:S(2)}, u32[]{:S(2)}) collective-permute-start(bf16[32,4608]{1,0:T(8,128)(2,1)} %collective-permute-done.100), channel_id=1, source_target_pairs={{0,8},{8,16},{16,24},{24,28},{28,20},{20,12},{12,4},{4,0},{1,9},{9... | collective-permute-start | bytes 884744 | tf_op jit(solution)/shard_map/ppermute | solution.py:313
  542.1 57.5 %collective-permute-start.61 = (bf16[256,1024]{1,0:T(8,128)(2,1)}, bf16[256,1024]{1,0:T(8,128)(2,1)}, u32[]{:S(2)}, u32[]{:S(2)}) collective-permute-start(bf16[256,1024]{1,0:T(8,128)(2,1)} %select_convert_fusion.3), channel_id=1, source_target_pairs={{0,2},{2,0},{1,3},{3,1},{4,6},{6,4},{5,7},{7,5},{8,10},{10,8},{9,1... | collective-permute-start | bytes 1572872 | tf_op jit(solution)/shard_map/ppermute | solution.py:286
  576.7 141.9 %collective-permute-start.30 = (bf16[512,1024]{1,0:T(8,128)(2,1)}, bf16[512,1024]{1,0:T(8,128)(2,1)}, u32[]{:S(2)}, u32[]{:S(2)}) collective-permute-start(bf16[512,1024]{1,0:T(8,128)(2,1)} %select_convert_fusion), channel_id=1, source_target_pairs={{0,2},{2,0},{1,3},{3,1},{4,6},{6,4},{5,7},{7,5},{8,10},{10,8},{9,1... | collective-permute-start | bytes 3145736 | tf_op jit(solution)/shard_map/ppermute | solution.py:286
  582.3 138.7 %collective-permute-start.23 = (bf16[512,1024]{1,0:T(8,128)(2,1)S(1)}, bf16[512,1024]{1,0:T(8,128)(2,1)S(1)}, u32[]{:S(2)}, u32[]{:S(2)}) collective-permute-start(bf16[512,1024]{1,0:T(8,128)(2,1)S(1)} %bitcast.694), channel_id=1, source_target_pairs={{0,1},{1,0},{2,3},{3,2},{4,5},{5,4},{6,7},{7,6},{8,9},{9,8},{10,11... | collective-permute-start | bytes 3145736 | tf_op jit(solution)/shard_map/ppermute | solution.py:290
  595.8 46.2 %collective-permute-start.119 = (bf16[32,4608]{1,0:T(8,128)(2,1)S(1)}, bf16[32,4608]{1,0:T(8,128)(2,1)S(1)}, u32[]{:S(2)}, u32[]{:S(2)}) collective-permute-start(bf16[32,4608]{1,0:T(8,128)(2,1)S(1)} %collective-permute-done.118), channel_id=1, source_target_pairs={{4,12},{12,20},{20,28},{28,24},{24,16},{16,8},{8,0},{0,4},{5,13},{... | collective-permute-start | bytes 884744 | tf_op jit(solution)/shard_map/ppermute | solution.py:313
  597.3 47.1 %collective-permute-start.103 = (bf16[32,4608]{1,0:T(8,128)(2,1)S(1)}, bf16[32,4608]{1,0:T(8,128)(2,1)S(1)}, u32[]{:S(2)}, u32[]{:S(2)}) collective-permute-start(bf16[32,4608]{1,0:T(8,128)(2,1)S(1)} %collective-permute-done.102), channel_id=1, source_target_pairs={{0,8},{8,16},{16,24},{24,28},{28,20},{20,12},{12,4},{4,0},{1,9},{9... | collective-permute-start | bytes 884744 | tf_op jit(solution)/shard_map/ppermute | solution.py:313
  644.4 70.6 %collective-permute-start.120 = (bf16[32,4608]{1,0:T(8,128)(2,1)S(1)}, bf16[32,4608]{1,0:T(8,128)(2,1)S(1)}, u32[]{:S(2)}, u32[]{:S(2)}) collective-permute-start(bf16[32,4608]{1,0:T(8,128)(2,1)S(1)} %collective-permute-done.119), channel_id=1, source_target_pairs={{4,12},{12,20},{20,28},{28,24},{24,16},{16,8},{8,0},{0,4},{5,13},{... | collective-permute-start | bytes 884744 | tf_op jit(solution)/shard_map/ppermute | solution.py:313
  646.9 70.5 %collective-permute-start.104 = (bf16[32,4608]{1,0:T(8,128)(2,1)S(1)}, bf16[32,4608]{1,0:T(8,128)(2,1)S(1)}, u32[]{:S(2)}, u32[]{:S(2)}) collective-permute-start(bf16[32,4608]{1,0:T(8,128)(2,1)S(1)} %collective-permute-done.103), channel_id=1, source_target_pairs={{0,8},{8,16},{16,24},{24,28},{28,20},{20,12},{12,4},{4,0},{1,9},{9... | collective-permute-start | bytes 884744 | tf_op jit(solution)/shard_map/ppermute | solution.py:313
  714.9 38.3 %collective-permute-start.121 = (bf16[32,4608]{1,0:T(8,128)(2,1)S(1)}, bf16[32,4608]{1,0:T(8,128)(2,1)S(1)}, u32[]{:S(2)}, u32[]{:S(2)}) collective-permute-start(bf16[32,4608]{1,0:T(8,128)(2,1)S(1)} %collective-permute-done.120), channel_id=1, source_target_pairs={{4,12},{12,20},{20,28},{28,24},{24,16},{16,8},{8,0},{0,4},{5,13},{... | collective-permute-start | bytes 884744 | tf_op jit(solution)/shard_map/ppermute | solution.py:313
  717.5 36.6 %collective-permute-start.105 = (bf16[32,4608]{1,0:T(8,128)(2,1)S(1)}, bf16[32,4608]{1,0:T(8,128)(2,1)S(1)}, u32[]{:S(2)}, u32[]{:S(2)}) collective-permute-start(bf16[32,4608]{1,0:T(8,128)(2,1)S(1)} %collective-permute-done.104), channel_id=1, source_target_pairs={{0,8},{8,16},{16,24},{24,28},{28,20},{20,12},{12,4},{4,0},{1,9},{9... | collective-permute-start | bytes 884744 | tf_op jit(solution)/shard_map/ppermute | solution.py:313
  722.8 19.3 %collective-permute-start.46 = (bf16[2,32,512]{2,1,0:T(8,128)(2,1)S(1)}, bf16[2,32,512]{2,1,0:T(8,128)(2,1)S(1)}, u32[]{:S(2)}, u32[]{:S(2)}) collective-permute-start(bf16[2,32,512]{2,1,0:T(8,128)(2,1)S(1)} %fusion.88), channel_id=1, source_target_pairs={{4,12},{12,20},{20,28},{28,24},{24,16},{16,8},{8,0},{0,4},{5,13},{... | collective-permute-start | bytes 196616 | tf_op jit(solution)/shard_map/ppermute | solution.py:313
  725.2 18.0 %collective-permute-start.31 = (bf16[2,32,512]{2,1,0:T(8,128)(2,1)S(1)}, bf16[2,32,512]{2,1,0:T(8,128)(2,1)S(1)}, u32[]{:S(2)}, u32[]{:S(2)}) collective-permute-start(bf16[2,32,512]{2,1,0:T(8,128)(2,1)S(1)} %fusion.89), channel_id=1, source_target_pairs={{0,8},{8,16},{16,24},{24,28},{28,20},{20,12},{12,4},{4,0},{1,9},{9... | collective-permute-start | bytes 196616 | tf_op jit(solution)/shard_map/ppermute | solution.py:313
  740.3 32.8 %collective-permute-start.24 = (bf16[256,1024]{1,0:T(8,128)(2,1)S(1)}, bf16[256,1024]{1,0:T(8,128)(2,1)}, u32[]{:S(2)}, u32[]{:S(2)}) collective-permute-start(bf16[256,1024]{1,0:T(8,128)(2,1)S(1)} %select_convert_fusion.4), channel_id=1, source_target_pairs={{0,2},{2,0},{1,3},{3,1},{4,6},{6,4},{5,7},{7,5},{8,10},{10,8},{9,1... | collective-permute-start | bytes 1572872 | tf_op jit(solution)/shard_map/ppermute | solution.py:286
  (191 other events, 1807.0 us)

commit v2 on v1

--- a/solution.py
+++ b/solution.py
@@ -22,6 +22,7 @@
 
 Y_SWAP = [(0, 2), (2, 0), (1, 3), (3, 1)]
 CORE_SWAP = [(0, 1), (1, 0), (2, 3), (3, 2)]
+CROSS_SWAP = [(0, 3), (3, 0), (1, 2), (2, 1)]
 
 
 def contract(left, right, left_dim, right_dim):
@@ -286,8 +287,16 @@
     return lax.ppermute(value, "group", Y_SWAP)
 
 
+def swap_cross(value):
+    return lax.ppermute(value, "group", CROSS_SWAP)
+
+
 def swap_core(value):
     return lax.ppermute(value, "group", CORE_SWAP)
+
+
+def after(value, *earlier):
+    return lax.optimization_barrier((value, earlier))[0]
 
 
 def cycle_of(count):
@@ -297,52 +306,88 @@
 class Ring:
     def __init__(self, way):
         count = lax.axis_size("replica")
-        cycle = cycle_of(count)
-        if way < 0:
-            cycle = cycle[::-1]
-        places = [cycle.index(member) for member in range(count)]
+        cycle = cycle_of(count)[::way]
         self.count = count
-        self.cycle = jnp.array(cycle, jnp.int32)
-        self.place = jnp.array(places, jnp.int32)[lax.axis_index("replica")]
+        self.way = way
         self.hops = [(cycle[at], cycle[(at + 1) % count]) for at in range(count)]
+        mine = lax.axis_index("replica")
+        self.place = jnp.where(lax.rem(mine, 2) == 0, mine // 2, count - 1 - mine // 2)
 
     def chunk_at(self, back):
-        return self.cycle[lax.rem(self.place - back + 2 * self.count, self.count)]
+        at = lax.rem(self.place - self.way * back + self.count, self.count)
+        return jnp.where(at < self.count // 2, 2 * at, 2 * (self.count - 1 - at) + 1)
 
     def send(self, value):
         return lax.ppermute(value, "replica", self.hops)
 
-    def reduce(self, pick):
-        moving = pick(self.chunk_at(1)).astype(BF)
-        for step in range(self.count - 1):
-            arrived = self.send(moving)
-            moving = (pick(self.chunk_at(step + 2)) + arrived.astype(F32)).astype(BF)
-        return moving
-
-    def gather(self, chunk, place):
-        moving = chunk
-        place(self.chunk_at(0), moving)
-        for step in range(self.count - 1):
-            moving = self.send(moving)
-            place(self.chunk_at(step + 1), moving)
-
-
-def pick_rows(whole, dim):
-    def pick(index):
-        return lax.dynamic_index_in_dim(whole, index, dim, keepdims=False).astype(F32)
-
-    return pick
-
-
-def gather_rows(ring, chunk, count):
-    rows, columns = chunk.shape
-    store = [jnp.zeros((count * rows, columns), F32)]
-
-    def place(index, value):
-        store[0] = lax.dynamic_update_slice(store[0], value.astype(F32), (index * rows, 0))
-
-    ring.gather(chunk, place)
-    return store[0]
+
+def sum_over_ring(ring, pick):
+    moving = pick(ring.chunk_at(1)).astype(BF)
+    for step in range(ring.count - 1):
+        arrived = ring.send(moving)
+        moving = (pick(ring.chunk_at(step + 2)) + arrived.astype(F32)).astype(BF)
+    return moving
+
+
+def place_kernel(step, targets, rows, index_ref, *refs):
+    chunks = refs[:2]
+    count = 1 + max(target[0] for target in targets)
+    outs = refs[-3 - count : -3]
+    wide = refs[-3:-1]
+    sems = refs[-1]
+    for side in range(2):
+        wide[side][...] = chunks[side][...].astype(F32)
+    copies = []
+    for at, (store, side, start, end, column) in enumerate(targets):
+        row = pl.multiple_of(index_ref[step, side] * rows, 8)
+        copies.append(
+            pltpu.make_async_copy(
+                wide[side].at[:, start:end],
+                outs[store].at[pl.ds(row, rows), column : column + end - start],
+                sems.at[at],
+            )
+        )
+    for copy in copies:
+        copy.start()
+    for copy in copies:
+        copy.wait()
+
+
+def place_chunks(step, indices, chunks, stores, shapes, targets):
+    rows = chunks[0].shape[0]
+    if rows % 8:
+        stores = stores or [jnp.zeros(shape, F32) for shape in shapes]
+        for store, side, start, end, column in targets:
+            stores[store] = lax.dynamic_update_slice(
+                stores[store],
+                chunks[side][:, start:end].astype(F32),
+                (indices[step, side] * rows, column),
+            )
+        return stores
+    given = stores or []
+    return list(
+        pl.pallas_call(
+            functools.partial(place_kernel, step, targets, rows),
+            out_shape=[jax.ShapeDtypeStruct(shape, F32) for shape in shapes],
+            in_specs=[pl.BlockSpec(memory_space=pltpu.SMEM)]
+            + [pl.BlockSpec(memory_space=pltpu.VMEM)] * 2
+            + [pl.BlockSpec(memory_space=pl.ANY)] * len(given),
+            out_specs=[pl.BlockSpec(memory_space=pl.ANY)] * len(shapes),
+            scratch_shapes=[pltpu.VMEM(chunk.shape, F32) for chunk in chunks]
+            + [pltpu.SemaphoreType.DMA((len(targets),))],
+            input_output_aliases={3 + at: at for at in range(len(given))},
+            compiler_params=pltpu.CompilerParams(vmem_limit_bytes=16 * 1024 * 1024),
+            name="place_chunks",
+        )(indices, *chunks, *given)
+    )
+
+
+def gather_over_rings(rings, indices, chunks, shapes, targets):
+    stores = place_chunks(0, indices, chunks, None, shapes, targets)
+    for step in range(1, rings[0].count):
+        chunks = [ring.send(chunk) for ring, chunk in zip(rings, chunks)]
+        stores = place_chunks(step, indices, chunks, stores, shapes, targets)
+    return stores
 
 
 def per_device(
@@ -383,6 +428,11 @@
     def at_core(low, high):
         return jnp.where(on_low_core, low, high), jnp.where(on_low_core, high, low)
 
+    seq_mine, seq_other = at_y(hidden_in[0], hidden_in[1])
+    seq_got = swap_y(seq_other)
+    w_query, w_key, w_value = after((w_query, w_key, w_value), seq_other)
+    w_gate, w_up, w_out = after((w_gate, w_up, w_out), seq_got)
+
     small = jnp.concatenate(
         [
             attn_gain.astype(F32)[None],
@@ -402,49 +452,52 @@
     seg = jnp.where(on_low_y, small_rows[2], small_rows[3])
     place = jnp.where(on_low_y, small_rows[4], small_rows[5])
 
-    seq_mine, seq_other = at_y(hidden_in[0], hidden_in[1])
-    own_low, own_high = by_y(seq_mine, swap_y(seq_other))
+    own_low, own_high = by_y(seq_mine, seq_got)
     own_in = jnp.stack([own_low, own_high])
     all_even, all_odd = by_core(own_in, swap_core(own_in))
     all_in = jnp.stack([all_even, all_odd], 1).reshape(4 * span, width)
 
-    def head_columns(weight):
-        rows = weight.shape[0]
-        parts = weight.reshape(rows, 2, 2, -1)
-        mine, other = at_core(parts[:, :, 0], parts[:, :, 1])
-        return mine.reshape(rows, -1), other.reshape(rows, -1)
-
-    columns = [head_columns(weight) for weight in (w_query, w_key, w_value)]
-    mine_cols = jnp.concatenate([mine for mine, other in columns], 1)
-    other_cols = jnp.concatenate([other for mine, other in columns], 1)
-    two_rows = jnp.concatenate(by_core(mine_cols, swap_core(other_cols)), 0)
-    w_attn = jnp.concatenate(by_y(two_rows, swap_y(two_rows)), 0)
+    def quarters(weight):
+        size = weight.shape[1] // 4
+        return [weight[:, at * size : (at + 1) * size] for at in range(4)]
+
+    low_cols = []
+    high_cols = []
+    for weight in (w_query, w_key, w_value):
+        parts = quarters(weight)
+        low_cols += [parts[0], parts[2]]
+        high_cols += [parts[1], parts[3]]
+    mine_cols, other_cols = at_core(jnp.concatenate(low_cols, 1), jnp.concatenate(high_cols, 1))
+    rows_core = swap_core(other_cols)
+    rows_y = swap_y(mine_cols)
+    rows_cross = swap_cross(other_cols)
+
+    def in_order(mine, at_y, sibling, across):
+        here = jnp.concatenate(by_core(mine, sibling), 0)
+        there = jnp.concatenate(by_core(at_y, across), 0)
+        return jnp.concatenate(by_y(here, there), 0)
+
+    w_attn = in_order(mine_cols, rows_y, rows_core, rows_cross)
     w_mix = jnp.concatenate(by_y(w_out, swap_y(w_out)), 0)
-
-    def unit_columns(weight):
-        rows = weight.shape[0]
-        parts = weight.reshape(rows, 2, 2, -1)
-        return at_core(parts[:, :, 0], parts[:, :, 1])
-
-    gate_mine, gate_other = unit_columns(w_gate)
-    up_mine, up_other = unit_columns(w_up)
-    ffn_mine = jnp.concatenate([gate_mine, up_mine], -1)
-    ffn_other = jnp.concatenate([gate_other, up_other], -1)
-    ffn_rows = jnp.concatenate(by_core(ffn_mine, swap_core(ffn_other)), 0)
-    ffn_here, ffn_there = at_y(ffn_rows[:, 0], ffn_rows[:, 1])
-    w_ffn = jnp.concatenate(by_y(ffn_here, swap_y(ffn_there)), 0)
-
-    dy_mine, dy_other = at_y(out_grad[0], out_grad[1])
-    dy_y = swap_y(out_grad)
-    dy_y_mine, dy_y_other = at_y(dy_y[0], dy_y[1])
-    dy_own = jnp.concatenate(by_y(dy_mine, dy_y_mine), 0)
-    dy_next = jnp.concatenate(by_y(dy_other, dy_y_other), 0)
-    dy_sib = swap_core(dy_own)
-    dy_diag = swap_core(dy_next)
-    dy_near = jnp.concatenate([dy_own, dy_sib], 0)
-    dy_far = jnp.concatenate([dy_next, dy_diag], 0)
-
-    normed_all, _ = norm_rows(all_in.astype(F32))
+    gate_parts = quarters(w_gate)
+    up_parts = quarters(w_up)
+    even = lax.rem(lax.axis_index("replica"), 2) == 0
+
+    def halves_by_y(parts):
+        pairs = [at_y(parts[at], parts[at + 2]) for at in range(2)]
+        return [pair[0] for pair in pairs], [pair[1] for pair in pairs]
+
+    gate_here, gate_there = halves_by_y(gate_parts)
+    up_here, up_there = halves_by_y(up_parts)
+    gate_mine, gate_sib = at_core(*gate_here)
+    up_mine, up_sib = at_core(*up_here)
+    one_there = [jnp.where(even, *pair) for pair in zip(gate_there, up_there)]
+    one_y, one_cross = at_core(*one_there)
+    kind_core = swap_core(jnp.concatenate([gate_sib, up_sib], 1))
+    kind_y = swap_y(one_y)
+    kind_cross = swap_cross(one_cross)
+    by_replica = [(at, at ^ 1) for at in range(copies)]
+    normed_all, inv_all = norm_rows(all_in.astype(F32))
     hidden_one = (normed_all * gain_one).astype(BF)
     freq = THETA ** (-(jnp.arange(HALF, dtype=F32) * 2.0 / HD))
     angle = freq[:, None] * place[None, :]
@@ -456,6 +509,27 @@
         hidden_one, w_attn, cosine, sine, seg_row, seg_col, gains
     )
 
+    kind_y, kind_cross = after((kind_y, kind_cross), mixed)
+    other_y = lax.ppermute(kind_y, "replica", by_replica)
+    other_cross = lax.ppermute(kind_cross, "replica", by_replica)
+
+    def both_kinds(first, second):
+        return jnp.concatenate(
+            [jnp.where(even, first, second), jnp.where(even, second, first)], 1
+        )
+
+    w_ffn = in_order(
+        jnp.concatenate([gate_mine, up_mine], 1),
+        both_kinds(kind_y, other_y),
+        kind_core,
+        both_kinds(kind_cross, other_cross),
+    )
+
+    dy_mine, dy_other = at_y(out_grad[0], out_grad[1])
+    dy_own = jnp.concatenate(by_y(dy_mine, swap_y(after(dy_other, mixed))), 0)
+    dy_sib = swap_core(dy_own)
+    dy_near = jnp.concatenate([dy_own, dy_sib], 0)
+
     def own_and_other(rows):
         parts = rows.reshape(2, 2, span, rows.shape[-1])
         mine, other = at_core(parts[:, 0], parts[:, 1])
@@ -471,6 +545,9 @@
     h2_next = swap_y(hidden_two)
     h2_sib = swap_core(hidden_two)
     h2_diag = swap_core(h2_next)
+    dy_next = jnp.concatenate(by_y(dy_other, swap_y(after(dy_mine, hidden_two))), 0)
+    dy_diag = swap_core(dy_next)
+    dy_far = jnp.concatenate([dy_next, dy_diag], 0)
     h2_near = jnp.concatenate([hidden_two, h2_sib], 0)
     h2_far = jnp.concatenate([h2_next, h2_diag], 0)
     units = hidden_units
@@ -488,27 +565,20 @@
     act_near, grad_near = ffn(h2_near, dy_near)
     act_far, grad_far = ffn(h2_far, dy_far)
     down_grad = (contract(act_near, dy_near, 0, 0) + contract(act_far, dy_far, 0, 0)).astype(BF)
+    grad_far = after(grad_far, down_grad)
     back_far = contract(grad_far, w_ffn, 1, 1)
     back_near = contract(grad_near, w_ffn, 1, 1)
     rows_own = 2 * span
     dh2_far = back_far[:rows_own] + swap_core(back_far[rows_own:].astype(BF)).astype(F32)
     dh2_near = back_near[:rows_own] + swap_core(back_near[rows_own:].astype(BF)).astype(F32)
-    grad_hidden_two = dh2_near + swap_y(dh2_far.astype(BF)).astype(F32)
+    dh2_got = swap_y(dh2_far.astype(BF))
     ffn_grad = (contract(h2_near, grad_near, 0, 0) + contract(h2_far, grad_far, 0, 0)).astype(BF)
-
-    out_near = contract(act_near, w_down, 1, 0)
-    out_far = contract(act_far, w_down, 1, 0)
-    out_own = middle + out_near[:rows_own] + swap_core(out_near[rows_own:].astype(BF)).astype(F32)
-    out_next = out_far[:rows_own] + swap_core(out_far[rows_own:].astype(BF)).astype(F32)
+    dh2_got, dh2_near = after((dh2_got, dh2_near), down_grad, ffn_grad)
+    grad_hidden_two = dh2_near + dh2_got.astype(F32)
 
     def chunk_pair(rows):
         parts = rows.reshape(2, span, width)
         return at_y(parts[0], parts[1])
-
-    own_here, own_there = chunk_pair(out_own)
-    next_here, next_there = chunk_pair(out_next)
-    out_back = swap_y(jnp.stack([own_there, next_there]).astype(BF)).astype(F32)
-    block_out = jnp.stack(by_y(own_here + out_back[1], next_here + out_back[0])).astype(BF)
 
     ffn_gain_part = jnp.sum(grad_hidden_two * normed_two, 0)
     grad_middle = dy_own.astype(F32) + norm_back(grad_hidden_two * gain_two, normed_two, inv_two)
@@ -534,21 +604,106 @@
     back_one = contract(grad_heads, w_attn, 1, 1)
     one_mine, one_other = own_and_other(back_one)
     grad_hidden_one = one_mine + swap_core(one_other.astype(BF)).astype(F32)
-    normed_one, inv_one = norm_rows(inputs)
+    inv_one, _ = own_and_other(inv_all)
+    normed_one = inputs * inv_one
     attn_gain_part = jnp.sum(grad_hidden_one * normed_one, 0)
     grad_input = grad_middle + norm_back(grad_hidden_one * gain_one, normed_one, inv_one)
     input_here, input_there = chunk_pair(grad_input)
-    input_back = swap_y(input_there.astype(BF)).astype(F32)
-    input_grad = jnp.stack(by_y(input_here, input_back))
-
+    input_back = swap_y(input_there.astype(BF))
+
+    act_near, act_far = after((act_near, act_far), back_one)
+    out_near = contract(act_near, w_down, 1, 0)
+    out_far = contract(act_far, w_down, 1, 0)
+    out_own = middle + out_near[:rows_own] + swap_core(out_near[rows_own:].astype(BF)).astype(F32)
+    out_next = out_far[:rows_own] + swap_core(out_far[rows_own:].astype(BF)).astype(F32)
+
+    own_here, own_there = chunk_pair(out_own)
+    next_here, next_there = chunk_pair(out_next)
+    out_back = swap_y(jnp.stack([own_there, next_there]).astype(BF))
     attn_grad = contract(hidden_one, grad_heads, 0, 0).reshape(2, 2 * span, -1)
     rows_here, rows_there = at_y(attn_grad[0], attn_grad[1])
     attn_grad_y = rows_here + swap_y(rows_there.astype(BF)).astype(F32)
     mix_here, mix_there = at_y(mix_grad[:span], mix_grad[span:])
     mix_grad_y = mix_here + swap_y(mix_there.astype(BF)).astype(F32)
 
+    right, left = Ring(1), Ring(-1)
+    half = width // 2
+    rows = span // copies
+
+    def replica_sum(value, dim):
+        return lax.psum_scatter(value, "replica", scatter_dimension=dim, tiled=True)
+
+    down_part = replica_sum(down_grad, 0)
+    ffn_part = replica_sum(ffn_grad.reshape(4, span, 2 * units), 1)
+
+    def own_rows(part):
+        parts = part.reshape(2, 2, rows, units)
+        mine, other = at_core(parts[:, 0], parts[:, 1])
+        both_cores = jnp.stack(by_core(mine, swap_core(other)), 1)
+        here, there = at_y(both_cores[0], both_cores[1])
+        all_units = jnp.stack(by_y(here, swap_y(there)))
+        return all_units.transpose(2, 0, 1, 3).reshape(rows, 4 * units)
+
+    gate_all = own_rows(ffn_part[..., :units])
+    up_all = own_rows(ffn_part[..., units:])
+    indices = jnp.stack(
+        [jnp.stack([ring.chunk_at(step) for ring in (right, left)]) for step in range(copies)]
+    )
+    down_part = after(down_part, rows_there)
+    (w_down_grad,) = gather_over_rings(
+        (right, left),
+        indices,
+        [down_part[:, :half], down_part[:, half:]],
+        [(hidden_units, width)],
+        [(0, 0, 0, half, 0), (0, 1, 0, half, half)],
+    )
+
+    query_width = 2 * span
+    head_sum = jnp.concatenate([attn_grad_y.reshape(2, span, -1), mix_grad_y[None]])
+    head_sum = head_sum.reshape(3, copies, rows, width)
+
+    def pick_half(start):
+        def pick(index):
+            return lax.dynamic_index_in_dim(
+                head_sum[..., start : start + half], index, 1, keepdims=False
+            )
+
+        return pick
+
+    head_right = sum_over_ring(right, pick_half(0))
+    head_left = sum_over_ring(left, pick_half(half))
+
+    def all_heads(part, kinds):
+        mine, other = at_core(part[0], part[1])
+        even, odd = by_core(mine, swap_core(other))
+        shape = (rows, kinds, 2, 1, part.shape[-1] // (2 * kinds))
+        return jnp.concatenate([even.reshape(shape), odd.reshape(shape)], 3).reshape(rows, -1)
+
+    query_all = all_heads(head_right[:2], 1)
+    rest_all = all_heads(head_left[:2], 2)
+    chunk_right = jnp.concatenate([gate_all, query_all, head_right[2]], 1)
+    chunk_left = jnp.concatenate([up_all, rest_all, head_left[2]], 1)
+    full = 4 * span
+    gate_end = 4 * units
+    heads_end = gate_end + full
+    w_gate_grad, w_up_grad, w_query_grad, w_key_grad, w_value_grad, w_out_grad = gather_over_rings(
+        (right, left),
+        indices,
+        [chunk_right, chunk_left],
+        [(span, value.shape[1]) for value in (w_gate, w_up, w_query, w_key, w_value, w_out)],
+        [
+            (0, 0, 0, gate_end, 0),
+            (1, 1, 0, gate_end, 0),
+            (2, 0, gate_end, heads_end, 0),
+            (3, 1, gate_end, gate_end + full // 2, 0),
+            (4, 1, gate_end + full // 2, heads_end, 0),
+            (5, 0, heads_end, heads_end + half, 0),
+            (5, 1, heads_end, heads_end + half, half),
+        ],
+    )
+
     sums = jnp.concatenate([attn_gain_part, ffn_gain_part, head_gain_part.T.reshape(-1)])
-    sums = sums.reshape(-1, 128)
+    sums = after(sums.reshape(-1, 128), head_right)
     sums = sums + swap_core(sums)
     sums = sums + swap_y(sums)
     step = 1
@@ -561,54 +716,10 @@
     query_gain_grad = sums[2 * width : 2 * width + HD]
     key_gain_grad = sums[2 * width + HD : 2 * width + 2 * HD]
 
-    right, left = Ring(1), Ring(-1)
-    half = width // 2
-    down_rows = hidden_units // copies
-    down_view = down_grad.reshape(copies, down_rows, width)
-    down_right = right.reduce(pick_rows(down_view[:, :, :half], 0))
-    down_left = left.reduce(pick_rows(down_view[:, :, half:], 0))
-    w_down_grad = jnp.concatenate(
-        [gather_rows(right, down_right, copies), gather_rows(left, down_left, copies)], 1
-    )
-
-    rows = span // copies
-    ffn_view = ffn_grad.reshape(4, copies, rows, 2 * units)
-    gate_part = right.reduce(pick_rows(ffn_view[..., :units], 1))
-    up_part = left.reduce(pick_rows(ffn_view[..., units:], 1))
-
-    def own_rows(part):
-        parts = part.reshape(2, 2, rows, units)
-        mine, other = at_core(parts[:, 0], parts[:, 1])
-        both_cores = jnp.stack(by_core(mine, swap_core(other)), 1)
-        here, there = at_y(both_cores[0], both_cores[1])
-        all_units = jnp.stack(by_y(here, swap_y(there)))
-        return all_units.transpose(2, 0, 1, 3).reshape(rows, 4 * units)
-
-    w_gate_grad = gather_rows(right, own_rows(gate_part), copies)
-    w_up_grad = gather_rows(left, own_rows(up_part), copies)
-
-    query_width = 2 * span
-    attn_view = attn_grad_y.reshape(2, copies, rows, -1)
-    query_part = right.reduce(pick_rows(attn_view[..., :query_width], 1))
-    rest_part = left.reduce(pick_rows(attn_view[..., query_width:], 1))
-    mix_view = mix_grad_y.reshape(copies, rows, width)
-    mix_right = right.reduce(pick_rows(mix_view[..., :half], 0))
-    mix_left = left.reduce(pick_rows(mix_view[..., half:], 0))
-
-    def all_heads(part, kinds):
-        mine, other = at_core(part[0], part[1])
-        even, odd = by_core(mine, swap_core(other))
-        shape = (rows, kinds, 2, 1, part.shape[-1] // (2 * kinds))
-        return jnp.concatenate([even.reshape(shape), odd.reshape(shape)], 3).reshape(rows, -1)
-
-    query_all = gather_rows(right, all_heads(query_part, 1), copies)
-    rest_all = gather_rows(left, all_heads(rest_part, 2), copies)
-    w_out_grad = jnp.concatenate(
-        [gather_rows(right, mix_right, copies), gather_rows(left, mix_left, copies)], 1
-    )
-    w_query_grad = query_all
-    w_key_grad = rest_all[:, : 2 * span]
-    w_value_grad = rest_all[:, 2 * span :]
+    out_back, input_back = after((out_back, input_back), head_right)
+    out_back, input_back = out_back.astype(F32), input_back.astype(F32)
+    input_grad = jnp.stack(by_y(input_here, input_back))
+    block_out = jnp.stack(by_y(own_here + out_back[1], next_here + out_back[0])).astype(BF)
 
     return (
         block_out,

time: 815 us -> 563 us (0.69)
  waiting for transfers between devices: 314 us -> 180 us
  starting transfers between devices: 149 us -> 84.4 us
  between operations: 66.1 us -> 16.3 us
  Pallas kernels: 53.4 us -> 83.9 us
  local copies, waits for them, and re-layouts: 46.3 us -> 24.7 us
  other arithmetic: 86.7 us -> 71.4 us
    ppermute x112 -> x42, waiting for transfers between devices: 224 us -> 44.7 us  [send(): return lax.ppermute(value, 'replica', self.hops)]
    ppermute x112 -> x42, starting transfers between devices: 127 us -> 47 us  [send(): return lax.ppermute(value, 'replica', self.hops)]
    ppermute x15 -> x16, waiting for transfers between devices: 79.7 us -> 118 us  [swap_y(): return lax.ppermute(value, 'group', Y_SWAP)]
    pallas_call x0 -> x16, Pallas kernels: none -> 29.3 us  [place_chunks(): pl.pallas_call(functools.partial(place_kernel, step, targets, rows), out_...]
    dynamic_update_slice x64 -> x0, other arithmetic: 18.3 us -> none  [place(): lax.dynamic_update_slice(store[0], value.astype(F32), (index * rows, 0))]
    unnamed x194 -> x191, local copies, waits for them, and re-layouts: 23.1 us -> 11.6 us
    ppermute x0 -> x4, waiting for transfers between devices: none -> 11.2 us  [the longest x1 10.6 us: per_device(): other_y = lax.ppermute(kind_y, 'replica', by_replica)]
    ppermute x15 -> x16, starting transfers between devices: 18.2 us -> 23.6 us  [swap_y(): return lax.ppermute(value, 'group', Y_SWAP)]
  transfers between devices with their start and end apart: 150 -> 87, of which waited for: 83 -> 41; matrix products, arithmetic and copies ran while one was open for 22% -> 27% of each run, Pallas kernels for 7% -> 15%
where the time goes in v2:
time: 563 us; the launch traced here: 554 us
  waiting for transfers between devices  180 us (32%)
  matrix products  94 us (17%)
  starting transfers between devices  84.4 us (15%)
  Pallas kernels  83.9 us (15%)
  other arithmetic  71.4 us (13%)
  local copies, waits for them, and re-layouts  24.7 us (4%)
  between operations  16.3 us (3%)
    ppermute x16, waiting for transfers between devices, swap_y(): return lax.ppermute(value, 'group', Y_SWAP)  118 us
    dot_general x16, matrix products, contract(): lax.dot_general(left, right, (((left_dim,), (right_dim,)), ((), ())), pre...  92.8 us
    ppermute x42, starting transfers between devices, send(): return lax.ppermute(value, 'replica', self.hops)  47 us
    ppermute x42, waiting for transfers between devices, send(): return lax.ppermute(value, 'replica', self.hops)  44.7 us
    pallas_call x16, Pallas kernels, place_chunks(): pl.pallas_call(functools.partial(place_kernel, step, targets, rows), out_...  29.3 us
    pallas_call x1, Pallas kernels, attention_backward(): pl.pallas_call(backward_kernel, out_shape=[jax.ShapeDtypeStruct((length,...  27.7 us
    pallas_call x1, Pallas kernels, attention_forward(): pl.pallas_call(forward_kernel, out_shape=[jax.ShapeDtypeStruct(shape, kin...  26.9 us
    ppermute x16, starting transfers between devices, swap_y(): return lax.ppermute(value, 'group', Y_SWAP)  23.6 us
  transfers between devices with their start and end apart: 87, of which 41 were waited for; matrix products, arithmetic and copies ran while one was open for 27% of the time, Pallas kernels for 15%

profile of v2, /device:TPU:0, one launch (start us, length us, event | category | flops | bytes accessed | tf_op | source)
XLA Modules:
  0.0 554.4 jit_solution(11104192746132443276)
XLA Ops:
  9.5 3.0 collective-permute-start
  22.3 13.7 %collective-permute-done.2 = f32[6,256]{1,0:T(8,128)S(1)} collective-permute-done((f32[6,256]{1,0:T(8,128)S(1)}, f32[6,256]{1,0:T(8,128)S(1)}, u32[]{:S(2)}, u32[]{:S(2)}) %collective-permute-start.2) | collective-permute-done | bytes 6176 | tf_op jit(solution)/shard_map/ppermute | solution.py:287
  51.2 4.3 collective-permute-done.5
  61.1 5.6 %collective-permute-done.7 = bf16[256,1024]{1,0:T(8,128)(2,1)S(1)} collective-permute-done((bf16[256,1024]{1,0:T(8,128)(2,1)S(1)}, bf16[256,1024]{1,0:T(8,128)(2,1)S(1)}, u32[]{:S(2)}, u32[]{:S(2)}) %collective-permute-start.7) | collective-permute-done | bytes 524320 | tf_op jit(solution)/shard_map/ppermute | solution.py:287
  71.2 26.9 %attention_forward.1 = (bf16[1024,512]{1,0:T(8,128)(2,1)S(1)}, bf16[768,1024]{1,0:T(8,128)(2,1)S(1)}, bf16[4,1024,64]{2,1,0:T(8,128)(2,1)S(1)}, bf16[1024,256]{1...) custom-call(bf16[1024,1024]{1,0:T(8,128)(2,1)} %fusion.1.hidden_ref,, ...), custom_call_target="tpu_custom_call" | custom-call | flops 12000000000 | bytes 16777216 | tf_op jit(solution)/shard_map/attention_forward/pallas_call | solution.py:236
  100.0 2.4 collective-permute-start.8
  108.6 9.3 %collective-permute-done.17 = bf16[256,1024]{1,0:T(8,128)(2,1)S(1)} collective-permute-done((bf16[256,1024]{1,0:T(8,128)(2,1)S(1)}, bf16[256,1024]{1,0:T(8,128)(2,1)S(1)}, u32[]{:S(2)}, u32[]{:S(2)}) %collective-permute-start.17) | collective-permute-done | bytes 524320 | tf_op jit(solution)/shard_map/ppermute | solution.py:287
  120.0 10.6 %collective-permute-done.13 = bf16[256,1152]{1,0:T(8,128)(2,1)S(1)} collective-permute-done((bf16[256,1152]{1,0:T(8,128)(2,1)}, bf16[256,1152]{1,0:T(8,128)(2,1)S(1)}, u32[]{:S(2)}, u32[]{:S(2)}) %collective-permute-start.13) | collective-permute-done | bytes 589856 | tf_op jit(solution)/shard_map/ppermute | solution.py:513
  136.2 33.4 %collective-permute-done.18 = bf16[256,1024]{1,0:T(8,128)(2,1)S(1)} collective-permute-done((bf16[256,1024]{1,0:T(8,128)(2,1)S(1)}, bf16[256,1024]{1,0:T(8,128)(2,1)S(1)}, u32[]{:S(2)}, u32[]{:S(2)}) %collective-permute-start.18) | collective-permute-done | bytes 524320 | tf_op jit(solution)/shard_map/ppermute | solution.py:287
  170.3 8.2 %fusion.16 = f32[1024,2304]{1,0:T(8,128)} fusion(bf16[512,1024]{1,0:T(8,128)(2,1)S(1)} %collective-permute-done.9, bf16[512,1024]{1,0:T(8,128)(2,1)S(1)} %multiply_convert_fusion.6, bf16[512,2304]{1,0:T(8,128)(2,1)S(1)} %get-tuple-element.189, bf16[512,2304]{1,0:T(8,128)(2,1)S(1)} %get-tuple-element.188), kind=kOutput, calls=%fused_computation.76 | convolution fusion | flops 4845469696 | bytes 16252928 | tf_op jit(solution)/shard_map/dot_general | solution.py:29
  178.5 9.9 %multiply_convert_fusion.1 = (bf16[1024,1152]{1,0:T(8,128)(2,1)S(1)}, bf16[1024,1152]{1,0:T(8,128)(2,1)}, bf16[1024,1152]{1,0:T(8,128)(2,1)}) fusion(f32[1024,2304]{1,0:T(8,128)} %fusion.16, bf16[1152,1024]{1,0:T(8,128)(2,1)S(1)} %copy-done, bf16[512,1024]{1,0:T(8,128)(2,1)} %collective-permute-done.20, bf16[256,1024]{1,0:T(8,128)(2,1)S(1)} %broadcast_select_fusion.31, ...), kind=kOutput, calls=%fused_computation.5 | convolution fusion | flops 2441084928 | bytes 20971520 | tf_op jit(solution)/shard_map/dot_general | solution.py:29
  188.5 10.1 %fusion.2 = f32[1024,2304]{1,0:T(8,128)} fusion(bf16[1024,1152]{1,0:T(8,128)(2,1)} %get-tuple-element.181, bf16[1024,1152]{1,0:T(8,128)(2,1)S(1)} %get-tuple-element.180, bf16[512,1024]{1,0:T(8,128)(2,1)S(1)} %collective-permute-done.9, bf16[512,1024]{1,0:T(8,128)(2,1)S(1)} %multiply_convert_fusion.6), kind=kOutput, calls=%fused_computation.19 | convolution fusion | flops 4845469696 | bytes 16252928 | tf_op jit(solution)/shard_map/dot_general | solution.py:29
  198.7 7.4 %fusion.94 = f32[1024,2304]{1,0:T(8,128)} fusion(bf16[1024,1024]{1,0:T(8,128)(2,1)S(1)} %constant_dynamic-update-slice_fusion, bf16[512,2304]{1,0:T(8,128)(2,1)S(1)} %get-tuple-element.189, bf16[512,2304]{1,0:T(8,128)(2,1)S(1)} %get-tuple-element.188), kind=kOutput, calls=%fused_computation.315 | convolution fusion | flops 4841275392 | bytes 16252928 | tf_op jit(solution)/shard_map/dot_general | solution.py:29
  206.1 8.4 %multiply_convert_fusion.3 = (bf16[1024,1152]{1,0:T(8,128)(2,1)S(1)}, bf16[1024,1152]{1,0:T(8,128)(2,1)S(1)}, bf16[1024,1152]{1,0:T(8,128)(2,1)S(1)}) fusion(f32[1024,2304]{1,0:T(8,128)} %fusion.94, bf16[1152,1024]{1,0:T(8,128)(2,1)S(1)} %copy-done, bf16[512,1024]{1,0:T(8,128)(2,1)S(1)} %collective-permute-done.19, ...), kind=kOutput, calls=%fused_computation.8 | convolution fusion | flops 2441084928 | bytes 20971520 | tf_op jit(solution)/shard_map/dot_general | solution.py:29
  214.6 2.7 pad_maximum_fusion.1
  217.4 2.7 fusion.22
  220.1 5.4 add_convert_fusion.1
  225.6 10.8 %add_convert_fusion = bf16[1024,2304]{1,0:T(8,128)(2,1)} fusion(f32[1024,2304]{1,0:T(8,128)} %fusion.2, bf16[1024,1024]{1,0:T(8,128)(2,1)} %copy-done.66, bf16[1024,2304]{1,0:T(8,128)(2,1)} %pad_maximum_fusion.1), kind=kOutput, calls=%fused_computation | convolution fusion | flops 4836556800 | bytes 20971520 | tf_op jit(solution)/shard_map/dot_general | solution.py:29
  236.5 9.0 %fusion.93 = f32[1024,1024]{1,0:T(8,128)S(1)} fusion(bf16[1024,2304]{1,0:T(8,128)(2,1)} %pad_maximum_fusion.1, bf16[512,2304]{1,0:T(8,128)(2,1)} %copy-done.57, bf16[512,2304]{1,0:T(8,128)(2,1)} %copy-done.55), kind=kOutput, calls=%fused_computation.314 | convolution fusion | flops 4841275392 | bytes 13631488 | tf_op jit(solution)/shard_map/dot_general | solution.py:29
  245.8 5.1 fusion.3
  254.1 23.0 %collective-permute-done.22 = bf16[512,1024]{1,0:T(8,128)(2,1)S(1)} collective-permute-done((bf16[512,1024]{1,0:T(8,128)(2,1)S(1)}, bf16[512,1024]{1,0:T(8,128)(2,1)S(1)}, u32[]{:S(2)}, u32[]{:S(2)}) %collective-permute-start.22) | collective-permute-done | bytes 1048608 | tf_op jit(solution)/shard_map/ppermute | solution.py:287
  277.9 2.4 fusion.96
  290.0 27.7 %attention_backward.1 = (bf16[1024,1024]{1,0:T(8,128)(2,1)}, f32[64,2]{1,0:T(8,128)}) custom-call(bf16[1024,512]{1,0:T(8,128)(2,1)} %convolution_convert_fusion.grad_ref, bf16[768,1024]{1,0:T(8,128)(2,1)} %copy-done.14, bf16[4,1024,64]{2,1,0:T(8,128)(2,1)} %copy-done.15, bf16[1024,256]{1,0:T(8,128)(2,1)} %copy-done.16, ...), custom_call_target="tpu_custom_call" | custom-call | flops 24999999488 | bytes 16777216 | tf_op jit(solution)/shard_map/attention_backward/pallas_call | solution.py:253
  317.7 4.1 fusion.95
  321.9 2.4 fusion.104
  325.1 2.9 fusion.103
  330.3 2.9 fusion.102
  341.1 2.8 slice_select_fusion.1
  343.9 8.4 %collective-permute-done.31 = bf16[256,1024]{1,0:T(8,128)(2,1)} collective-permute-done((bf16[256,1024]{1,0:T(8,128)(2,1)}, bf16[256,1024]{1,0:T(8,128)(2,1)}, u32[]{:S(2)}, u32[]{:S(2)}) %collective-permute-start.31) | collective-permute-done | bytes 524320 | tf_op jit(solution)/shard_map/ppermute | solution.py:287
  358.5 16.3 %collective-permute-done.30 = bf16[512,1024]{1,0:T(8,128)(2,1)} collective-permute-done((bf16[512,1024]{1,0:T(8,128)(2,1)}, bf16[512,1024]{1,0:T(8,128)(2,1)}, u32[]{:S(2)}, u32[]{:S(2)}) %collective-permute-start.30) | collective-permute-done | bytes 1048608 | tf_op jit(solution)/shard_map/ppermute | solution.py:287
  379.4 2.9 collective-permute-done.32
  384.5 2.5 collective-permute-done.33
  389.2 3.3 collective-permute-done.34
  392.6 2.5 collective-permute-start.35
  397.0 2.8 collective-permute-done.35
  399.9 2.7 collective-permute-start.36
  402.6 3.0 collective-permute-done.59
  406.2 2.8 collective-permute-start.37
  411.3 2.5 collective-permute-start.38
  416.1 3.6 collective-permute-done.62
  427.9 3.9 collective-permute-done.45
  439.4 4.7 fusion.13
  446.3 3.4 collective-permute-done.64.refs_1_
  456.4 3.0 collective-permute-done.65.refs_1_
  475.5 2.5 collective-permute-start.43
  478.1 3.5 collective-permute-done.78.refs_1_
  494.4 3.1 collective-permute-done.73.refs_0_
  501.5 2.9 collective-permute-done.74.refs_0_
  (512 shorter events, 200.8 us)
Async XLA Ops:
  7.2 415.3 %reduce-scatter.3.cloned.1.call-start = ((), (), s32[]{:S(2)}) async-start(), calls=%async_computation.2 | async-start | bytes 5308416 | tf_op jit(solution)/shard_map/reduce_scatter | solution.py:634
  9.5 30.2 %collective-permute-start = (bf16[256,1024]{1,0:T(8,128)(2,1)}, bf16[256,1024]{1,0:T(8,128)(2,1)}, u32[]{:S(2)}, u32[]{:S(2)}) collective-permute-start(bf16[256,1024]{1,0:T(8,128)(2,1)} %select_bitcast_fusion.6), channel_id=1, source_target_pairs={{0,2},{2,0},{1,3},{3,1},{4,6},{6,4},{5,7},{7,5},{8,10},{10,8},{9,1... | collective-permute-start | bytes 1572872 | tf_op jit(solution)/shard_map/ppermute | solution.py:287
  19.1 22.5 %collective-permute-start.4 = (bf16[256,1024]{1,0:T(8,128)(2,1)}, bf16[256,1024]{1,0:T(8,128)(2,1)}, u32[]{:S(2)}, u32[]{:S(2)}) collective-permute-start(bf16[256,1024]{1,0:T(8,128)(2,1)} %broadcast_select_fusion.26), channel_id=1, source_target_pairs={{0,1},{1,0},{2,3},{3,2},{4,5},{5,4},{6,7},{7,6},{8,9},{9,8},{10,11... | collective-permute-start | bytes 1572872 | tf_op jit(solution)/shard_map/ppermute | solution.py:295
  19.2 31.9 %collective-permute-start.6 = (bf16[256,1024]{1,0:T(8,128)(2,1)}, bf16[256,1024]{1,0:T(8,128)(2,1)}, u32[]{:S(2)}, u32[]{:S(2)}) collective-permute-start(bf16[256,1024]{1,0:T(8,128)(2,1)} %broadcast_select_fusion.26), channel_id=1, source_target_pairs={{0,3},{3,0},{1,2},{2,1},{4,7},{7,4},{5,6},{6,5},{8,11},{11,8},{9,1... | collective-permute-start | bytes 1572872 | tf_op jit(solution)/shard_map/ppermute | solution.py:291
  19.3 16.7 %collective-permute-start.2 = (f32[6,256]{1,0:T(8,128)S(1)}, f32[6,256]{1,0:T(8,128)S(1)}, u32[]{:S(2)}, u32[]{:S(2)}) collective-permute-start(f32[6,256]{1,0:T(8,128)S(1)} %pad_maximum_fusion.41), channel_id=1, source_target_pairs={{0,2},{2,0},{1,3},{3,1},{4,6},{6,4},{5,7},{7,5},{8,10},{10,8},{9,1... | collective-permute-start | bytes 18440 | tf_op jit(solution)/shard_map/ppermute | solution.py:287
  41.4 26.4 %collective-permute-start.1 = (bf16[2,256,1024]{2,1,0:T(8,128)(2,1)S(1)}, bf16[2,256,1024]{2,1,0:T(8,128)(2,1)S(1)}, u32[]{:S(2)}, u32[]{:S(2)}) collective-permute-start(bf16[2,256,1024]{2,1,0:T(8,128)(2,1)S(1)} %pad_maximum_fusion.19), channel_id=1, source_target_pairs={{0,1},{1,0},{2,3},{3,2},{4,5},{5,4},{6,7},{7,6},{8,9},{9,8},{10,11... | collective-permute-start | bytes 3145736 | tf_op jit(solution)/shard_map/ppermute | solution.py:295
  41.7 13.8 %collective-permute-start.5 = (bf16[256,1024]{1,0:T(8,128)(2,1)S(1)}, bf16[256,1024]{1,0:T(8,128)(2,1)S(1)}, u32[]{:S(2)}, u32[]{:S(2)}) collective-permute-start(bf16[256,1024]{1,0:T(8,128)(2,1)S(1)} %get-tuple-element.179), channel_id=1, source_target_pairs={{0,2},{2,0},{1,3},{3,1},{4,6},{6,4},{5,7},{7,5},{8,10},{10,8},{9,1... | collective-permute-start | bytes 1572872 | tf_op jit(solution)/shard_map/ppermute | solution.py:287
  43.5 23.2 %collective-permute-start.7 = (bf16[256,1024]{1,0:T(8,128)(2,1)S(1)}, bf16[256,1024]{1,0:T(8,128)(2,1)S(1)}, u32[]{:S(2)}, u32[]{:S(2)}) collective-permute-start(bf16[256,1024]{1,0:T(8,128)(2,1)S(1)} %copy-done.65), channel_id=1, source_target_pairs={{0,2},{2,0},{1,3},{3,1},{4,6},{6,4},{5,7},{7,5},{8,10},{10,8},{9,1... | collective-permute-start | bytes 1572872 | tf_op jit(solution)/shard_map/ppermute | solution.py:287
  47.3 55.1 %collective-permute-start.11 = (bf16[256,1152]{1,0:T(8,128)(2,1)}, bf16[256,1152]{1,0:T(8,128)(2,1)}, u32[]{:S(2)}, u32[]{:S(2)}) collective-permute-start(bf16[256,1152]{1,0:T(8,128)(2,1)} %broadcast_select_fusion.17), channel_id=1, source_target_pairs={{0,2},{2,0},{1,3},{3,1},{4,6},{6,4},{5,7},{7,5},{8,10},{10,8},{9,1... | collective-permute-start | bytes 1769480 | tf_op jit(solution)/shard_map/ppermute | solution.py:287
  51.1 51.4 %collective-permute-start.12 = (bf16[256,1152]{1,0:T(8,128)(2,1)}, bf16[256,1152]{1,0:T(8,128)(2,1)}, u32[]{:S(2)}, u32[]{:S(2)}) collective-permute-start(bf16[256,1152]{1,0:T(8,128)(2,1)} %get-tuple-element.196), channel_id=1, source_target_pairs={{0,3},{3,0},{1,2},{2,1},{4,7},{7,4},{5,6},{6,5},{8,11},{11,8},{9,1... | collective-permute-start | bytes 1769480 | tf_op jit(solution)/shard_map/ppermute | solution.py:291
  55.5 51.3 %collective-permute-start.10 = (bf16[256,2304]{1,0:T(8,128)(2,1)}, bf16[256,2304]{1,0:T(8,128)(2,1)}, u32[]{:S(2)}, u32[]{:S(2)}) collective-permute-start(bf16[256,2304]{1,0:T(8,128)(2,1)} %pad_maximum_fusion.16), channel_id=1, source_target_pairs={{0,1},{1,0},{2,3},{3,2},{4,5},{5,4},{6,7},{7,6},{8,9},{9,8},{10,11... | collective-permute-start | bytes 3538952 | tf_op jit(solution)/shard_map/ppermute | solution.py:295
  100.0 31.8 %collective-permute-start.8 = (bf16[512,1024]{1,0:T(8,128)(2,1)S(1)}, bf16[512,1024]{1,0:T(8,128)(2,1)S(1)}, u32[]{:S(2)}, u32[]{:S(2)}) collective-permute-start(bf16[512,1024]{1,0:T(8,128)(2,1)S(1)} %bitcast.419), channel_id=1, source_target_pairs={{0,1},{1,0},{2,3},{3,2},{4,5},{5,4},{6,7},{7,6},{8,9},{9,8},{10,11... | collective-permute-start | bytes 3145736 | tf_op jit(solution)/shard_map/ppermute | solution.py:295
  102.5 16.4 %collective-permute-start.14 = (bf16[256,1152]{1,0:T(8,128)(2,1)}, bf16[256,1152]{1,0:T(8,128)(2,1)S(1)}, u32[]{:S(2)}, u32[]{:S(2)}) collective-permute-start(bf16[256,1152]{1,0:T(8,128)(2,1)} %collective-permute-done.12), channel_id=1, source_target_pairs={{0,4},{4,0},{8,12},{12,8},{16,20},{20,16},{24,28},{28,24},{1,5},{5... | collective-permute-start | bytes 1769480 | tf_op jit(solution)/shard_map/ppermute | solution.py:514
  104.2 26.5 %collective-permute-start.13 = (bf16[256,1152]{1,0:T(8,128)(2,1)}, bf16[256,1152]{1,0:T(8,128)(2,1)S(1)}, u32[]{:S(2)}, u32[]{:S(2)}) collective-permute-start(bf16[256,1152]{1,0:T(8,128)(2,1)} %collective-permute-done.11), channel_id=1, source_target_pairs={{0,4},{4,0},{8,12},{12,8},{16,20},{20,16},{24,28},{28,24},{1,5},{5... | collective-permute-start | bytes 1769480 | tf_op jit(solution)/shard_map/ppermute | solution.py:513
  104.5 13.4 %collective-permute-start.17 = (bf16[256,1024]{1,0:T(8,128)(2,1)S(1)}, bf16[256,1024]{1,0:T(8,128)(2,1)S(1)}, u32[]{:S(2)}, u32[]{:S(2)}) collective-permute-start(bf16[256,1024]{1,0:T(8,128)(2,1)S(1)} %copy-done.67), channel_id=1, source_target_pairs={{0,2},{2,0},{1,3},{3,1},{4,6},{6,4},{5,7},{7,5},{8,10},{10,8},{9,1... | collective-permute-start | bytes 1572872 | tf_op jit(solution)/shard_map/ppermute | solution.py:287
  118.2 60.3 %collective-permute-start.20 = (bf16[512,1024]{1,0:T(8,128)(2,1)S(1)}, bf16[512,1024]{1,0:T(8,128)(2,1)}, u32[]{:S(2)}, u32[]{:S(2)}) collective-permute-start(bf16[512,1024]{1,0:T(8,128)(2,1)S(1)} %pad_maximum_fusion.23), channel_id=1, source_target_pairs={{0,1},{1,0},{2,3},{3,2},{4,5},{5,4},{6,7},{7,6},{8,9},{9,8},{10,11... | collective-permute-start | bytes 3145736 | tf_op jit(solution)/shard_map/ppermute | solution.py:295
  132.6 37.6 %collective-permute-start.9 = (bf16[512,1024]{1,0:T(8,128)(2,1)S(1)}, bf16[512,1024]{1,0:T(8,128)(2,1)S(1)}, u32[]{:S(2)}, u32[]{:S(2)}) collective-permute-start(bf16[512,1024]{1,0:T(8,128)(2,1)S(1)} %multiply_convert_fusion.6), channel_id=1, source_target_pairs={{0,1},{1,0},{2,3},{3,2},{4,5},{5,4},{6,7},{7,6},{8,9},{9,8},{10,11... | collective-permute-start | bytes 3145736 | tf_op jit(solution)/shard_map/ppermute | solution.py:295
  132.7 37.1 %collective-permute-start.15 = (bf16[512,1024]{1,0:T(8,128)(2,1)S(1)}, bf16[512,1024]{1,0:T(8,128)(2,1)S(1)}, u32[]{:S(2)}, u32[]{:S(2)}) collective-permute-start(bf16[512,1024]{1,0:T(8,128)(2,1)S(1)} %multiply_convert_fusion.6), channel_id=1, source_target_pairs={{0,2},{2,0},{1,3},{3,1},{4,6},{6,4},{5,7},{7,5},{8,10},{10,8},{9,1... | collective-permute-start | bytes 3145736 | tf_op jit(solution)/shard_map/ppermute | solution.py:287
  134.5 35.0 %collective-permute-start.18 = (bf16[256,1024]{1,0:T(8,128)(2,1)S(1)}, bf16[256,1024]{1,0:T(8,128)(2,1)S(1)}, u32[]{:S(2)}, u32[]{:S(2)}) collective-permute-start(bf16[256,1024]{1,0:T(8,128)(2,1)S(1)} %get-tuple-element.99), channel_id=1, source_target_pairs={{0,2},{2,0},{1,3},{3,1},{4,6},{6,4},{5,7},{7,5},{8,10},{10,8},{9,1... | collective-permute-start | bytes 1572872 | tf_op jit(solution)/shard_map/ppermute | solution.py:287
  169.7 36.4 %collective-permute-start.19 = (bf16[512,1024]{1,0:T(8,128)(2,1)S(1)}, bf16[512,1024]{1,0:T(8,128)(2,1)S(1)}, u32[]{:S(2)}, u32[]{:S(2)}) collective-permute-start(bf16[512,1024]{1,0:T(8,128)(2,1)S(1)} %pad_maximum_fusion.24), channel_id=1, source_target_pairs={{0,1},{1,0},{2,3},{3,2},{4,5},{5,4},{6,7},{7,6},{8,9},{9,8},{10,11... | collective-permute-start | bytes 3145736 | tf_op jit(solution)/shard_map/ppermute | solution.py:295
  169.8 28.8 %collective-permute-start.16 = (bf16[512,1024]{1,0:T(8,128)(2,1)S(1)}, bf16[512,1024]{1,0:T(8,128)(2,1)S(1)}, u32[]{:S(2)}, u32[]{:S(2)}) collective-permute-start(bf16[512,1024]{1,0:T(8,128)(2,1)S(1)} %collective-permute-done.15), channel_id=1, source_target_pairs={{0,1},{1,0},{2,3},{3,2},{4,5},{5,4},{6,7},{7,6},{8,9},{9,8},{10,11... | collective-permute-start | bytes 3145736 | tf_op jit(solution)/shard_map/ppermute | solution.py:295
  236.4 224.2 %reduce-scatter.5.cloned.1.call-start = ((), (), s32[]{:S(2)}) async-start(), calls=%async_computation.3 | async-start | bytes 2654208 | tf_op jit(solution)/shard_map/reduce_scatter | solution.py:634
  251.9 25.2 %collective-permute-start.22 = (bf16[512,1024]{1,0:T(8,128)(2,1)S(1)}, bf16[512,1024]{1,0:T(8,128)(2,1)S(1)}, u32[]{:S(2)}, u32[]{:S(2)}) collective-permute-start(bf16[512,1024]{1,0:T(8,128)(2,1)S(1)} %fusion.14), channel_id=1, source_target_pairs={{0,2},{2,0},{1,3},{3,1},{4,6},{6,4},{5,7},{7,5},{8,10},{10,8},{9,1... | collective-permute-start | bytes 3145736 | tf_op jit(solution)/shard_map/ppermute | solution.py:287
  330.3 119.7 %collective-permute-start.26 = (bf16[512,1024]{1,0:T(8,128)(2,1)}, bf16[512,1024]{1,0:T(8,128)(2,1)}, u32[]{:S(2)}, u32[]{:S(2)}) collective-permute-start(bf16[512,1024]{1,0:T(8,128)(2,1)} %slice.707), channel_id=1, source_target_pairs={{0,1},{1,0},{2,3},{3,2},{4,5},{5,4},{6,7},{7,6},{8,9},{9,8},{10,11... | collective-permute-start | bytes 3145736 | tf_op jit(solution)/shard_map/ppermute | solution.py:295
  334.5 104.9 %collective-permute-start.25 = (bf16[512,1024]{1,0:T(8,128)(2,1)}, bf16[512,1024]{1,0:T(8,128)(2,1)}, u32[]{:S(2)}, u32[]{:S(2)}) collective-permute-start(bf16[512,1024]{1,0:T(8,128)(2,1)} %slice.708), channel_id=1, source_target_pairs={{0,1},{1,0},{2,3},{3,2},{4,5},{5,4},{6,7},{7,6},{8,9},{9,8},{10,11... | collective-permute-start | bytes 3145736 | tf_op jit(solution)/shard_map/ppermute | solution.py:295
  336.1 17.5 %collective-permute-start.28 = (bf16[512,1024]{1,0:T(8,128)(2,1)}, bf16[512,1024]{1,0:T(8,128)(2,1)S(1)}, u32[]{:S(2)}, u32[]{:S(2)}) collective-permute-start(bf16[512,1024]{1,0:T(8,128)(2,1)} %bitcast.31), channel_id=1, source_target_pairs={{0,1},{1,0},{2,3},{3,2},{4,5},{5,4},{6,7},{7,6},{8,9},{9,8},{10,11... | collective-permute-start | bytes 3145736 | tf_op jit(solution)/shard_map/ppermute | solution.py:295
  337.2 15.1 %collective-permute-start.31 = (bf16[256,1024]{1,0:T(8,128)(2,1)}, bf16[256,1024]{1,0:T(8,128)(2,1)}, u32[]{:S(2)}, u32[]{:S(2)}) collective-permute-start(bf16[256,1024]{1,0:T(8,128)(2,1)} %select_convert_fusion.4), channel_id=1, source_target_pairs={{0,2},{2,0},{1,3},{3,1},{4,6},{6,4},{5,7},{7,5},{8,10},{10,8},{9,1... | collective-permute-start | bytes 1572872 | tf_op jit(solution)/shard_map/ppermute | solution.py:287
  340.1 34.6 %collective-permute-start.30 = (bf16[512,1024]{1,0:T(8,128)(2,1)}, bf16[512,1024]{1,0:T(8,128)(2,1)}, u32[]{:S(2)}, u32[]{:S(2)}) collective-permute-start(bf16[512,1024]{1,0:T(8,128)(2,1)} %slice_select_fusion), channel_id=1, source_target_pairs={{0,2},{2,0},{1,3},{3,1},{4,6},{6,4},{5,7},{7,5},{8,10},{10,8},{9,1... | collective-permute-start | bytes 3145736 | tf_op jit(solution)/shard_map/ppermute | solution.py:287
  356.8 117.1 %collective-permute-start.29 = (bf16[256,1024]{1,0:T(8,128)(2,1)}, bf16[256,1024]{1,0:T(8,128)(2,1)}, u32[]{:S(2)}, u32[]{:S(2)}) collective-permute-start(bf16[256,1024]{1,0:T(8,128)(2,1)} %select_convert_fusion.5), channel_id=1, source_target_pairs={{0,2},{2,0},{1,3},{3,1},{4,6},{6,4},{5,7},{7,5},{8,10},{10,8},{9,1... | collective-permute-start | bytes 1572872 | tf_op jit(solution)/shard_map/ppermute | solution.py:287
  432.4 11.7 %collective-permute-start.47 = (bf16[32,6144]{1,0:T(8,128)(2,1)S(1)}, bf16[32,6144]{1,0:T(8,128)(2,1)S(1)}, u32[]{:S(2)}, u32[]{:S(2)}) collective-permute-start(bf16[32,6144]{1,0:T(8,128)(2,1)S(1)} %pad_maximum_fusion.33.refs_0_), channel_id=1, source_target_pairs={{0,8},{8,16},{16,24},{24,28},{28,20},{20,12},{12,4},{4,0},{1,9},{9... | collective-permute-start | bytes 1179656 | tf_op jit(solution)/shard_map/ppermute | solution.py:321
  439.2 10.4 %collective-permute-start.64 = (bf16[32,6144]{1,0:T(8,128)(2,1)S(1)}, bf16[32,6144]{1,0:T(8,128)(2,1)S(1)}, u32[]{:S(2)}, u32[]{:S(2)}) collective-permute-start(bf16[32,6144]{1,0:T(8,128)(2,1)S(1)} %pad_maximum_fusion.34.refs_1_), channel_id=1, source_target_pairs={{4,12},{12,20},{20,28},{28,24},{24,16},{16,8},{8,0},{0,4},{5,13},{... | collective-permute-start | bytes 1179656 | tf_op jit(solution)/shard_map/ppermute | solution.py:321
  444.2 10.3 %collective-permute-start.48 = (bf16[32,6144]{1,0:T(8,128)(2,1)S(1)}, bf16[32,6144]{1,0:T(8,128)(2,1)}, u32[]{:S(2)}, u32[]{:S(2)}) collective-permute-start(bf16[32,6144]{1,0:T(8,128)(2,1)S(1)} %collective-permute-done.47.refs_0_), channel_id=1, source_target_pairs={{0,8},{8,16},{16,24},{24,28},{28,20},{20,12},{12,4},{4,0},{1,9},{9... | collective-permute-start | bytes 1179656 | tf_op jit(solution)/shard_map/ppermute | solution.py:321
  449.6 9.7 %collective-permute-start.65 = (bf16[32,6144]{1,0:T(8,128)(2,1)S(1)}, bf16[32,6144]{1,0:T(8,128)(2,1)}, u32[]{:S(2)}, u32[]{:S(2)}) collective-permute-start(bf16[32,6144]{1,0:T(8,128)(2,1)S(1)} %collective-permute-done.64.refs_1_), channel_id=1, source_target_pairs={{4,12},{12,20},{20,28},{28,24},{24,16},{16,8},{8,0},{0,4},{5,13},{... | collective-permute-start | bytes 1179656 | tf_op jit(solution)/shard_map/ppermute | solution.py:321
  451.6 9.0 %collective-permute-start.40 = (f32[17,128]{1,0:T(8,128)S(1)}, f32[17,128]{1,0:T(8,128)}, u32[]{:S(2)}, u32[]{:S(2)}) collective-permute-start(f32[17,128]{1,0:T(8,128)S(1)} %add.447), channel_id=1, source_target_pairs={{0,2},{2,0},{1,3},{3,1},{4,6},{6,4},{5,7},{7,5},{8,10},{10,8},{9,1... | collective-permute-start | bytes 26120 | tf_op jit(solution)/shard_map/ppermute | solution.py:287
  454.5 12.7 %collective-permute-start.49 = (bf16[32,6144]{1,0:T(8,128)(2,1)}, bf16[32,6144]{1,0:T(8,128)(2,1)}, u32[]{:S(2)}, u32[]{:S(2)}) collective-permute-start(bf16[32,6144]{1,0:T(8,128)(2,1)} %collective-permute-done.48.refs_0_), channel_id=1, source_target_pairs={{0,8},{8,16},{16,24},{24,28},{28,20},{20,12},{12,4},{4,0},{1,9},{9... | collective-permute-start | bytes 1179656 | tf_op jit(solution)/shard_map/ppermute | solution.py:321
  459.4 9.5 %collective-permute-start.66 = (bf16[32,6144]{1,0:T(8,128)(2,1)}, bf16[32,6144]{1,0:T(8,128)(2,1)}, u32[]{:S(2)}, u32[]{:S(2)}) collective-permute-start(bf16[32,6144]{1,0:T(8,128)(2,1)} %collective-permute-done.65.refs_1_), channel_id=1, source_target_pairs={{4,12},{12,20},{20,28},{28,24},{24,16},{16,8},{8,0},{0,4},{5,13},{... | collective-permute-start | bytes 1179656 | tf_op jit(solution)/shard_map/ppermute | solution.py:321
  462.7 12.9 %collective-permute-start.71 = (bf16[144,512]{1,0:T(8,128)(2,1)S(1)}, bf16[144,512]{1,0:T(8,128)(2,1)S(1)}, u32[]{:S(2)}, u32[]{:S(2)}) collective-permute-start(bf16[144,512]{1,0:T(8,128)(2,1)S(1)} %get-tuple-element.236.refs_0_), channel_id=1, source_target_pairs={{0,8},{8,16},{16,24},{24,28},{28,20},{20,12},{12,4},{4,0},{1,9},{9... | collective-permute-start | bytes 442376 | tf_op jit(solution)/shard_map/ppermute | solution.py:321
  467.2 17.8 %collective-permute-start.50 = (bf16[32,6144]{1,0:T(8,128)(2,1)}, bf16[32,6144]{1,0:T(8,128)(2,1)}, u32[]{:S(2)}, u32[]{:S(2)}) collective-permute-start(bf16[32,6144]{1,0:T(8,128)(2,1)} %collective-permute-done.49.refs_0_), channel_id=1, source_target_pairs={{0,8},{8,16},{16,24},{24,28},{28,20},{20,12},{12,4},{4,0},{1,9},{9... | collective-permute-start | bytes 1179656 | tf_op jit(solution)/shard_map/ppermute | solution.py:321
  468.8 18.1 %collective-permute-start.67 = (bf16[32,6144]{1,0:T(8,128)(2,1)}, bf16[32,6144]{1,0:T(8,128)(2,1)}, u32[]{:S(2)}, u32[]{:S(2)}) collective-permute-start(bf16[32,6144]{1,0:T(8,128)(2,1)} %collective-permute-done.66.refs_1_), channel_id=1, source_target_pairs={{4,12},{12,20},{20,28},{28,24},{24,16},{16,8},{8,0},{0,4},{5,13},{... | collective-permute-start | bytes 1179656 | tf_op jit(solution)/shard_map/ppermute | solution.py:321
  470.9 10.8 %collective-permute-start.78 = (bf16[144,512]{1,0:T(8,128)(2,1)S(1)}, bf16[144,512]{1,0:T(8,128)(2,1)S(1)}, u32[]{:S(2)}, u32[]{:S(2)}) collective-permute-start(bf16[144,512]{1,0:T(8,128)(2,1)S(1)} %get-tuple-element.235.refs_1_), channel_id=1, source_target_pairs={{4,12},{12,20},{20,28},{28,24},{24,16},{16,8},{8,0},{0,4},{5,13},{... | collective-permute-start | bytes 442376 | tf_op jit(solution)/shard_map/ppermute | solution.py:321
  473.9 37.7 %collective-permute-start.27 = (bf16[2,256,1024]{2,1,0:T(8,128)(2,1)}, bf16[2,256,1024]{2,1,0:T(8,128)(2,1)}, u32[]{:S(2)}, u32[]{:S(2)}) collective-permute-start(bf16[2,256,1024]{2,1,0:T(8,128)(2,1)} %pad_maximum_fusion.25), channel_id=1, source_target_pairs={{0,2},{2,0},{1,3},{3,1},{4,6},{6,4},{5,7},{7,5},{8,10},{10,8},{9,1... | collective-permute-start | bytes 3145736 | tf_op jit(solution)/shard_map/ppermute | solution.py:287
  485.0 14.5 %collective-permute-start.51 = (bf16[32,6144]{1,0:T(8,128)(2,1)}, bf16[32,6144]{1,0:T(8,128)(2,1)}, u32[]{:S(2)}, u32[]{:S(2)}) collective-permute-start(bf16[32,6144]{1,0:T(8,128)(2,1)} %collective-permute-done.50.refs_0_), channel_id=1, source_target_pairs={{0,8},{8,16},{16,24},{24,28},{28,20},{20,12},{12,4},{4,0},{1,9},{9... | collective-permute-start | bytes 1179656 | tf_op jit(solution)/shard_map/ppermute | solution.py:321
  487.0 14.5 %collective-permute-start.68 = (bf16[32,6144]{1,0:T(8,128)(2,1)}, bf16[32,6144]{1,0:T(8,128)(2,1)}, u32[]{:S(2)}, u32[]{:S(2)}) collective-permute-start(bf16[32,6144]{1,0:T(8,128)(2,1)} %collective-permute-done.67.refs_1_), channel_id=1, source_target_pairs={{4,12},{12,20},{20,28},{28,24},{24,16},{16,8},{8,0},{0,4},{5,13},{... | collective-permute-start | bytes 1179656 | tf_op jit(solution)/shard_map/ppermute | solution.py:321
  499.5 15.8 %collective-permute-start.52 = (bf16[32,6144]{1,0:T(8,128)(2,1)}, bf16[32,6144]{1,0:T(8,128)(2,1)S(1)}, u32[]{:S(2)}, u32[]{:S(2)}) collective-permute-start(bf16[32,6144]{1,0:T(8,128)(2,1)} %collective-permute-done.51.refs_0_), channel_id=1, source_target_pairs={{0,8},{8,16},{16,24},{24,28},{28,20},{20,12},{12,4},{4,0},{1,9},{9... | collective-permute-start | bytes 1179656 | tf_op jit(solution)/shard_map/ppermute | solution.py:321
  501.4 15.8 %collective-permute-start.69 = (bf16[32,6144]{1,0:T(8,128)(2,1)}, bf16[32,6144]{1,0:T(8,128)(2,1)S(1)}, u32[]{:S(2)}, u32[]{:S(2)}) collective-permute-start(bf16[32,6144]{1,0:T(8,128)(2,1)} %collective-permute-done.68.refs_1_), channel_id=1, source_target_pairs={{4,12},{12,20},{20,28},{28,24},{24,16},{16,8},{8,0},{0,4},{5,13},{... | collective-permute-start | bytes 1179656 | tf_op jit(solution)/shard_map/ppermute | solution.py:321
  515.3 30.1 %collective-permute-start.53 = (bf16[32,6144]{1,0:T(8,128)(2,1)S(1)}, bf16[32,6144]{1,0:T(8,128)(2,1)S(1)}, u32[]{:S(2)}, u32[]{:S(2)}) collective-permute-start(bf16[32,6144]{1,0:T(8,128)(2,1)S(1)} %collective-permute-done.52.refs_0_), channel_id=1, source_target_pairs={{0,8},{8,16},{16,24},{24,28},{28,20},{20,12},{12,4},{4,0},{1,9},{9... | collective-permute-start | bytes 1179656 | tf_op jit(solution)/shard_map/ppermute | solution.py:321
  517.2 28.2 %collective-permute-start.70 = (bf16[32,6144]{1,0:T(8,128)(2,1)S(1)}, bf16[32,6144]{1,0:T(8,128)(2,1)S(1)}, u32[]{:S(2)}, u32[]{:S(2)}) collective-permute-start(bf16[32,6144]{1,0:T(8,128)(2,1)S(1)} %collective-permute-done.69.refs_1_), channel_id=1, source_target_pairs={{4,12},{12,20},{20,28},{28,24},{24,16},{16,8},{8,0},{0,4},{5,13},{... | collective-permute-start | bytes 1179656 | tf_op jit(solution)/shard_map/ppermute | solution.py:321
  520.0 8.9 %collective-permute-start.77 = (bf16[144,512]{1,0:T(8,128)(2,1)S(1)}, bf16[144,512]{1,0:T(8,128)(2,1)S(1)}, u32[]{:S(2)}, u32[]{:S(2)}) collective-permute-start(bf16[144,512]{1,0:T(8,128)(2,1)S(1)} %collective-permute-done.76.refs_0_), channel_id=1, source_target_pairs={{0,8},{8,16},{16,24},{24,28},{28,20},{20,12},{12,4},{4,0},{1,9},{9... | collective-permute-start | bytes 442376 | tf_op jit(solution)/shard_map/ppermute | solution.py:321
  (128 other events, 1688.7 us)
Sparse Core Ops, SparseCore 0:
  236.5 96.7 reduce-scatter.2
  336.8 72.1 reduce-scatter.4

commit v3 on v2

v3 whole, which is shorter than its diff:
```python
import functools

import jax
import jax.numpy as jnp
from jax import lax
from jax.experimental import pallas as pl
from jax.experimental.pallas import tpu as pltpu
from jax.sharding import PartitionSpec as P

HEADS = 8
PAIRS = 4
HD = 64
HALF = 32
SPAN = 256
LANES = 128

EPS = 1e-05
THETA = 1000000.0
NEG = -1e30

BF = jnp.bfloat16
F32 = jnp.float32
NO_COST = pl.CostEstimate(flops=0, bytes_accessed=0, transcendentals=0)

Y_SWAP = [(0, 2), (2, 0), (1, 3), (3, 1)]
CORE_SWAP = [(0, 1), (1, 0), (2, 3), (3, 2)]
CROSS_SWAP = [(0, 3), (3, 0), (1, 2), (2, 1)]


def contract(left, right, left_dim, right_dim):
    return lax.dot_general(
        left, right, (((left_dim,), (right_dim,)), ((), ())), preferred_element_type=F32
    )


def visible_block(seg_col, seg_row, block):
    end = (block + 1) * SPAN
    key_at = lax.broadcasted_iota(jnp.int32, (end, SPAN), 0)
    query_at = lax.broadcasted_iota(jnp.int32, (end, SPAN), 1) + block * SPAN
    return (seg_col[0:end, :] == seg_row[:, block * SPAN : end]) & (key_at <= query_at)


def project_kernel(
    hidden_ref,
    weight_ref,
    cos_ref,
    sin_ref,
    gain_ref,
    rot_ref,
    key_ref,
    value_ref,
    value_t_ref,
    normed_ref,
    inv_ref,
):
    blocks = hidden_ref.shape[0] // SPAN
    heads = HEADS + PAIRS
    for block in range(blocks):
        span = slice(block * SPAN, (block + 1) * SPAN)
        raw = jnp.dot(hidden_ref[span, :], weight_ref[...], preferred_element_type=F32)
        raw_t = raw.T
        for half in range(2):
            cols = slice(half * 2 * SPAN + 3 * LANES, (half + 1) * 2 * SPAN)
            place = slice(half * LANES, (half + 1) * LANES)
            value_ref[span, place] = raw[:, cols].astype(BF)
            value_t_ref[place, span] = raw_t[cols, :].astype(BF)
        cosine = cos_ref[:, span]
        sine = sin_ref[:, span]
        for head in range(heads):
            rows = slice(head * HD, (head + 1) * HD)
            if head < HEADS:
                at = head // 4 * 2 * SPAN + head % 4 * HD
            else:
                at = (head - HEADS) // 2 * 2 * SPAN + SPAN + head % 2 * HD
            part = raw_t[at : at + HD, :]
            inv = lax.rsqrt(jnp.mean(part * part, 0, keepdims=True) + EPS)
            normed = part * inv
            normed_ref[rows, span] = normed
            inv_ref[head : head + 1, span] = inv
            kind = 0 if head < HEADS else 1
            scaled = normed * gain_ref[:, kind : kind + 1]
            first = scaled[:HALF, :]
            second = scaled[HALF:, :]
            turned = jnp.concatenate(
                [first * cosine - second * sine, second * cosine + first * sine], 0
            )
            if head < HEADS:
                rot_ref[rows, span] = turned.astype(BF) * BF(HD**-0.5)
            else:
                rot_ref[rows, span] = turned.astype(BF)
    for pair in range(PAIRS):
        rows = slice((HEADS + pair) * HD, (HEADS + pair + 1) * HD)
        key_ref[pair] = rot_ref[rows, :].astype(F32).T.astype(BF)


def forward_kernel(
    rot_ref,
    key_ref,
    value_t_ref,
    seg_row_ref,
    seg_col_ref,
    at_ref,
    w_own_ref,
    w_got_ref,
    mixed_ref,
    log_ref,
    w_mix_ref,
    mine_ref,
    other_ref,
):
    w_mix_ref[pl.ds(pl.multiple_of(at_ref[0] * SPAN, SPAN), SPAN), :] = w_own_ref[...]
    w_mix_ref[pl.ds(pl.multiple_of((1 - at_ref[0]) * SPAN, SPAN), SPAN), :] = w_got_ref[...]
    for block in range(mixed_ref.shape[0] // SPAN):
        end = (block + 1) * SPAN
        span = slice(block * SPAN, end)
        visible = visible_block(seg_col_ref[...], seg_row_ref[...], block)

        def one_pair(pair, carry, end=end, span=span, visible=visible):
            keys = key_ref[pair, 0:end, :]
            values_t = value_t_ref[pl.ds(pl.multiple_of(pair * HD, HD), HD), 0:end]
            outs = []
            for side in range(2):
                head = pair * 2 + side
                rows = pl.ds(pl.multiple_of(head * HD, HD), HD)
                score = jnp.dot(keys, rot_ref[rows, span], preferred_element_type=F32)
                score = jnp.where(visible, score, NEG)
                top = jnp.max(score, 0, keepdims=True)
                weight = jnp.exp(score - top)
                total = jnp.sum(weight, 0, keepdims=True)
                log_ref[pl.ds(head, 1), span] = top + jnp.log(total)
                prob = (weight * (1.0 / total)).astype(BF)
                outs.append(jnp.dot(values_t, prob, preferred_element_type=F32))
            both = jnp.concatenate(outs, 0).T
            cols = pl.ds(pl.multiple_of(pair * 2 * HD, 2 * HD), 2 * HD)
            mixed_ref[span, cols] = both.astype(BF)
            return carry

        lax.fori_loop(0, PAIRS, one_pair, 0)
    core = at_ref[1]
    for part in range(2):
        span = slice(part * SPAN, (part + 1) * SPAN)
        for where, out in ((core, mine_ref), (1 - core, other_ref)):
            rows = pl.ds(pl.multiple_of((2 * part + where) * SPAN, SPAN), SPAN)
            out[span, :] = jnp.dot(
                mixed_ref[rows, :], w_mix_ref[...], preferred_element_type=F32
            ).astype(out.dtype)


def backward_kernel(
    half,
    grad_ref,
    query_ref,
    key_t_ref,
    key_ref,
    value_ref,
    query_normed_ref,
    key_normed_ref,
    inv_ref,
    log_ref,
    cos_ref,
    sin_ref,
    seg_row_ref,
    seg_col_ref,
    gain_ref,
    out_ref,
    gain_grad_ref,
    grad_t,
    head_grad,
    value_one,
    key_sum,
    value_sum,
    out_t,
):
    length = grad_ref.shape[0]
    heads = HEADS // 2
    pairs = PAIRS // 2
    for part in range(pairs):
        cols = slice(part * 2 * HD, (part + 1) * 2 * HD)
        grad_t[cols, :] = grad_ref[:, cols].astype(F32).T.astype(BF)
    values_t = value_ref[...].astype(F32).T
    for pair in range(pairs):
        value_one[pair] = values_t[pair * HD : (pair + 1) * HD, :].T.astype(BF)
    left_lane = lax.broadcasted_iota(jnp.int32, (SPAN, 2 * HD), 1) < HD
    zero = jnp.zeros((SPAN, 2 * HD), BF)

    def one_pair(pair, carry):
        key_sum[...] = jnp.zeros_like(key_sum)
        value_sum[...] = jnp.zeros_like(value_sum)
        keys_t = key_t_ref[pl.ds(pl.multiple_of(pair * HD, HD), HD), :]
        both = pl.ds(pl.multiple_of(pair * 2 * HD, 2 * HD), 2 * HD)
        for block in range(length // SPAN):
            end = (block + 1) * SPAN
            span = slice(block * SPAN, end)
            visible = visible_block(seg_col_ref[...], seg_row_ref[...], block)
            queries = query_ref[both, span].astype(F32).T.astype(BF)
            grads = grad_ref[span, both]
            for side in range(2):
                head = pair * 2 + side
                rows = pl.ds(pl.multiple_of(head * HD, HD), HD)
                score = jnp.dot(
                    key_ref[pair, 0:end, :], query_ref[rows, span], preferred_element_type=F32
                )
                logs = log_ref[pl.ds(half * heads + head, 1), span]
                prob = jnp.where(visible, jnp.exp(score - logs), 0.0)
                grad_prob = jnp.dot(
                    value_one[pair, 0:end, :], grad_t[rows, span], preferred_element_type=F32
                )
                inner = jnp.sum(prob * grad_prob, 0, keepdims=True)
                grad_score = (prob * (grad_prob - inner)).astype(BF)
                mine = left_lane if side == 0 else jnp.logical_not(left_lane)
                value_sum[0:end, :] += jnp.dot(
                    prob.astype(BF), jnp.where(mine, grads, zero), preferred_element_type=F32
                )
                key_sum[0:end, :] += jnp.dot(
                    grad_score, jnp.where(mine, queries, zero), preferred_element_type=F32
                )
                head_grad[rows, span] = jnp.dot(
                    keys_t[:, 0:end], grad_score, preferred_element_type=F32
                ) * (HD**-0.5)
        key_t = key_sum[...].T
        value_t = value_sum[...].T
        key_rows = pl.ds(pl.multiple_of((heads + pair) * HD, HD), HD)
        head_grad[key_rows, :] = key_t[:HD, :] + key_t[HD:, :]
        value_rows = pl.ds(pl.multiple_of((heads + pairs + pair) * HD, HD), HD)
        out_t[value_rows, :] = value_t[:HD, :] + value_t[HD:, :]
        return carry

    lax.fori_loop(0, pairs, one_pair, 0)

    cosine = cos_ref[...]
    sine = sin_ref[...]
    gain_sums = [jnp.zeros((HD, length), F32), jnp.zeros((HD, length), F32)]
    for head in range(heads + pairs):
        rows = slice(head * HD, (head + 1) * HD)
        kind = 0 if head < heads else 1
        part = head_grad[rows, :]
        first = part[:HALF, :]
        second = part[HALF:, :]
        turned = jnp.concatenate(
            [first * cosine + second * sine, second * cosine - first * sine], 0
        )
        if kind == 0:
            normed = query_normed_ref[rows, :]
            line = half * heads + head
        else:
            normed = key_normed_ref[(head - heads) * HD : (head - heads + 1) * HD, :]
            line = HEADS + half * pairs + head - heads
        gain_sums[kind] = gain_sums[kind] + turned * normed
        scaled = turned * gain_ref[:, kind : kind + 1]
        mean = jnp.mean(scaled * normed, 0, keepdims=True)
        out_t[rows, :] = inv_ref[line : line + 1, :] * (scaled - normed * mean)
    for kind in range(2):
        gain_grad_ref[:, kind : kind + 1] = jnp.sum(gain_sums[kind], 1, keepdims=True)
    for part in range(out_t.shape[0] // (2 * HD)):
        cols = slice(part * 2 * HD, (part + 1) * 2 * HD)
        out_ref[:, cols] = out_t[cols, :].T.astype(BF)


def in_hbm(shape, kind):
    return pltpu.HBM(shape, kind)


def from_hbm(*operands):
    return [
        pltpu.with_memory_space_constraint(value, pltpu.HBM) if value.size >= 2**16 else value
        for value in operands
    ]


def whole_refs(count):
    return [pl.BlockSpec(memory_space=pltpu.VMEM)] * count


def project(hidden, weight, cosine, sine, gains):
    length = hidden.shape[0]
    rows = (HEADS + PAIRS) * HD
    outs = [
        ((rows, length), BF),
        ((PAIRS, length, HD), BF),
        ((length, PAIRS * HD), BF),
        ((PAIRS * HD, length), BF),
        ((rows, length), F32),
        ((16, length), F32),
    ]
    return pl.pallas_call(
        project_kernel,
        out_shape=[in_hbm(shape, kind) for shape, kind in outs],
        in_specs=whole_refs(5),
        out_specs=whole_refs(len(outs)),
        compiler_params=pltpu.CompilerParams(vmem_limit_bytes=24 * 1024 * 1024),
        cost_estimate=NO_COST,
        name="project",
    )(*from_hbm(hidden, weight), cosine, sine, gains)


def attention_forward(rot, key, value_t, seg_row, seg_col, at, w_own, w_got):
    length = rot.shape[1]
    width = w_own.shape[1]
    outs = [
        ((length, HEADS * HD), BF),
        ((HEADS, length), F32),
        ((HEADS * HD, width), BF),
        ((length // 2, width), F32),
        ((length // 2, width), BF),
    ]
    return pl.pallas_call(
        forward_kernel,
        out_shape=[in_hbm(shape, kind) for shape, kind in outs],
        in_specs=whole_refs(5) + [pl.BlockSpec(memory_space=pltpu.SMEM)] + whole_refs(2),
        out_specs=whole_refs(len(outs)),
        compiler_params=pltpu.CompilerParams(vmem_limit_bytes=24 * 1024 * 1024),
        cost_estimate=NO_COST,
        name="attention_forward",
    )(*from_hbm(rot, key, value_t), seg_row, seg_col, at, *from_hbm(w_own, w_got))


def middle_kernel(inputs_ref, mine_ref, got_ref, gain_ref, middle_ref, hidden_ref):
    middle = inputs_ref[...].astype(F32) + mine_ref[...] + got_ref[...].astype(F32)
    middle_ref[...] = middle
    normed, _ = norm_rows(middle)
    hidden_ref[...] = (normed * gain_ref[...]).astype(BF)


def by_rows(kernel, name, rows_in, whole_in, rows_out, sums_out=0):
    rows, width = rows_in[0].shape
    tile = 2 * LANES
    block = pl.BlockSpec((tile, width), lambda at: (at, 0))
    line = pl.BlockSpec((1, width), lambda at: (0, 0))
    return pl.pallas_call(
        kernel,
        grid=(rows // tile,),
        out_shape=[in_hbm((rows, width), kind) for kind in rows_out]
        + [jax.ShapeDtypeStruct((1, width), F32)] * sums_out,
        in_specs=[block] * len(rows_in) + [line] * len(whole_in),
        out_specs=[block] * len(rows_out) + [line] * sums_out,
        compiler_params=pltpu.CompilerParams(vmem_limit_bytes=16 * 1024 * 1024),
        cost_estimate=NO_COST,
        name=name,
    )(*[from_hbm(value)[0] if value.dtype == F32 else value for value in rows_in], *whole_in)


def middle_grad_kernel(
    own_ref, sib_ref, got_ref, middle_ref, dy_ref, gain_ref, grad_ref, branch_ref, gain_grad_ref
):
    dh2 = own_ref[...] + sib_ref[...].astype(F32) + got_ref[...].astype(F32)
    normed, inv = norm_rows(middle_ref[...])

    @pl.when(pl.program_id(0) == 0)
    def _():
        gain_grad_ref[...] = jnp.zeros_like(gain_grad_ref)

    gain_grad_ref[...] += jnp.sum(dh2 * normed, 0, keepdims=True)
    grad = dy_ref[...].astype(F32) + norm_back(dh2 * gain_ref[...], normed, inv)
    grad_ref[...] = grad
    branch_ref[...] = grad.astype(BF)


def attention_backward(half, grad, rot, key, value, normed, inv, log, cosine, sine, seg_row, seg_col, gains):
    length = grad.shape[0]
    queries = HEADS * HD // 2
    keys = PAIRS * HD // 2
    width = queries + 2 * keys

    def rows_of(count, at):
        return pl.BlockSpec((count, length), lambda step: (at, 0))

    def columns_of(count):
        return pl.BlockSpec((length, count), lambda step: (0, half))

    key_at = 2 * queries // keys + half
    return pl.pallas_call(
        functools.partial(backward_kernel, half),
        grid=(1,),
        out_shape=[
            in_hbm((length, width), BF),
            jax.ShapeDtypeStruct((HD, 2), F32),
        ],
        in_specs=[
            columns_of(queries),
            rows_of(queries, half),
            rows_of(keys, key_at),
            pl.BlockSpec((PAIRS // 2, length, HD), lambda step: (half, 0, 0)),
            columns_of(keys),
            rows_of(queries, half),
            rows_of(keys, key_at),
        ]
        + whole_refs(7),
        out_specs=whole_refs(2),
        scratch_shapes=[
            pltpu.VMEM((queries, length), BF),
            pltpu.VMEM((queries + keys, length), F32),
            pltpu.VMEM((PAIRS // 2, length, HD), BF),
            pltpu.VMEM((length, 2 * HD), F32),
            pltpu.VMEM((length, 2 * HD), F32),
            pltpu.VMEM((width, length), F32),
        ],
        compiler_params=pltpu.CompilerParams(vmem_limit_bytes=28 * 1024 * 1024),
        cost_estimate=NO_COST,
        name="attention_backward",
    )(
        *from_hbm(grad, rot, rot, key, value, normed, normed),
        inv,
        log,
        cosine,
        sine,
        seg_row,
        seg_col,
        gains,
    )


def feed_forward_kernel(
    at_ref,
    h2_a,
    h2_b,
    dy_a,
    dy_a_got,
    dy_b,
    dy_b_got,
    w_gate,
    w_up,
    w_sib,
    piece_0,
    piece_1,
    piece_2,
    piece_3,
    w_down,
    act_a,
    act_b,
    grad_a,
    grad_b,
    back_a,
    back_b,
    dy_out_a,
    dy_out_b,
    h2_v,
    dy_v,
    in_v,
    down_v,
    act_v,
    grad_v,
    back_own,
    back_sib,
    grad_act,
    load_sems,
    store_sems,
):
    units = down_v.shape[0]

    def rows_at(index):
        return pl.ds(pl.multiple_of(at_ref[index], SPAN), SPAN)

    def units_at(index):
        return pl.ds(pl.multiple_of(at_ref[index], LANES), units)

    loads = []

    def load(source, target):
        loads.append(pltpu.make_async_copy(source, target, load_sems.at[len(loads)]))
        loads[-1].start()

    def load_dy(part, own, got):
        load(own.at[at_ref[0]], dy_v.at[part, rows_at(1)])
        load(got.at[at_ref[0]], dy_v.at[part, rows_at(2)])

    load_dy(0, dy_a, dy_a_got)
    load(w_down, down_v)
    load(h2_a, h2_v.at[0])
    load(w_gate.at[:, units_at(3)], in_v.at[rows_at(4), 0:units])
    load(w_up.at[:, units_at(3)], in_v.at[rows_at(4), units : 2 * units])
    load(w_sib, in_v.at[rows_at(5)])
    for at, piece in enumerate((piece_0, piece_1, piece_2, piece_3)):
        load(piece, in_v.at[rows_at(6 + at), units_at(10 + at)])
    weights_end = len(loads)
    load_dy(1, dy_b, dy_b_got)
    load(h2_b, h2_v.at[1])
    stores = []
    for part in range(2):
        for at in range(3) if part == 0 else range(weights_end, weights_end + 2):
            loads[at].wait()
        for start in range(0, units, 256):
            end = min(start + 256, units)
            grad_act[:, start:end] = contract(dy_v[part], down_v[start:end, :], 1, 1)
        for at in range(3, weights_end) if part == 0 else [weights_end + 2]:
            loads[at].wait()
        for start in range(0, units, LANES):
            gate_cols = slice(start, start + LANES)
            up_cols = slice(units + start, units + start + LANES)
            weight = jnp.concatenate([in_v[:, gate_cols], in_v[:, up_cols]], 1)
            both = jnp.dot(h2_v[part], weight, preferred_element_type=F32)
            gate, up = both[:, :LANES], both[:, LANES:]
            sig = jax.nn.sigmoid(gate)
            silu = gate * sig
            grad = grad_act[:, gate_cols]
            act_v[part, :, gate_cols] = (silu * up).astype(BF)
            grad_gate = grad * up * sig * (1.0 + gate * (1.0 - sig))
            grad_v[part, :, gate_cols] = grad_gate.astype(BF)
            grad_v[part, :, up_cols] = (grad * silu).astype(BF)
        back = contract(grad_v[part], in_v[...], 1, 1)
        if part == 0:
            back_own[...] = back
        else:
            back_sib[...] = back.astype(BF)
        for at, (source, target) in enumerate(
            [
                (act_v.at[part], (act_a, act_b)[part]),
                (grad_v.at[part], (grad_a, grad_b)[part]),
                ((back_own, back_sib)[part], (back_a, back_b)[part]),
                (dy_v.at[part], (dy_out_a, dy_out_b)[part]),
            ]
        ):
            stores.append(pltpu.make_async_copy(source, target, store_sems.at[part * 4 + at]))
            stores[-1].start()
    for store in stores:
        store.wait()


def feed_forward(at, h2, dy, weights, w_down):
    rows, width = h2[0].shape
    units = w_down.shape[0]
    outs = (
        [((rows, units), BF)] * 2
        + [((rows, 2 * units), BF)] * 2
        + [((rows, width), F32), ((rows, width), BF)]
        + [((rows, width), BF)] * 2
    )
    operands = from_hbm(*h2, *dy, *weights, w_down)
    return pl.pallas_call(
        feed_forward_kernel,
        out_shape=[in_hbm(shape, kind) for shape, kind in outs],
        in_specs=[pl.BlockSpec(memory_space=pltpu.SMEM)]
        + [pl.BlockSpec(memory_space=pl.ANY)] * len(operands),
        out_specs=[pl.BlockSpec(memory_space=pl.ANY)] * len(outs),
        scratch_shapes=[
            pltpu.VMEM((2, rows, width), BF),
            pltpu.VMEM((2, rows, width), BF),
            pltpu.VMEM((width, 2 * units), BF),
            pltpu.VMEM(w_down.shape, BF),
            pltpu.VMEM((2, rows, units), BF),
            pltpu.VMEM((2, rows, 2 * units), BF),
            pltpu.VMEM((rows, width), F32),
            pltpu.VMEM((rows, width), BF),
            pltpu.VMEM((rows, units), F32),
            pltpu.SemaphoreType.DMA((14,)),
            pltpu.SemaphoreType.DMA((8,)),
        ],
        compiler_params=pltpu.CompilerParams(vmem_limit_bytes=36 * 1024 * 1024),
        cost_estimate=NO_COST,
        name="feed_forward",
    )(at, *operands)


def weight_grad_kernel(count, *refs):
    left, right = refs[:count], refs[count : 2 * count]
    out, left_t = refs[-2:]

    @pl.when(pl.program_id(0) == 0)
    def _():
        for at in range(count):
            left_t[at] = left[at][...].T

    total = jnp.dot(left_t[0], right[0][...], preferred_element_type=F32)
    for at in range(1, count):
        total += jnp.dot(left_t[at], right[at][...], preferred_element_type=F32)
    out[...] = total.astype(BF)


def weight_grad(left, right):
    rows, height = left[0].shape
    width = right[0].shape[1]
    count = len(left)
    step = SPAN
    return pl.pallas_call(
        functools.partial(weight_grad_kernel, count),
        grid=(width // step,),
        out_shape=in_hbm((height, width), BF),
        in_specs=[pl.BlockSpec((rows, height), lambda at: (0, 0))] * count
        + [pl.BlockSpec((rows, step), lambda at: (0, at))] * count,
        out_specs=pl.BlockSpec((height, step), lambda at: (0, at)),
        scratch_shapes=[pltpu.VMEM((count, height, rows), BF)],
        compiler_params=pltpu.CompilerParams(vmem_limit_bytes=24 * 1024 * 1024),
        cost_estimate=NO_COST,
        name="weight_grad",
    )(*from_hbm(*left, *right))


def norm_rows(inputs):
    inv = lax.rsqrt(jnp.mean(inputs * inputs, -1, keepdims=True) + EPS)
    return (inputs * inv, inv)


def norm_back(grad, normed, inv):
    return inv * (grad - normed * jnp.mean(grad * normed, -1, keepdims=True))


def swap_y(value):
    return lax.ppermute(value, "group", Y_SWAP)


def swap_cross(value):
    return lax.ppermute(value, "group", CROSS_SWAP)


def swap_core(value):
    return lax.ppermute(value, "group", CORE_SWAP)


def after(value, *earlier):
    return lax.optimization_barrier((value, earlier))[0]


def cycle_of(count):
    return list(range(0, count, 2)) + list(range(count - 1, 0, -2))


class Ring:
    def __init__(self, way):
        count = lax.axis_size("replica")
        cycle = cycle_of(count)[::way]
        self.count = count
        self.way = way
        self.hops = [(cycle[at], cycle[(at + 1) % count]) for at in range(count)]
        mine = lax.axis_index("replica")
        self.place = jnp.where(lax.rem(mine, 2) == 0, mine // 2, count - 1 - mine // 2)

    def chunk_at(self, back):
        at = lax.rem(self.place - self.way * back + self.count, self.count)
        return jnp.where(at < self.count // 2, 2 * at, 2 * (self.count - 1 - at) + 1)

    def send(self, value):
        return lax.ppermute(value, "replica", self.hops)


def pick_kernel(step, count, index_ref, *refs):
    sources = refs[:count]
    arrived = refs[count:-5]
    outs = refs[-5:-3]
    low, high, sems = refs[-3:]
    rows_low = low.shape[1]
    half = low.shape[2]
    down_rows, rows = rows_low, high.shape[2]
    copies = []
    for side in range(2):
        index = index_ref[step, side]
        cols = slice(side * half, (side + 1) * half)
        copies.append(
            pltpu.make_async_copy(
                sources[0].at[pl.ds(pl.multiple_of(index * down_rows, 16), down_rows), cols],
                low.at[side],
                sems.at[side, 0],
            )
        )
        copies.append(
            pltpu.make_async_copy(
                sources[1].at[:, pl.ds(pl.multiple_of(index * rows, 16), rows), cols],
                high.at[side],
                sems.at[side, 1],
            )
        )
    for copy in copies:
        copy.start()
    for copy in copies:
        copy.wait()
    for side in range(2):
        parts = [(0, rows_low, low[side].astype(F32))]
        for at in range(high.shape[1]):
            start = rows_low + at * rows
            parts.append((start, start + rows, high[side, at].astype(F32)))
        for start, end, part in parts:
            if arrived:
                part = part + arrived[side][start:end, :].astype(F32)
            outs[side][start:end, :] = part.astype(BF)


def pick_chunks(step, indices, sources, arrived):
    copies = indices.shape[0]
    down_rows = sources[0].shape[0] // copies
    kinds, span, width = sources[1].shape
    rows = span // copies
    half = width // 2
    if rows % 16 or down_rows % 16:
        moving = []
        for side in range(2):
            index = indices[step, side]
            start = side * half
            low = lax.dynamic_slice(sources[0], (index * down_rows, start), (down_rows, half))
            high = lax.dynamic_slice(sources[1], (0, index * rows, start), (kinds, rows, half))
            part = jnp.concatenate([low.astype(F32), high.astype(F32).reshape(-1, half)])
            if arrived:
                part = part + arrived[side].astype(F32)
            moving.append(part.astype(BF))
        return moving
    total = down_rows + kinds * rows
    return pl.pallas_call(
        functools.partial(pick_kernel, step, 2),
        out_shape=[jax.ShapeDtypeStruct((total, half), BF)] * 2,
        in_specs=[pl.BlockSpec(memory_space=pltpu.SMEM)]
        + [pl.BlockSpec(memory_space=pl.ANY)] * 2
        + whole_refs(len(arrived)),
        out_specs=whole_refs(2),
        scratch_shapes=[
            pltpu.VMEM((2, down_rows, half), sources[0].dtype),
            pltpu.VMEM((2, kinds, rows, half), sources[1].dtype),
            pltpu.SemaphoreType.DMA((2, 2)),
        ],
        compiler_params=pltpu.CompilerParams(vmem_limit_bytes=8 * 1024 * 1024),
        cost_estimate=NO_COST,
        name="pick_chunks",
    )(indices, *from_hbm(*sources), *arrived)


def sum_over_rings(rings, indices, sources):
    moving = pick_chunks(1, indices, sources, [])
    for step in range(2, rings[0].count + 1):
        arrived = [ring.send(chunk) for ring, chunk in zip(rings, moving)]
        moving = pick_chunks(step % rings[0].count, indices, sources, arrived)
    return moving


def place_kernel(step, targets, stores, index_ref, *refs):
    chunks = refs[:2]
    outs = refs[-3 - stores : -3]
    wide = refs[-3:-1]
    sems = refs[-1]
    for side in range(2):
        wide[side][...] = chunks[side][...].astype(F32)
    copies = []
    for at, (store, side, (top, bottom), (start, end), column) in enumerate(targets):
        rows = bottom - top
        row = pl.multiple_of(index_ref[step, side] * rows, 8)
        copies.append(
            pltpu.make_async_copy(
                wide[side].at[top:bottom, start:end],
                outs[store].at[pl.ds(row, rows), column : column + end - start],
                sems.at[at],
            )
        )
    for copy in copies:
        copy.start()
    for copy in copies:
        copy.wait()


def place_chunks(step, indices, chunks, stores, shapes, targets):
    if any((bottom - top) % 8 for _, _, (top, bottom), _, _ in targets):
        stores = stores or [jnp.zeros(shape, F32) for shape in shapes]
        for store, side, (top, bottom), (start, end), column in targets:
            stores[store] = lax.dynamic_update_slice(
                stores[store],
                chunks[side][top:bottom, start:end].astype(F32),
                (indices[step, side] * (bottom - top), column),
            )
        return stores
    given = stores or []
    return list(
        pl.pallas_call(
            functools.partial(place_kernel, step, targets, len(shapes)),
            out_shape=[in_hbm(shape, F32) for shape in shapes],
            in_specs=[pl.BlockSpec(memory_space=pltpu.SMEM)]
            + [pl.BlockSpec(memory_space=pltpu.VMEM)] * 2
            + [pl.BlockSpec(memory_space=pl.ANY)] * len(given),
            out_specs=[pl.BlockSpec(memory_space=pl.ANY)] * len(shapes),
            scratch_shapes=[pltpu.VMEM(chunk.shape, F32) for chunk in chunks]
            + [pltpu.SemaphoreType.DMA((len(targets),))],
            input_output_aliases={3 + at: at for at in range(len(given))},
            compiler_params=pltpu.CompilerParams(vmem_limit_bytes=8 * 1024 * 1024),
            cost_estimate=NO_COST,
            name="place_chunks",
        )(indices, *chunks, *from_hbm(*given))
    )


def gather_over_rings(rings, indices, chunks, shapes, targets):
    stores = place_chunks(0, indices, chunks, None, shapes, targets)
    earlier = []
    for step in range(1, rings[0].count):
        chunks = [ring.send(chunk) for ring, chunk in zip(rings, after(chunks, *earlier))]
        earlier = stores
        stores = place_chunks(step, indices, chunks, stores, shapes, targets)
    return stores


def per_device(
    hidden_in,
    segments,
    positions,
    out_grad,
    attn_gain,
    w_query,
    w_key,
    w_value,
    query_gain,
    key_gain,
    w_out,
    ffn_gain,
    w_gate,
    w_up,
    w_down,
):
    copies = lax.axis_size("replica")
    member = lax.axis_index("group")
    y_at = member // 2
    core = lax.rem(member, 2)
    on_low_y = y_at == 0
    on_low_core = core == 0
    span, width = hidden_in.shape[1:]
    hidden_units = w_down.shape[0]

    def by_y(mine, other):
        return jnp.where(on_low_y, mine, other), jnp.where(on_low_y, other, mine)

    def by_core(mine, other):
        return jnp.where(on_low_core, mine, other), jnp.where(on_low_core, other, mine)

    def at_y(pair_low, pair_high):
        return jnp.where(on_low_y, pair_low, pair_high), jnp.where(on_low_y, pair_high, pair_low)

    def at_core(low, high):
        return jnp.where(on_low_core, low, high), jnp.where(on_low_core, high, low)

    def quarters(weight):
        size = weight.shape[1] // 4
        return [weight[:, at * size : (at + 1) * size] for at in range(4)]

    def core_columns(*weights):
        parts = [quarters(weight) for weight in weights]
        low = [part[0] for part in parts] + [part[2] for part in parts]
        high = [part[1] for part in parts] + [part[3] for part in parts]
        return at_core(jnp.concatenate(low, 1), jnp.concatenate(high, 1))

    def own_and_other(rows):
        parts = rows.reshape(2, 2, span, rows.shape[-1])
        mine, other = at_core(parts[:, 0], parts[:, 1])
        return mine.reshape(2 * span, -1), other.reshape(2 * span, -1)

    def in_order(mine, at_y, sibling, across):
        here = jnp.concatenate(by_core(mine, sibling), 0)
        there = jnp.concatenate(by_core(at_y, across), 0)
        return jnp.concatenate(by_y(here, there), 0)

    replica = lax.axis_index("replica")
    bit_low = lax.rem(replica, 2)
    bit_high = lax.rem(replica // 2, 2)

    def swap_replica(value, bit):
        return lax.ppermute(value, "replica", [(at, at ^ bit) for at in range(copies)])

    seq_mine, seq_other = at_y(hidden_in[0], hidden_in[1])
    seq_got = swap_y(seq_other)

    small = jnp.concatenate(
        [
            attn_gain.astype(F32)[None],
            ffn_gain.astype(F32)[None],
            segments.astype(F32),
            positions.astype(F32),
        ],
        0,
    )
    small_got = swap_y(small)
    w_query, w_key, w_value = after((w_query, w_key, w_value), seq_other, small)
    kv_rows = jnp.concatenate([w_key, w_value], 1)
    half_send = jnp.where(bit_low == 0, w_query, kv_rows)
    half_got = swap_y(half_send)
    w_query, w_key, w_value, w_gate, w_up = after(
        (w_query, w_key, w_value, w_gate, w_up), half_send
    )
    mine_cols, other_cols = core_columns(w_query, w_key, w_value)
    rows_core = swap_core(other_cols)

    def unit_columns(weight, owner):
        return lax.dynamic_slice(weight, (0, owner * hidden_units), (span, hidden_units))

    target = member ^ (2 + bit_high)
    piece_send = jnp.where(bit_low == 0, unit_columns(w_gate, target), unit_columns(w_up, target))
    pieces = {
        0: lax.ppermute(
            piece_send,
            ("replica", "group"),
            [
                (4 * at + of, 4 * at + (of ^ (2 + (at // 2) % 2)))
                for at in range(copies)
                for of in range(4)
            ],
        )
    }

    small_low, small_high = by_y(small, small_got)
    small_two = jnp.stack([small_low, small_high])
    small_even, small_odd = by_core(small_two, swap_core(small_two))
    small_all = jnp.stack([small_even, small_odd], 1).reshape(4, 6, span)
    small_rows = small_all.transpose(1, 0, 2).reshape(6, 4 * span)
    gain_one = small_rows[0]
    gain_two = small_rows[1]
    seg = jnp.where(on_low_y, small_rows[2], small_rows[3])
    place = jnp.where(on_low_y, small_rows[4], small_rows[5])

    own_low, own_high = by_y(seq_mine, seq_got)
    own_in = jnp.stack([own_low, own_high])
    all_even, all_odd = by_core(own_in, swap_core(own_in))
    all_in = jnp.stack([all_even, all_odd], 1).reshape(4 * span, width)
    normed_all, inv_all = norm_rows(all_in.astype(F32))
    hidden_one = (normed_all * gain_one).astype(BF)
    freq = THETA ** (-(jnp.arange(HALF, dtype=F32) * 2.0 / HD))
    angle = freq[:, None] * place[None, :]
    cosine, sine = jnp.cos(angle), jnp.sin(angle)
    gains = jnp.stack([query_gain, key_gain], 1).astype(F32)
    seg_row = seg[None, :]
    seg_col = seg[:, None]
    unit_core = swap_core(
        jnp.concatenate([unit_columns(w_gate, member ^ 1), unit_columns(w_up, member ^ 1)], 1)
    )

    half_swapped = swap_replica(half_got, 1)
    query_y = jnp.where(bit_low == 0, half_got, half_swapped)
    rest_y = jnp.where(bit_low == 0, half_swapped, half_got)
    mine_y, other_y = core_columns(query_y, rest_y[:, : width // 2], rest_y[:, width // 2 :])
    rows_cross = swap_core(after(other_y, pieces[0]))
    w_attn = in_order(mine_cols, mine_y, rows_core, rows_cross)
    pieces[1] = swap_replica(pieces[0], 1)
    pieces[2] = swap_replica(pieces[0], 2)
    w_out_send, dy_send = after((w_out, out_grad), pieces[0])
    out_got = swap_y(w_out_send)
    dy_got = swap_y(dy_send)

    rot, key_rot, value_low, value_t, head_normed, head_inv = project(
        hidden_one, w_attn, cosine, sine, gains
    )
    pieces[1], pieces[2], out_got, rot = after((pieces[1], pieces[2], out_got, rot), rot)
    pieces[3] = swap_replica(pieces[2], 1)
    rot = after(rot, pieces[1], pieces[2], out_got)
    mixed, log_total, w_mix, mix_mine, mix_other = attention_forward(
        rot, key_rot, value_t, seg_row, seg_col, jnp.stack([y_at, core]), w_out, out_got
    )
    mix_other, pieces[3], dy_got = after((mix_other, pieces[3], dy_got), mixed)
    mix_got = swap_core(mix_other)
    dy_got, mix_got = after((dy_got, mix_got), mix_got)

    inputs = own_in.reshape(2 * span, width)
    middle, hidden_two = by_rows(
        middle_kernel, "middle", [inputs, mix_mine, mix_got], [gain_two[None]], [F32, BF]
    )
    h2_got = swap_y(hidden_two)
    h2_sib = swap_core(hidden_two)
    dy_sib = swap_core(out_grad)
    dy_sib_got = swap_core(dy_got)
    units = hidden_units
    fours = bit_low + 2 * bit_high
    kinds = [fours ^ at for at in range(4)]
    places = [member * span, (member ^ 1) * span]
    places += [(member ^ (2 + kind // 2)) * span for kind in kinds]
    places += [lax.rem(kind, 2) * units for kind in kinds]

    def ffn(seq, h2):
        head = [seq, y_at * span, (1 - y_at) * span, member * units]
        return feed_forward(
            jnp.stack(head + places),
            h2,
            (out_grad, dy_got, dy_sib, dy_sib_got),
            (w_gate, w_up, unit_core, *[pieces[at] for at in range(4)]),
            w_down,
        )

    act_own, act_sib, grad_own, grad_sib, back_own, back_sib, dy_own, dy_sib_own = ffn(
        y_at, (hidden_two, h2_sib)
    )
    sib_got = swap_core(back_sib)
    h2_near = (hidden_two, h2_sib)
    h2_next = after(h2_got, sib_got)
    h2_far = (h2_next, swap_core(h2_next))
    act_next, act_diag, grad_next, grad_diag, back_next, back_diag, dy_next, dy_diag = ffn(
        1 - y_at, h2_far
    )
    dh2_send = (back_next + swap_core(back_diag).astype(F32)).astype(BF)
    dh2_got = swap_y(dh2_send)
    grads = after((grad_own, grad_sib, grad_next, grad_diag), dh2_send)
    ffn_grad = weight_grad((*h2_near, *h2_far), grads)
    down_grad = weight_grad(
        after((act_own, act_sib, act_next, act_diag), ffn_grad),
        (dy_own, dy_sib_own, dy_next, dy_diag),
    )
    ffn_part = lax.psum_scatter(
        ffn_grad.reshape(4, span, 2 * units), "replica", scatter_dimension=1, tiled=True
    )
    dh2_got = after(dh2_got, down_grad)

    def chunk_pair(rows):
        parts = rows.reshape(2, span, width)
        return at_y(parts[0], parts[1])

    grad_middle, grad_branch, ffn_gain_part = by_rows(
        middle_grad_kernel,
        "middle_grad",
        [back_own, sib_got, dh2_got, middle, dy_own],
        [gain_two[None]],
        [F32, BF],
        1,
    )
    grad_branch = grad_branch.reshape(2, span, width)
    branch_even, branch_odd = by_core(grad_branch, swap_core(grad_branch))
    branch_all = jnp.stack([branch_even, branch_odd], 1).reshape(4 * span, width)
    grad_mixed = contract(branch_all, w_mix, 1, 1).astype(BF)
    mix_grad = contract(mixed, branch_all, 0, 0)
    mix_here, mix_there = at_y(mix_grad[:span], mix_grad[span:])
    mix_there = mix_there.astype(BF)
    mix_grad_got = swap_y(mix_there)
    grad_mixed = after(grad_mixed, mix_there)
    head_grads = []
    head_gain_part = 0.0
    rows_here = []
    rows_got = []
    for part in range(2):
        grad_heads, gain_part = attention_backward(
            part,
            grad_mixed,
            rot,
            key_rot,
            value_low,
            head_normed,
            head_inv,
            log_total,
            cosine,
            sine,
            seg_row,
            seg_col,
            gains,
        )
        head_gain_part = head_gain_part + gain_part
        head_grads.append(grad_heads)
        attn_grad = contract(hidden_one, grad_heads, 0, 0).reshape(2, 2 * span, -1)
        here, there = at_y(attn_grad[0], attn_grad[1])
        there = there.astype(BF)
        rows_here.append(here)
        rows_got.append(swap_y(there))
        grad_mixed = after(grad_mixed, there)
    head_grads = jnp.concatenate(after(head_grads, grad_mixed), 1)
    back_one = contract(head_grads, w_attn, 1, 1)
    one_mine, one_other = own_and_other(back_one)
    grad_hidden_one = one_mine + swap_core(one_other.astype(BF)).astype(F32)
    inputs = inputs.astype(F32)
    inv_one, _ = own_and_other(inv_all)
    normed_one = inputs * inv_one
    attn_gain_part = jnp.sum(grad_hidden_one * normed_one, 0)
    grad_input = grad_middle + norm_back(grad_hidden_one * gain_one, normed_one, inv_one)
    input_here, input_there = chunk_pair(grad_input)
    input_back = swap_y(input_there.astype(BF))

    acts = after((act_own, act_sib, act_next, act_diag), back_one)
    out_own, out_sib, out_next, out_diag = [
        jnp.dot(act, w_down, preferred_element_type=F32) for act in acts
    ]
    out_own = middle + out_own + swap_core(out_sib.astype(BF)).astype(F32)
    out_next = out_next + swap_core(out_diag.astype(BF)).astype(F32)

    own_here, own_there = chunk_pair(out_own)
    next_here, next_there = chunk_pair(out_next)
    out_back = swap_y(jnp.stack([own_there, next_there]).astype(BF))
    right, left = Ring(1), Ring(-1)
    rows = span // copies
    indices = jnp.stack(
        [jnp.stack([ring.chunk_at(step) for ring in (right, left)]) for step in range(copies)]
    )
    half = width // 2
    head_sum = jnp.stack(
        [
            *jnp.concatenate(
                [here + got.astype(F32) for here, got in zip(rows_here, rows_got)], 1
            ).reshape(2, span, width),
            mix_here + mix_grad_got.astype(F32),
        ]
    )
    sums_right, sums_left = sum_over_rings((right, left), indices, (down_grad, head_sum))
    down_rows = units // copies

    def all_heads(part):
        owners = part[down_rows : down_rows + 2 * rows].reshape(2, rows, half)
        mine, other = at_core(owners[0], owners[1])
        both = by_core(mine, swap_core(other))
        return jnp.concatenate([part[:down_rows], *both, part[down_rows + 2 * rows :]])

    def own_rows(part):
        parts = part.reshape(2, 2, rows, 2 * units)
        mine, other = at_core(parts[:, 0], parts[:, 1])
        both_cores = jnp.stack(by_core(mine, swap_core(other)), 1)
        here, there = at_y(both_cores[0], both_cores[1])
        all_units = by_y(here, swap_y(there))
        blocks = [block[at] for block in all_units for at in range(2)]
        return [
            jnp.concatenate([block[:, start : start + units] for block in blocks], 1)
            for start in (0, units)
        ]

    w_gate_grad, w_up_grad = gather_over_rings(
        (right, left),
        indices,
        own_rows(ffn_part),
        [w_gate.shape, w_up.shape],
        [(side, side, (0, rows), (0, 4 * units), 0) for side in range(2)],
    )
    targets = []
    for side in range(2):
        targets.append((0, side, (0, down_rows), (0, half), side * half))
        for at in range(2):
            top = down_rows + at * rows
            place_rows = (top, top + rows)
            half_at = side * span + at * span // 2
            targets += [
                (1, side, place_rows, (0, span), side * 2 * span + at * span),
                (2, side, place_rows, (span, span + span // 2), half_at),
                (3, side, place_rows, (span + span // 2, 2 * span), half_at),
            ]
        top = down_rows + 2 * rows
        targets.append((4, side, (top, top + rows), (0, half), side * half))
    w_down_grad, w_query_grad, w_key_grad, w_value_grad, w_out_grad = gather_over_rings(
        (right, left),
        indices,
        [all_heads(sums_right), all_heads(sums_left)],
        [value.shape for value in (w_down, w_query, w_key, w_value, w_out)],
        targets,
    )

    sums = jnp.concatenate([attn_gain_part, ffn_gain_part[0], head_gain_part.T.reshape(-1)])
    sums = after(sums.reshape(-1, 128), sums_right)
    sums = sums + swap_core(sums)
    sums = sums + swap_y(sums)
    step = 1
    while step < copies:
        sums = sums + lax.ppermute(sums, "replica", [(at, at ^ step) for at in range(copies)])
        step *= 2
    sums = sums.reshape(-1)
    attn_gain_grad = lax.dynamic_slice(sums, (member * span,), (span,))
    ffn_gain_grad = lax.dynamic_slice(sums, (width + member * span,), (span,))
    query_gain_grad = sums[2 * width : 2 * width + HD]
    key_gain_grad = sums[2 * width + HD : 2 * width + 2 * HD]

    out_back, input_back = after((out_back, input_back), sums_right)
    out_back, input_back = out_back.astype(F32), input_back.astype(F32)
    input_grad = jnp.stack(by_y(input_here, input_back))
    block_out = jnp.stack(by_y(own_here + out_back[1], next_here + out_back[0])).astype(BF)

    return (
        block_out,
        input_grad,
        attn_gain_grad,
        w_query_grad,
        w_key_grad,
        w_value_grad,
        query_gain_grad,
        key_gain_grad,
        w_out_grad,
        ffn_gain_grad,
        w_gate_grad,
        w_up_grad,
        w_down_grad,
    )


def solution(mesh):
    rows = P("group", None)
    tokens = P("replica", "group", None)
    placed = (
        tokens,
        P("replica", "group"),
        P("replica", "group"),
        tokens,
        P("group"),
        rows,
        rows,
        rows,
        P(),
        P(),
        rows,
        P("group"),
        rows,
        rows,
        rows,
    )
    return jax.shard_map(
        per_device,
        mesh=mesh,
        in_specs=placed,
        out_specs=(
            tokens,
            tokens,
            P("group"),
            rows,
            rows,
            rows,
            P(),
            P(),
            rows,
            P("group"),
            rows,
            rows,
            rows,
        ),
        check_vma=False,
    )
```

time: 563 us -> 473 us (0.84); the launches traced: 554 us -> 471 us
  Pallas kernels: 83.9 us -> 191 us
  matrix products: 94 us -> 17.3 us
  waiting for transfers between devices: 180 us -> 124 us
  other arithmetic: 71.4 us -> 40.6 us
  local copies, waits for them, and re-layouts: 24.7 us -> 11.3 us
  starting transfers between devices: 84.4 us -> 71.3 us
    pallas_call x18 -> x34, Pallas kernels: 83.9 us -> 191 us  [the longest x2 39 us: feed_forward(): pl.pallas_call(feed_forward_kernel, out_shape=[in_hbm(shape, kind) for sh...]
    ppermute x16 -> x14, waiting for transfers between devices: 118 us -> 26.9 us  [swap_y(): return lax.ppermute(value, 'group', Y_SWAP)]
    dot_general x16 -> x5, matrix products: 92.8 us -> 11.1 us  [contract(): lax.dot_general(left, right, (((left_dim,), (right_dim,)), ((), ())), pre...]
    ppermute x42, waiting for transfers between devices: 44.7 us -> 67.3 us  [send(): return lax.ppermute(value, 'replica', self.hops)]
    ppermute x20, waiting for transfers between devices: 3.41 us -> 16.1 us  [swap_core(): return lax.ppermute(value, 'group', CORE_SWAP)]
    add x5 -> x2, other arithmetic: 9.88 us -> 0.53 us  [per_device(): here + got.astype(F32)]
    ppermute x16 -> x14, starting transfers between devices: 23.6 us -> 14.6 us  [swap_y(): return lax.ppermute(value, 'group', Y_SWAP)]
    select_n x5 -> x1, other arithmetic: 6.59 us -> 0.39 us  [at_core(): jnp.where(on_low_core, low, high)]
  transfers between devices with their start and end apart: 87 -> 85, of which waited for: 41 -> 42; matrix products, arithmetic and copies ran while one was open for 27% -> 13% of each run, Pallas kernels for 15% -> 35%
where the time goes in v3:
time: 473 us; the launch traced here: 471 us
  Pallas kernels  191 us (40%)
  waiting for transfers between devices  124 us (26%)
  starting transfers between devices  71.3 us (15%)
  other arithmetic  40.6 us (9%)
  matrix products  17.3 us (4%)
  between operations  15.7 us (3%)
  local copies, waits for them, and re-layouts  11.3 us (2%)
    ppermute x42, waiting for transfers between devices, send(): return lax.ppermute(value, 'replica', self.hops)  67.3 us
    ppermute x42, starting transfers between devices, send(): return lax.ppermute(value, 'replica', self.hops)  43.6 us
    pallas_call x2, Pallas kernels, feed_forward(): pl.pallas_call(feed_forward_kernel, out_shape=[in_hbm(shape, kind) for sh...  39 us
    pallas_call x1, Pallas kernels, attention_forward(): pl.pallas_call(forward_kernel, out_shape=[in_hbm(shape, kind) for shape,...  38.6 us
    pallas_call x2, Pallas kernels, attention_backward(): pl.pallas_call(functools.partial(backward_kernel, half), grid=(1,), out_s...  28.4 us
    pallas_call x2, Pallas kernels, weight_grad(): pl.pallas_call(functools.partial(weight_grad_kernel, count), grid=(width...  27.2 us
    pallas_call x16, Pallas kernels, place_chunks(): pl.pallas_call(functools.partial(place_kernel, step, targets, len(shapes)...  26.9 us
    ppermute x14, waiting for transfers between devices, swap_y(): return lax.ppermute(value, 'group', Y_SWAP)  26.9 us
  transfers between devices with their start and end apart: 85, of which 42 were waited for; matrix products, arithmetic and copies ran while one was open for 13% of the time, Pallas kernels for 35%

profile of v3, /device:TPU:0, one launch (start us, length us, event | category | flops | bytes accessed | tf_op | source)
XLA Modules:
  0.0 470.6 jit_solution(17455664642958373286)
XLA Ops:
  7.3 2.2 select_bitcast_fusion.4
  9.5 3.0 collective-permute-start
  15.2 2.2 maximum_select_fusion
  17.4 2.0 collective-permute-start.9
  19.4 2.7 constant_dynamic-slice_fusion.1
  31.3 5.6 %collective-permute-done.9 = bf16[256,1024]{1,0:T(8,128)(2,1)} collective-permute-done((bf16[256,1024]{1,0:T(8,128)(2,1)}, bf16[256,1024]{1,0:T(8,128)(2,1)}, u32[]{:S(2)}, u32[]{:S(2)}) %collective-permute-start.9) | collective-permute-done | bytes 524320 | tf_op jit(solution)/shard_map/ppermute | solution.py:597
  36.9 2.0 collective-permute-start.10
  41.4 7.2 %collective-permute-done.1.piece_0 = bf16[256,1152]{1,0:T(8,128)(2,1)S(1)} collective-permute-done((bf16[256,1152]{1,0:T(8,128)(2,1)}, bf16[256,1152]{1,0:T(8,128)(2,1)S(1)}, u32[]{:S(2)}, u32[]{:S(2)}) %collective-permute-start.1) | collective-permute-done | bytes 589856 | tf_op jit(solution)/shard_map/ppermute | solution.py:877
  62.1 8.0 %project.1 = (bf16[768,1024]{1,0:T(8,128)(2,1)}, bf16[4,1024,64]{2,1,0:T(8,128)(2,1)}, bf16[1024,256]{1,0:T(8,128)(2,1)}, bf16[256,1024]{1,0:T(8,128)(2,1)}, f32[768,1024]{1,0:T(8,128)}, /*index=5*/f32[16,1024]{1,0:T(8,128)}) custom-call(bf16[1024,1024]{1,0:T(8,128)(2,1)} %fusion.1.hidden_ref, bf16[1024,1024]{1,0:T(8,128)(2,1)} %pad_maximum_fusion.1.weight_ref, ...), custom_call_target="tpu_custom_call" | custom-call | tf_op jit(solution)/shard_map/project/pallas_call | solution.py:285
  71.3 38.6 %attention_forward.1 = (bf16[1024,512]{1,0:T(8,128)(2,1)}, f32[8,1024]{1,0:T(8,128)}, bf16[512,1024]{1,0:T(8,128)(2,1)}, f32[512,1024]{1,0:T(8,128)}, bf16[512,1024]{1,0:T(8,128)(2,1)}) custom-call(bf16[768,1024]{1,0:T(8,128)(2,1)} %get-tuple-element.206.rot_ref.query_ref.key_t_ref, bf16[4,1024,64]{2,1,0:T(8,128)(2,1)} %get-tuple-element.207.key_ref, ...), custom_call_target="tpu_custom_call" | custom-call | tf_op jit(solution)/shard_map/attention_forward/pallas_call | solution.py:306
  112.8 3.1 middle.1
  120.5 19.3 %feed_forward.2 = (bf16[512,1152]{1,0:T(8,128)(2,1)}, bf16[512,1152]{1,0:T(8,128)(2,1)}, bf16[512,2304]{1,0:T(8,128)(2,1)}, bf16[512,2304]{1,0:T(8,128)(2,1)}, f...) custom-call(s32[14]{0:T(128)S(1)} %stack.301.at_ref, ...), custom_call_target="tpu_custom_call" | custom-call | tf_op jit(solution)/shard_map/feed_forward/pallas_call | solution.py:528
  140.0 2.2 collective-permute-done.19.h2_a.refs_2_
  142.9 2.8 collective-permute-done.21.h2_b.refs_3_
  145.7 19.7 %feed_forward.3 = (bf16[512,1152]{1,0:T(8,128)(2,1)}, bf16[512,1152]{1,0:T(8,128)(2,1)}, bf16[512,2304]{1,0:T(8,128)(2,1)}, bf16[512,2304]{1,0:T(8,128)(2,1)}, f...) custom-call(s32[14]{0:T(128)S(1)} %stack.303.at_ref, ...), custom_call_target="tpu_custom_call" | custom-call | tf_op jit(solution)/shard_map/feed_forward/pallas_call | solution.py:528
  165.6 2.7 collective-permute-done.22
  168.4 2.0 add_convert_fusion
  171.6 16.6 %weight_grad.2 = bf16[1024,2304]{1,0:T(8,128)(2,1)} custom-call(bf16[512,1024]{1,0:T(8,128)(2,1)} %get-tuple-element.217.h2_a.refs_0_, bf16[512,1024]{1,0:T(8,128)(2,1)} %collective-permute-done.15.h2_b.refs_1_, bf16[512,1024]{1,0:T(8,128)(2,1)} %collective-permute-done.19.h2_a.refs_2_, bf16[512,1024]{1,0:T(8,128)(2,1)} %collective-permute-done.21.h2_b.refs_3_, ...), custom_call_target="tpu_custom_call" | custom-call | tf_op jit(solution)/shard_map/weight_grad/pallas_call | solution.py:573
  188.2 10.6 %weight_grad.3.refs_0_ = bf16[1152,1024]{1,0:T(8,128)(2,1)} custom-call(bf16[512,1152]{1,0:T(8,128)(2,1)} %get-tuple-element.258.refs_0_, bf16[512,1152]{1,0:T(8,128)(2,1)} %get-tuple-element.259.refs_1_, bf16[512,1152]{1,0:T(8,128)(2,1)} %get-tuple-element.260.refs_2_, bf16[512,1152]{1,0:T(8,128)(2,1)} %get-tuple-element.261.refs_3_, ...), custom_call_target="tpu_custom_call" | custom-call | tf_op jit(solution)/shard_map/weight_grad/pallas_call | solution.py:573
  198.9 4.5 middle_grad.1
  203.7 2.6 collective-permute-done.24
  211.8 2.3 convolution_convert_fusion.2.grad_ref
  214.0 14.2 %attention_backward.2 = (bf16[1024,512]{1,0:T(8,128)(2,1)}, f32[64,2]{1,0:T(8,128)S(1)}) custom-call(bf16[1024,512]{1,0:T(8,128)(2,1)} %convolution_convert_fusion.2.grad_ref, bf16[768,1024]{1,0:T(8,128)(2,1)} %get-tuple-element.206.rot_ref.query_ref.key_t_ref, bf16[768,1024]{1,0:T(8,128)(2,1)} %get-tuple-element.206.rot_ref.query_ref.key_t_ref, ...), custom_call_target="tpu_custom_call" | custom-call | tf_op jit(solution)/shard_map/attention_backward/pallas_call | solution.py:371
  228.2 2.5 fusion.35
  232.1 14.3 %attention_backward.3 = (bf16[1024,512]{1,0:T(8,128)(2,1)}, f32[64,2]{1,0:T(8,128)S(1)}) custom-call(bf16[1024,512]{1,0:T(8,128)(2,1)} %convolution_convert_fusion.2.grad_ref, bf16[768,1024]{1,0:T(8,128)(2,1)} %get-tuple-element.206.rot_ref.query_ref.key_t_ref, bf16[768,1024]{1,0:T(8,128)(2,1)} %get-tuple-element.206.rot_ref.query_ref.key_t_ref, ...), custom_call_target="tpu_custom_call" | custom-call | tf_op jit(solution)/shard_map/attention_backward/pallas_call | solution.py:371
  246.4 3.7 fusion.2
  257.0 12.3 %collective-permute-done.31 = bf16[512,512]{1,0:T(8,128)(2,1)S(1)} collective-permute-done((bf16[512,512]{1,0:T(8,128)(2,1)S(1)}, bf16[512,512]{1,0:T(8,128)(2,1)S(1)}, u32[]{:S(2)}, u32[]{:S(2)}) %collective-permute-start.31) | collective-permute-done | bytes 524320 | tf_op jit(solution)/shard_map/ppermute | solution.py:597
  269.7 1.9 pad_maximum_fusion.refs_1_
  275.8 8.9 %collective-permute-done.33.refs_2_ = bf16[240,512]{1,0:T(8,128)(2,1)S(1)} collective-permute-done((bf16[240,512]{1,0:T(8,128)(2,1)S(1)}, bf16[240,512]{1,0:T(8,128)(2,1)S(1)}, u32[]{:S(2)}, u32[]{:S(2)}) %collective-permute-start.33) | collective-permute-done | bytes 245792 | tf_op jit(solution)/shard_map/ppermute | solution.py:631
  284.7 8.8 %collective-permute-done.34.refs_3_ = bf16[240,512]{1,0:T(8,128)(2,1)S(1)} collective-permute-done((bf16[240,512]{1,0:T(8,128)(2,1)S(1)}, bf16[240,512]{1,0:T(8,128)(2,1)S(1)}, u32[]{:S(2)}, u32[]{:S(2)}) %collective-permute-start.34) | collective-permute-done | bytes 245792 | tf_op jit(solution)/shard_map/ppermute | solution.py:631
  293.6 1.9 pick_chunks.9
  295.5 2.0 collective-permute-start.36
  298.0 6.0 %collective-permute-done.35.refs_2_ = bf16[240,512]{1,0:T(8,128)(2,1)S(1)} collective-permute-done((bf16[240,512]{1,0:T(8,128)(2,1)S(1)}, bf16[240,512]{1,0:T(8,128)(2,1)S(1)}, u32[]{:S(2)}, u32[]{:S(2)}) %collective-permute-start.35) | collective-permute-done | bytes 245792 | tf_op jit(solution)/shard_map/ppermute | solution.py:631
  304.0 2.2 collective-permute-done.36.refs_3_
  318.1 2.4 collective-permute-start.39
  320.7 6.0 %collective-permute-done.39.refs_2_ = bf16[240,512]{1,0:T(8,128)(2,1)S(1)} collective-permute-done((bf16[240,512]{1,0:T(8,128)(2,1)S(1)}, bf16[240,512]{1,0:T(8,128)(2,1)S(1)}, u32[]{:S(2)}, u32[]{:S(2)}) %collective-permute-start.39) | collective-permute-done | bytes 245792 | tf_op jit(solution)/shard_map/ppermute | solution.py:631
  326.7 2.6 collective-permute-done.40.refs_3_
  331.3 2.1 collective-permute-start.42
  335.7 3.5 collective-permute-done.41.refs_2_
  344.1 4.3 collective-permute-done.43.refs_2_
  353.4 2.0 multiply_add_fusion
  355.4 2.1 collective-permute-done.45.refs_2_
  367.2 6.8 %collective-permute-done.69 = bf16[2,32,2304]{2,1,0:T(8,128)(2,1)S(1)} collective-permute-done((bf16[2,32,2304]{2,1,0:T(8,128)(2,1)S(1)}, bf16[2,32,2304]{2,1,0:T(8,128)(2,1)S(1)}, u32[]{:S(2)}, u32[]{:S(2)}) %collective-permute-start.69) | collective-permute-done | bytes 294944 | tf_op jit(solution)/shard_map/ppermute | solution.py:597
  380.8 3.4 collective-permute-done.70.refs_0_
  386.3 3.2 collective-permute-done.56.refs_0_
  392.5 4.4 collective-permute-done.57.refs_1_
  427.6 6.2 %collective-permute-done.50 = f32[17,128]{1,0:T(8,128)S(1)} collective-permute-done((f32[17,128]{1,0:T(8,128)S(1)}, f32[17,128]{1,0:T(8,128)S(1)}, u32[]{:S(2)}, u32[]{:S(2)}) %collective-permute-start.50) | collective-permute-done | bytes 8736 | tf_op jit(solution)/shard_map/ppermute | solution.py:1128
  449.7 2.0 collective-permute-done.80.refs_0_
  (359 shorter events, 163.2 us)
Async XLA Ops:
  7.2 353.8 %reduce-scatter.2.cloned.1.call-start = ((), (), s32[]{:S(2)}) async-start(), calls=%async_computation.1 | async-start | bytes 5308416 | tf_op jit(solution)/shard_map/reduce_scatter | solution.py:982
  9.5 29.5 %collective-permute-start = (bf16[256,1024]{1,0:T(8,128)(2,1)}, bf16[256,1024]{1,0:T(8,128)(2,1)}, u32[]{:S(2)}, u32[]{:S(2)}) collective-permute-start(bf16[256,1024]{1,0:T(8,128)(2,1)} %select_bitcast_fusion.4), channel_id=1, source_target_pairs={{0,2},{2,0},{1,3},{3,1},{4,6},{6,4},{5,7},{7,5},{8,10},{10,8},{9,1... | collective-permute-start | bytes 1572872 | tf_op jit(solution)/shard_map/ppermute | solution.py:597
  15.1 13.6 %collective-permute-start.6 = (f32[6,256]{1,0:T(8,128)S(1)}, f32[6,256]{1,0:T(8,128)S(1)}, u32[]{:S(2)}, u32[]{:S(2)}) collective-permute-start(f32[6,256]{1,0:T(8,128)S(1)} %pad_maximum_fusion.18), channel_id=1, source_target_pairs={{0,2},{2,0},{1,3},{3,1},{4,6},{6,4},{5,7},{7,5},{8,10},{10,8},{9,1... | collective-permute-start | bytes 18440 | tf_op jit(solution)/shard_map/ppermute | solution.py:597
  17.4 19.5 %collective-permute-start.9 = (bf16[256,1024]{1,0:T(8,128)(2,1)}, bf16[256,1024]{1,0:T(8,128)(2,1)}, u32[]{:S(2)}, u32[]{:S(2)}) collective-permute-start(bf16[256,1024]{1,0:T(8,128)(2,1)} %maximum_select_fusion), channel_id=1, source_target_pairs={{0,2},{2,0},{1,3},{3,1},{4,6},{6,4},{5,7},{7,5},{8,10},{10,8},{9,1... | collective-permute-start | bytes 1572872 | tf_op jit(solution)/shard_map/ppermute | solution.py:597
  22.0 26.6 %collective-permute-start.1 = (bf16[256,1152]{1,0:T(8,128)(2,1)}, bf16[256,1152]{1,0:T(8,128)(2,1)S(1)}, u32[]{:S(2)}, u32[]{:S(2)}) collective-permute-start(bf16[256,1152]{1,0:T(8,128)(2,1)} %get-tuple-element.376), channel_id=1, source_target_pairs={{0,2},{1,3},{2,0},{3,1},{4,6},{5,7},{6,4},{7,5},{8,11},{9,10},{10,... | collective-permute-start | bytes 1769480 | tf_op jit(solution)/shard_map/ppermute | solution.py:877
  28.7 11.6 %collective-permute-start.8 = (bf16[256,1024]{1,0:T(8,128)(2,1)}, bf16[256,1024]{1,0:T(8,128)(2,1)}, u32[]{:S(2)}, u32[]{:S(2)}) collective-permute-start(bf16[256,1024]{1,0:T(8,128)(2,1)} %broadcast_select_fusion.8), channel_id=1, source_target_pairs={{0,1},{1,0},{2,3},{3,2},{4,5},{5,4},{6,7},{7,6},{8,9},{9,8},{10,11... | collective-permute-start | bytes 1572872 | tf_op jit(solution)/shard_map/ppermute | solution.py:605
  36.9 15.5 %collective-permute-start.10 = (bf16[256,1024]{1,0:T(8,128)(2,1)}, bf16[256,1024]{1,0:T(8,128)(2,1)S(1)}, u32[]{:S(2)}, u32[]{:S(2)}) collective-permute-start(bf16[256,1024]{1,0:T(8,128)(2,1)} %collective-permute-done.9), channel_id=1, source_target_pairs={{0,4},{4,0},{8,12},{12,8},{16,20},{20,16},{24,28},{28,24},{1,5},{5... | collective-permute-start | bytes 1572872 | tf_op jit(solution)/shard_map/ppermute | solution.py:846
  40.2 14.4 %collective-permute-start.5 = (bf16[2,256,1024]{2,1,0:T(8,128)(2,1)S(1)}, bf16[2,256,1024]{2,1,0:T(8,128)(2,1)S(1)}, u32[]{:S(2)}, u32[]{:S(2)}) collective-permute-start(bf16[2,256,1024]{2,1,0:T(8,128)(2,1)S(1)} %pad_maximum_fusion.6), channel_id=1, source_target_pairs={{0,1},{1,0},{2,3},{3,2},{4,5},{5,4},{6,7},{7,6},{8,9},{9,8},{10,11... | collective-permute-start | bytes 3145736 | tf_op jit(solution)/shard_map/ppermute | solution.py:605
  48.6 21.4 %collective-permute-start.4 = (bf16[256,1024]{1,0:T(8,128)(2,1)S(1)}, bf16[256,1024]{1,0:T(8,128)(2,1)S(1)}, u32[]{:S(2)}, u32[]{:S(2)}) collective-permute-start(bf16[256,1024]{1,0:T(8,128)(2,1)S(1)} %copy-done.29), channel_id=1, source_target_pairs={{0,2},{2,0},{1,3},{3,1},{4,6},{6,4},{5,7},{7,5},{8,10},{10,8},{9,1... | collective-permute-start | bytes 1572872 | tf_op jit(solution)/shard_map/ppermute | solution.py:597
  50.4 59.5 %collective-permute-start.13 = (bf16[2,256,1024]{2,1,0:T(8,128)(2,1)}, bf16[2,256,1024]{2,1,0:T(8,128)(2,1)}, u32[]{:S(2)}, u32[]{:S(2)}) collective-permute-start(bf16[2,256,1024]{2,1,0:T(8,128)(2,1)} %dy_a.3), channel_id=1, source_target_pairs={{0,2},{2,0},{1,3},{3,1},{4,6},{6,4},{5,7},{7,5},{8,10},{10,8},{9,1... | collective-permute-start | bytes 3145736 | tf_op jit(solution)/shard_map/ppermute | solution.py:597
  50.6 19.4 %collective-permute-start.2 = (bf16[256,1152]{1,0:T(8,128)(2,1)S(1)}, bf16[256,1152]{1,0:T(8,128)(2,1)S(1)}, u32[]{:S(2)}, u32[]{:S(2)}) collective-permute-start(bf16[256,1152]{1,0:T(8,128)(2,1)S(1)} %collective-permute-done.1.piece_0), channel_id=1, source_target_pairs={{0,4},{4,0},{8,12},{12,8},{16,20},{20,16},{24,28},{28,24},{1,5},{5... | collective-permute-start | bytes 1769480 | tf_op jit(solution)/shard_map/ppermute | solution.py:846
  52.4 17.7 %collective-permute-start.3 = (bf16[256,1152]{1,0:T(8,128)(2,1)S(1)}, bf16[256,1152]{1,0:T(8,128)(2,1)}, u32[]{:S(2)}, u32[]{:S(2)}) collective-permute-start(bf16[256,1152]{1,0:T(8,128)(2,1)S(1)} %collective-permute-done.1.piece_0), channel_id=1, source_target_pairs={{0,8},{4,12},{8,0},{12,4},{16,24},{20,28},{24,16},{28,20},{1,9},{5... | collective-permute-start | bytes 1769480 | tf_op jit(solution)/shard_map/ppermute | solution.py:846
  70.1 39.8 %collective-permute-start.12 = (bf16[256,1152]{1,0:T(8,128)(2,1)}, bf16[256,1152]{1,0:T(8,128)(2,1)S(1)}, u32[]{:S(2)}, u32[]{:S(2)}) collective-permute-start(bf16[256,1152]{1,0:T(8,128)(2,1)} %collective-permute-done.3.piece_2), channel_id=1, source_target_pairs={{0,4},{4,0},{8,12},{12,8},{16,20},{20,16},{24,28},{28,24},{1,5},{5... | collective-permute-start | bytes 1769480 | tf_op jit(solution)/shard_map/ppermute | solution.py:846
  116.6 25.6 %collective-permute-start.19 = (bf16[512,1024]{1,0:T(8,128)(2,1)}, bf16[512,1024]{1,0:T(8,128)(2,1)}, u32[]{:S(2)}, u32[]{:S(2)}) collective-permute-start(bf16[512,1024]{1,0:T(8,128)(2,1)} %get-tuple-element.217.h2_a.refs_0_), channel_id=1, source_target_pairs={{0,2},{2,0},{1,3},{3,1},{4,6},{6,4},{5,7},{7,5},{8,10},{10,8},{9,1... | collective-permute-start | bytes 3145736 | tf_op jit(solution)/shard_map/ppermute | solution.py:597
  170.4 28.5 %collective-permute-start.23 = (bf16[512,1024]{1,0:T(8,128)(2,1)S(1)}, bf16[512,1024]{1,0:T(8,128)(2,1)S(1)}, u32[]{:S(2)}, u32[]{:S(2)}) collective-permute-start(bf16[512,1024]{1,0:T(8,128)(2,1)S(1)} %add_convert_fusion), channel_id=1, source_target_pairs={{0,2},{2,0},{1,3},{3,1},{4,6},{6,4},{5,7},{7,5},{8,10},{10,8},{9,1... | collective-permute-start | bytes 3145736 | tf_op jit(solution)/shard_map/ppermute | solution.py:597
  210.9 45.5 %collective-permute-start.32 = (bf16[256,1024]{1,0:T(8,128)(2,1)S(1)}, bf16[256,1024]{1,0:T(8,128)(2,1)S(1)}, u32[]{:S(2)}, u32[]{:S(2)}) collective-permute-start(bf16[256,1024]{1,0:T(8,128)(2,1)S(1)} %select_convert_fusion.8), channel_id=1, source_target_pairs={{0,2},{2,0},{1,3},{3,1},{4,6},{6,4},{5,7},{7,5},{8,10},{10,8},{9,1... | collective-permute-start | bytes 1572872 | tf_op jit(solution)/shard_map/ppermute | solution.py:597
  230.8 25.9 %collective-permute-start.30 = (bf16[512,512]{1,0:T(8,128)(2,1)S(1)}, bf16[512,512]{1,0:T(8,128)(2,1)S(1)}, u32[]{:S(2)}, u32[]{:S(2)}) collective-permute-start(bf16[512,512]{1,0:T(8,128)(2,1)S(1)} %select_convert_fusion.7), channel_id=1, source_target_pairs={{0,2},{2,0},{1,3},{3,1},{4,6},{6,4},{5,7},{7,5},{8,10},{10,8},{9,1... | collective-permute-start | bytes 1572872 | tf_op jit(solution)/shard_map/ppermute | solution.py:597
  251.7 60.1 %collective-permute-start.26 = (bf16[512,1024]{1,0:T(8,128)(2,1)S(1)}, bf16[512,1024]{1,0:T(8,128)(2,1)S(1)}, u32[]{:S(2)}, u32[]{:S(2)}) collective-permute-start(bf16[512,1024]{1,0:T(8,128)(2,1)S(1)} %convolution_convert_fusion), channel_id=1, source_target_pairs={{0,1},{1,0},{2,3},{3,2},{4,5},{5,4},{6,7},{7,6},{8,9},{9,8},{10,11... | collective-permute-start | bytes 3145736 | tf_op jit(solution)/shard_map/ppermute | solution.py:605
  253.4 56.8 %collective-permute-start.25 = (bf16[512,1024]{1,0:T(8,128)(2,1)S(1)}, bf16[512,1024]{1,0:T(8,128)(2,1)S(1)}, u32[]{:S(2)}, u32[]{:S(2)}) collective-permute-start(bf16[512,1024]{1,0:T(8,128)(2,1)S(1)} %convolution_convert_fusion.1), channel_id=1, source_target_pairs={{0,1},{1,0},{2,3},{3,2},{4,5},{5,4},{6,7},{7,6},{8,9},{9,8},{10,11... | collective-permute-start | bytes 3145736 | tf_op jit(solution)/shard_map/ppermute | solution.py:605
  255.3 13.9 %collective-permute-start.31 = (bf16[512,512]{1,0:T(8,128)(2,1)S(1)}, bf16[512,512]{1,0:T(8,128)(2,1)S(1)}, u32[]{:S(2)}, u32[]{:S(2)}) collective-permute-start(bf16[512,512]{1,0:T(8,128)(2,1)S(1)} %select_convert_fusion.3), channel_id=1, source_target_pairs={{0,2},{2,0},{1,3},{3,1},{4,6},{6,4},{5,7},{7,5},{8,10},{10,8},{9,1... | collective-permute-start | bytes 1572872 | tf_op jit(solution)/shard_map/ppermute | solution.py:597
  273.5 11.2 %collective-permute-start.33 = (bf16[240,512]{1,0:T(8,128)(2,1)S(1)}, bf16[240,512]{1,0:T(8,128)(2,1)S(1)}, u32[]{:S(2)}, u32[]{:S(2)}) collective-permute-start(bf16[240,512]{1,0:T(8,128)(2,1)S(1)} %get-tuple-element.263), channel_id=1, source_target_pairs={{0,8},{8,16},{16,24},{24,28},{28,20},{20,12},{12,4},{4,0},{1,9},{9... | collective-permute-start | bytes 737288 | tf_op jit(solution)/shard_map/ppermute | solution.py:631
  275.2 18.3 %collective-permute-start.34 = (bf16[240,512]{1,0:T(8,128)(2,1)S(1)}, bf16[240,512]{1,0:T(8,128)(2,1)S(1)}, u32[]{:S(2)}, u32[]{:S(2)}) collective-permute-start(bf16[240,512]{1,0:T(8,128)(2,1)S(1)} %get-tuple-element.264), channel_id=1, source_target_pairs={{4,12},{12,20},{20,28},{28,24},{24,16},{16,8},{8,0},{0,4},{5,13},{... | collective-permute-start | bytes 737288 | tf_op jit(solution)/shard_map/ppermute | solution.py:631
  275.7 67.5 %collective-permute-start.28 = (bf16[512,1024]{1,0:T(8,128)(2,1)S(1)}, bf16[512,1024]{1,0:T(8,128)(2,1)S(1)}, u32[]{:S(2)}, u32[]{:S(2)}) collective-permute-start(bf16[512,1024]{1,0:T(8,128)(2,1)S(1)} %bitcast.269), channel_id=1, source_target_pairs={{0,1},{1,0},{2,3},{3,2},{4,5},{5,4},{6,7},{7,6},{8,9},{9,8},{10,11... | collective-permute-start | bytes 3145736 | tf_op jit(solution)/shard_map/ppermute | solution.py:605
  295.5 10.7 %collective-permute-start.36 = (bf16[240,512]{1,0:T(8,128)(2,1)S(1)}, bf16[240,512]{1,0:T(8,128)(2,1)S(1)}, u32[]{:S(2)}, u32[]{:S(2)}) collective-permute-start(bf16[240,512]{1,0:T(8,128)(2,1)S(1)} %get-tuple-element.266), channel_id=1, source_target_pairs={{4,12},{12,20},{20,28},{28,24},{24,16},{16,8},{8,0},{0,4},{5,13},{... | collective-permute-start | bytes 737288 | tf_op jit(solution)/shard_map/ppermute | solution.py:631
  334.6 68.2 %collective-permute-start.27 = (bf16[2,256,1024]{2,1,0:T(8,128)(2,1)}, bf16[2,256,1024]{2,1,0:T(8,128)(2,1)}, u32[]{:S(2)}, u32[]{:S(2)}) collective-permute-start(bf16[2,256,1024]{2,1,0:T(8,128)(2,1)} %pad_maximum_fusion.9), channel_id=1, source_target_pairs={{0,2},{2,0},{1,3},{3,1},{4,6},{6,4},{5,7},{7,5},{8,10},{10,8},{9,1... | collective-permute-start | bytes 3145736 | tf_op jit(solution)/shard_map/ppermute | solution.py:597
  365.1 11.3 %collective-permute-start.54 = (bf16[240,512]{1,0:T(8,128)(2,1)S(1)}, bf16[240,512]{1,0:T(8,128)(2,1)S(1)}, u32[]{:S(2)}, u32[]{:S(2)}) collective-permute-start(bf16[240,512]{1,0:T(8,128)(2,1)S(1)} %pad_maximum_fusion.14.refs_0_), channel_id=1, source_target_pairs={{0,8},{8,16},{16,24},{24,28},{28,20},{20,12},{12,4},{4,0},{1,9},{9... | collective-permute-start | bytes 737288 | tf_op jit(solution)/shard_map/ppermute | solution.py:631
  365.9 12.6 %collective-permute-start.55 = (bf16[240,512]{1,0:T(8,128)(2,1)S(1)}, bf16[240,512]{1,0:T(8,128)(2,1)S(1)}, u32[]{:S(2)}, u32[]{:S(2)}) collective-permute-start(bf16[240,512]{1,0:T(8,128)(2,1)S(1)} %pad_maximum_fusion.15.refs_1_), channel_id=1, source_target_pairs={{4,12},{12,20},{20,28},{28,24},{24,16},{16,8},{8,0},{0,4},{5,13},{... | collective-permute-start | bytes 737288 | tf_op jit(solution)/shard_map/ppermute | solution.py:631
  374.3 10.0 %collective-permute-start.70 = (bf16[32,4608]{1,0:T(8,128)(2,1)S(1)}, bf16[32,4608]{1,0:T(8,128)(2,1)S(1)}, u32[]{:S(2)}, u32[]{:S(2)}) collective-permute-start(bf16[32,4608]{1,0:T(8,128)(2,1)S(1)} %pad_maximum_fusion.12.refs_0_), channel_id=1, source_target_pairs={{0,8},{8,16},{16,24},{24,28},{28,20},{20,12},{12,4},{4,0},{1,9},{9... | collective-permute-start | bytes 884744 | tf_op jit(solution)/shard_map/ppermute | solution.py:631
  376.4 24.5 %collective-permute-start.29 = (bf16[256,1024]{1,0:T(8,128)(2,1)S(1)}, bf16[256,1024]{1,0:T(8,128)(2,1)S(1)}, u32[]{:S(2)}, u32[]{:S(2)}) collective-permute-start(bf16[256,1024]{1,0:T(8,128)(2,1)S(1)} %select_convert_fusion.4), channel_id=1, source_target_pairs={{0,2},{2,0},{1,3},{3,1},{4,6},{6,4},{5,7},{7,5},{8,10},{10,8},{9,1... | collective-permute-start | bytes 1572872 | tf_op jit(solution)/shard_map/ppermute | solution.py:597
  378.5 11.0 %collective-permute-start.56 = (bf16[240,512]{1,0:T(8,128)(2,1)S(1)}, bf16[240,512]{1,0:T(8,128)(2,1)S(1)}, u32[]{:S(2)}, u32[]{:S(2)}) collective-permute-start(bf16[240,512]{1,0:T(8,128)(2,1)S(1)} %collective-permute-done.54.refs_0_), channel_id=1, source_target_pairs={{0,8},{8,16},{16,24},{24,28},{28,20},{20,12},{12,4},{4,0},{1,9},{9... | collective-permute-start | bytes 737288 | tf_op jit(solution)/shard_map/ppermute | solution.py:631
  384.3 14.6 %collective-permute-start.72 = (bf16[32,4608]{1,0:T(8,128)(2,1)S(1)}, bf16[32,4608]{1,0:T(8,128)(2,1)S(1)}, u32[]{:S(2)}, u32[]{:S(2)}) collective-permute-start(bf16[32,4608]{1,0:T(8,128)(2,1)S(1)} %collective-permute-done.70.refs_0_), channel_id=1, source_target_pairs={{0,8},{8,16},{16,24},{24,28},{28,20},{20,12},{12,4},{4,0},{1,9},{9... | collective-permute-start | bytes 884744 | tf_op jit(solution)/shard_map/ppermute | solution.py:631
  384.9 15.8 %collective-permute-start.73 = (bf16[32,4608]{1,0:T(8,128)(2,1)S(1)}, bf16[32,4608]{1,0:T(8,128)(2,1)S(1)}, u32[]{:S(2)}, u32[]{:S(2)}) collective-permute-start(bf16[32,4608]{1,0:T(8,128)(2,1)S(1)} %collective-permute-done.71.refs_1_), channel_id=1, source_target_pairs={{4,12},{12,20},{20,28},{28,24},{24,16},{16,8},{8,0},{0,4},{5,13},{... | collective-permute-start | bytes 884744 | tf_op jit(solution)/shard_map/ppermute | solution.py:631
  400.6 10.3 %collective-permute-start.74 = (bf16[32,4608]{1,0:T(8,128)(2,1)S(1)}, bf16[32,4608]{1,0:T(8,128)(2,1)S(1)}, u32[]{:S(2)}, u32[]{:S(2)}) collective-permute-start(bf16[32,4608]{1,0:T(8,128)(2,1)S(1)} %collective-permute-done.72.refs_0_), channel_id=1, source_target_pairs={{0,8},{8,16},{16,24},{24,28},{28,20},{20,12},{12,4},{4,0},{1,9},{9... | collective-permute-start | bytes 884744 | tf_op jit(solution)/shard_map/ppermute | solution.py:631
  401.0 9.9 %collective-permute-start.75 = (bf16[32,4608]{1,0:T(8,128)(2,1)S(1)}, bf16[32,4608]{1,0:T(8,128)(2,1)S(1)}, u32[]{:S(2)}, u32[]{:S(2)}) collective-permute-start(bf16[32,4608]{1,0:T(8,128)(2,1)S(1)} %collective-permute-done.73.refs_1_), channel_id=1, source_target_pairs={{4,12},{12,20},{20,28},{28,24},{24,16},{16,8},{8,0},{0,4},{5,13},{... | collective-permute-start | bytes 884744 | tf_op jit(solution)/shard_map/ppermute | solution.py:631
  407.2 9.8 %collective-permute-start.60 = (bf16[240,512]{1,0:T(8,128)(2,1)S(1)}, bf16[240,512]{1,0:T(8,128)(2,1)S(1)}, u32[]{:S(2)}, u32[]{:S(2)}) collective-permute-start(bf16[240,512]{1,0:T(8,128)(2,1)S(1)} %collective-permute-done.58.refs_0_), channel_id=1, source_target_pairs={{0,8},{8,16},{16,24},{24,28},{28,20},{20,12},{12,4},{4,0},{1,9},{9... | collective-permute-start | bytes 737288 | tf_op jit(solution)/shard_map/ppermute | solution.py:631
  407.5 9.5 %collective-permute-start.61 = (bf16[240,512]{1,0:T(8,128)(2,1)S(1)}, bf16[240,512]{1,0:T(8,128)(2,1)S(1)}, u32[]{:S(2)}, u32[]{:S(2)}) collective-permute-start(bf16[240,512]{1,0:T(8,128)(2,1)S(1)} %collective-permute-done.59.refs_1_), channel_id=1, source_target_pairs={{4,12},{12,20},{20,28},{28,24},{24,16},{16,8},{8,0},{0,4},{5,13},{... | collective-permute-start | bytes 737288 | tf_op jit(solution)/shard_map/ppermute | solution.py:631
  410.9 11.5 %collective-permute-start.76 = (bf16[32,4608]{1,0:T(8,128)(2,1)S(1)}, bf16[32,4608]{1,0:T(8,128)(2,1)S(1)}, u32[]{:S(2)}, u32[]{:S(2)}) collective-permute-start(bf16[32,4608]{1,0:T(8,128)(2,1)S(1)} %collective-permute-done.74.refs_0_), channel_id=1, source_target_pairs={{0,8},{8,16},{16,24},{24,28},{28,20},{20,12},{12,4},{4,0},{1,9},{9... | collective-permute-start | bytes 884744 | tf_op jit(solution)/shard_map/ppermute | solution.py:631
  411.2 11.4 %collective-permute-start.77 = (bf16[32,4608]{1,0:T(8,128)(2,1)S(1)}, bf16[32,4608]{1,0:T(8,128)(2,1)S(1)}, u32[]{:S(2)}, u32[]{:S(2)}) collective-permute-start(bf16[32,4608]{1,0:T(8,128)(2,1)S(1)} %collective-permute-done.75.refs_1_), channel_id=1, source_target_pairs={{4,12},{12,20},{20,28},{28,24},{24,16},{16,8},{8,0},{0,4},{5,13},{... | collective-permute-start | bytes 884744 | tf_op jit(solution)/shard_map/ppermute | solution.py:631
  413.8 11.3 %collective-permute-start.49 = (f32[17,128]{1,0:T(8,128)S(1)}, f32[17,128]{1,0:T(8,128)S(1)}, u32[]{:S(2)}, u32[]{:S(2)}) collective-permute-start(f32[17,128]{1,0:T(8,128)S(1)} %add.300), channel_id=1, source_target_pairs={{0,4},{4,0},{8,12},{12,8},{16,20},{20,16},{24,28},{28,24},{1,5},{5... | collective-permute-start | bytes 26120 | tf_op jit(solution)/shard_map/ppermute | solution.py:1128
  417.0 20.0 %collective-permute-start.62 = (bf16[240,512]{1,0:T(8,128)(2,1)S(1)}, bf16[240,512]{1,0:T(8,128)(2,1)S(1)}, u32[]{:S(2)}, u32[]{:S(2)}) collective-permute-start(bf16[240,512]{1,0:T(8,128)(2,1)S(1)} %collective-permute-done.60.refs_0_), channel_id=1, source_target_pairs={{0,8},{8,16},{16,24},{24,28},{28,20},{20,12},{12,4},{4,0},{1,9},{9... | collective-permute-start | bytes 737288 | tf_op jit(solution)/shard_map/ppermute | solution.py:631
  418.4 18.6 %collective-permute-start.63 = (bf16[240,512]{1,0:T(8,128)(2,1)S(1)}, bf16[240,512]{1,0:T(8,128)(2,1)S(1)}, u32[]{:S(2)}, u32[]{:S(2)}) collective-permute-start(bf16[240,512]{1,0:T(8,128)(2,1)S(1)} %collective-permute-done.61.refs_1_), channel_id=1, source_target_pairs={{4,12},{12,20},{20,28},{28,24},{24,16},{16,8},{8,0},{0,4},{5,13},{... | collective-permute-start | bytes 737288 | tf_op jit(solution)/shard_map/ppermute | solution.py:631
  422.7 18.1 %collective-permute-start.78 = (bf16[32,4608]{1,0:T(8,128)(2,1)S(1)}, bf16[32,4608]{1,0:T(8,128)(2,1)S(1)}, u32[]{:S(2)}, u32[]{:S(2)}) collective-permute-start(bf16[32,4608]{1,0:T(8,128)(2,1)S(1)} %collective-permute-done.76.refs_0_), channel_id=1, source_target_pairs={{0,8},{8,16},{16,24},{24,28},{28,20},{20,12},{12,4},{4,0},{1,9},{9... | collective-permute-start | bytes 884744 | tf_op jit(solution)/shard_map/ppermute | solution.py:631
  423.6 17.2 %collective-permute-start.79 = (bf16[32,4608]{1,0:T(8,128)(2,1)S(1)}, bf16[32,4608]{1,0:T(8,128)(2,1)S(1)}, u32[]{:S(2)}, u32[]{:S(2)}) collective-permute-start(bf16[32,4608]{1,0:T(8,128)(2,1)S(1)} %collective-permute-done.77.refs_1_), channel_id=1, source_target_pairs={{4,12},{12,20},{20,28},{28,24},{24,16},{16,8},{8,0},{0,4},{5,13},{... | collective-permute-start | bytes 884744 | tf_op jit(solution)/shard_map/ppermute | solution.py:631
  433.8 10.2 %collective-permute-start.51 = (f32[17,128]{1,0:T(8,128)S(1)}, f32[17,128]{1,0:T(8,128)S(1)}, u32[]{:S(2)}, u32[]{:S(2)}) collective-permute-start(f32[17,128]{1,0:T(8,128)S(1)} %add.302), channel_id=1, source_target_pairs={{0,16},{4,20},{8,24},{12,28},{16,0},{20,4},{24,8},{28,12},{1,17},{... | collective-permute-start | bytes 26120 | tf_op jit(solution)/shard_map/ppermute | solution.py:1128
  440.8 10.9 %collective-permute-start.80 = (bf16[32,4608]{1,0:T(8,128)(2,1)S(1)}, bf16[32,4608]{1,0:T(8,128)(2,1)S(1)}, u32[]{:S(2)}, u32[]{:S(2)}) collective-permute-start(bf16[32,4608]{1,0:T(8,128)(2,1)S(1)} %collective-permute-done.78.refs_0_), channel_id=1, source_target_pairs={{0,8},{8,16},{16,24},{24,28},{28,20},{20,12},{12,4},{4,0},{1,9},{9... | collective-permute-start | bytes 884744 | tf_op jit(solution)/shard_map/ppermute | solution.py:631
  441.1 11.2 %collective-permute-start.81 = (bf16[32,4608]{1,0:T(8,128)(2,1)S(1)}, bf16[32,4608]{1,0:T(8,128)(2,1)S(1)}, u32[]{:S(2)}, u32[]{:S(2)}) collective-permute-start(bf16[32,4608]{1,0:T(8,128)(2,1)S(1)} %collective-permute-done.79.refs_1_), channel_id=1, source_target_pairs={{4,12},{12,20},{20,28},{28,24},{24,16},{16,8},{8,0},{0,4},{5,13},{... | collective-permute-start | bytes 884744 | tf_op jit(solution)/shard_map/ppermute | solution.py:631
  446.0 11.3 %collective-permute-start.66 = (bf16[240,512]{1,0:T(8,128)(2,1)S(1)}, bf16[240,512]{1,0:T(8,128)(2,1)S(1)}, u32[]{:S(2)}, u32[]{:S(2)}) collective-permute-start(bf16[240,512]{1,0:T(8,128)(2,1)S(1)} %collective-permute-done.64.refs_0_), channel_id=1, source_target_pairs={{0,8},{8,16},{16,24},{24,28},{28,20},{20,12},{12,4},{4,0},{1,9},{9... | collective-permute-start | bytes 737288 | tf_op jit(solution)/shard_map/ppermute | solution.py:631
  447.8 9.8 %collective-permute-start.67 = (bf16[240,512]{1,0:T(8,128)(2,1)S(1)}, bf16[240,512]{1,0:T(8,128)(2,1)S(1)}, u32[]{:S(2)}, u32[]{:S(2)}) collective-permute-start(bf16[240,512]{1,0:T(8,128)(2,1)S(1)} %collective-permute-done.65.refs_1_), channel_id=1, source_target_pairs={{4,12},{12,20},{20,28},{28,24},{24,16},{16,8},{8,0},{0,4},{5,13},{... | collective-permute-start | bytes 737288 | tf_op jit(solution)/shard_map/ppermute | solution.py:631
  (73 other events, 549.0 us)
Sparse Core Ops, SparseCore 0:
  203.6 102.1 reduce-scatter.1

commit v4 on v3

--- a/solution.py
+++ b/solution.py
@@ -107,6 +107,7 @@
     w_mix_ref,
     mine_ref,
     other_ref,
+    mixed_t,
 ):
     w_mix_ref[pl.ds(pl.multiple_of(at_ref[0] * SPAN, SPAN), SPAN), :] = w_own_ref[...]
     w_mix_ref[pl.ds(pl.multiple_of((1 - at_ref[0]) * SPAN, SPAN), SPAN), :] = w_got_ref[...]
@@ -115,27 +116,26 @@
         span = slice(block * SPAN, end)
         visible = visible_block(seg_col_ref[...], seg_row_ref[...], block)
 
-        def one_pair(pair, carry, end=end, span=span, visible=visible):
-            keys = key_ref[pair, 0:end, :]
+        def one_head(head, carry, end=end, span=span, visible=visible):
+            pair = head // 2
+            rows = pl.ds(pl.multiple_of(head * HD, HD), HD)
+            score = jnp.dot(
+                key_ref[pair, 0:end, :], rot_ref[rows, span], preferred_element_type=F32
+            )
+            score = jnp.where(visible, score, NEG)
+            top = jnp.max(score, 0, keepdims=True)
+            weight = jnp.exp(score - top)
+            total = jnp.sum(weight, 0, keepdims=True)
+            log_ref[pl.ds(head, 1), span] = top + jnp.log(total)
+            prob = (weight * (1.0 / total)).astype(BF)
             values_t = value_t_ref[pl.ds(pl.multiple_of(pair * HD, HD), HD), 0:end]
-            outs = []
-            for side in range(2):
-                head = pair * 2 + side
-                rows = pl.ds(pl.multiple_of(head * HD, HD), HD)
-                score = jnp.dot(keys, rot_ref[rows, span], preferred_element_type=F32)
-                score = jnp.where(visible, score, NEG)
-                top = jnp.max(score, 0, keepdims=True)
-                weight = jnp.exp(score - top)
-                total = jnp.sum(weight, 0, keepdims=True)
-                log_ref[pl.ds(head, 1), span] = top + jnp.log(total)
-                prob = (weight * (1.0 / total)).astype(BF)
-                outs.append(jnp.dot(values_t, prob, preferred_element_type=F32))
-            both = jnp.concatenate(outs, 0).T
-            cols = pl.ds(pl.multiple_of(pair * 2 * HD, 2 * HD), 2 * HD)
-            mixed_ref[span, cols] = both.astype(BF)
+            mixed_t[rows, :] = jnp.dot(values_t, prob, preferred_element_type=F32)
             return carry
 
-        lax.fori_loop(0, PAIRS, one_pair, 0)
+        lax.fori_loop(0, HEADS, one_head, 0)
+        for pair in range(PAIRS):
+            cols = slice(pair * 2 * HD, (pair + 1) * 2 * HD)
+            mixed_ref[span, cols] = mixed_t[cols, :].T.astype(BF)
     core = at_ref[1]
     for part in range(2):
         span = slice(part * SPAN, (part + 1) * SPAN)
@@ -308,6 +308,7 @@
         out_shape=[in_hbm(shape, kind) for shape, kind in outs],
         in_specs=whole_refs(5) + [pl.BlockSpec(memory_space=pltpu.SMEM)] + whole_refs(2),
         out_specs=whole_refs(len(outs)),
+        scratch_shapes=[pltpu.VMEM((HEADS * HD, SPAN), F32)],
         compiler_params=pltpu.CompilerParams(vmem_limit_bytes=24 * 1024 * 1024),
         cost_estimate=NO_COST,
         name="attention_forward",
@@ -633,88 +634,95 @@
 
 def pick_kernel(step, count, index_ref, *refs):
     sources = refs[:count]
-    arrived = refs[count:-5]
-    outs = refs[-5:-3]
-    low, high, sems = refs[-3:]
-    rows_low = low.shape[1]
-    half = low.shape[2]
-    down_rows, rows = rows_low, high.shape[2]
+    outs, shares, sems = refs[-count - 3 : -count - 1], refs[-count - 1 : -1], refs[-1]
+    arrived = refs[count : -count - 3]
     copies = []
     for side in range(2):
-        index = index_ref[step, side]
-        cols = slice(side * half, (side + 1) * half)
-        copies.append(
-            pltpu.make_async_copy(
-                sources[0].at[pl.ds(pl.multiple_of(index * down_rows, 16), down_rows), cols],
-                low.at[side],
-                sems.at[side, 0],
+        for at, (source, share) in enumerate(zip(sources, shares)):
+            _, _, rows, half = share.shape
+            row = pl.multiple_of(index_ref[step, side] * rows, 8)
+            copies.append(
+                pltpu.make_async_copy(
+                    source.at[:, pl.ds(row, rows), side * half : (side + 1) * half],
+                    share.at[side],
+                    sems.at[side, at],
+                )
             )
-        )
-        copies.append(
-            pltpu.make_async_copy(
-                sources[1].at[:, pl.ds(pl.multiple_of(index * rows, 16), rows), cols],
-                high.at[side],
-                sems.at[side, 1],
-            )
-        )
     for copy in copies:
         copy.start()
     for copy in copies:
         copy.wait()
     for side in range(2):
-        parts = [(0, rows_low, low[side].astype(F32))]
-        for at in range(high.shape[1]):
-            start = rows_low + at * rows
-            parts.append((start, start + rows, high[side, at].astype(F32)))
-        for start, end, part in parts:
-            if arrived:
-                part = part + arrived[side][start:end, :].astype(F32)
-            outs[side][start:end, :] = part.astype(BF)
+        start = 0
+        for share in shares:
+            _, kinds, rows, _ = share.shape
+            for kind in range(kinds):
+                span = slice(start, start + rows)
+                part = share[side, kind].astype(F32)
+                if arrived:
+                    part = part + arrived[side][span, :].astype(F32)
+                outs[side][span, :] = part.astype(BF)
+                start += rows
 
 
 def pick_chunks(step, indices, sources, arrived):
     copies = indices.shape[0]
-    down_rows = sources[0].shape[0] // copies
-    kinds, span, width = sources[1].shape
-    rows = span // copies
-    half = width // 2
-    if rows % 16 or down_rows % 16:
+    rows = [source.shape[1] // copies for source in sources]
+    half = sources[0].shape[2] // 2
+    if any(count % 16 for count in rows):
         moving = []
         for side in range(2):
-            index = indices[step, side]
-            start = side * half
-            low = lax.dynamic_slice(sources[0], (index * down_rows, start), (down_rows, half))
-            high = lax.dynamic_slice(sources[1], (0, index * rows, start), (kinds, rows, half))
-            part = jnp.concatenate([low.astype(F32), high.astype(F32).reshape(-1, half)])
+            parts = [
+                lax.dynamic_slice(
+                    source,
+                    (0, indices[step, side] * count, side * half),
+                    (source.shape[0], count, half),
+                ).reshape(-1, half)
+                for source, count in zip(sources, rows)
+            ]
+            part = jnp.concatenate([part.astype(F32) for part in parts])
             if arrived:
                 part = part + arrived[side].astype(F32)
             moving.append(part.astype(BF))
         return moving
-    total = down_rows + kinds * rows
+    total = sum(source.shape[0] * count for source, count in zip(sources, rows))
     return pl.pallas_call(
-        functools.partial(pick_kernel, step, 2),
+        functools.partial(pick_kernel, step, len(sources)),
         out_shape=[jax.ShapeDtypeStruct((total, half), BF)] * 2,
         in_specs=[pl.BlockSpec(memory_space=pltpu.SMEM)]
-        + [pl.BlockSpec(memory_space=pl.ANY)] * 2
+        + [pl.BlockSpec(memory_space=pl.ANY)] * len(sources)
         + whole_refs(len(arrived)),
         out_specs=whole_refs(2),
         scratch_shapes=[
-            pltpu.VMEM((2, down_rows, half), sources[0].dtype),
-            pltpu.VMEM((2, kinds, rows, half), sources[1].dtype),
-            pltpu.SemaphoreType.DMA((2, 2)),
-        ],
+            pltpu.VMEM((2, source.shape[0], count, half), source.dtype)
+            for source, count in zip(sources, rows)
+        ]
+        + [pltpu.SemaphoreType.DMA((2, len(sources)))],
         compiler_params=pltpu.CompilerParams(vmem_limit_bytes=8 * 1024 * 1024),
         cost_estimate=NO_COST,
         name="pick_chunks",
     )(indices, *from_hbm(*sources), *arrived)
 
 
-def sum_over_rings(rings, indices, sources):
-    moving = pick_chunks(1, indices, sources, [])
-    for step in range(2, rings[0].count + 1):
-        arrived = [ring.send(chunk) for ring, chunk in zip(rings, moving)]
-        moving = pick_chunks(step % rings[0].count, indices, sources, arrived)
-    return moving
+class RingSum:
+    def __init__(self, rings, indices, sources):
+        self.rings, self.indices, self.sources = rings, indices, sources
+        self.moving = pick_chunks(1, indices, sources, [])
+        self.step = 1
+
+    def advance(self, *earlier):
+        count = self.rings[0].count
+        if self.step == count:
+            return
+        self.step += 1
+        arrived = [ring.send(chunk) for ring, chunk in zip(self.rings, self.moving)]
+        arrived = after(arrived, *earlier)
+        self.moving = pick_chunks(self.step % count, self.indices, self.sources, arrived)
+
+    def finish(self):
+        while self.step < self.rings[0].count:
+            self.advance()
+        return self.moving
 
 
 def place_kernel(step, targets, stores, index_ref, *refs):
@@ -770,14 +778,25 @@
     )
 
 
-def gather_over_rings(rings, indices, chunks, shapes, targets):
-    stores = place_chunks(0, indices, chunks, None, shapes, targets)
-    earlier = []
-    for step in range(1, rings[0].count):
-        chunks = [ring.send(chunk) for ring, chunk in zip(rings, after(chunks, *earlier))]
-        earlier = stores
-        stores = place_chunks(step, indices, chunks, stores, shapes, targets)
-    return stores
+class RingGather:
+    def __init__(self, rings, indices, chunks, shapes, targets):
+        self.rings, self.indices, self.chunks = rings, indices, chunks
+        self.shapes, self.targets = shapes, targets
+        self.stores = place_chunks(0, indices, chunks, None, shapes, targets)
+        self.earlier = []
+        self.step = 0
+
+    def advance(self, steps):
+        while steps and self.step + 1 < self.rings[0].count:
+            steps -= 1
+            self.step += 1
+            held = after(self.chunks, *self.earlier)
+            self.chunks = [ring.send(chunk) for ring, chunk in zip(self.rings, held)]
+            self.earlier = self.stores
+            self.stores = place_chunks(
+                self.step, self.indices, self.chunks, self.stores, self.shapes, self.targets
+            )
+        return self.stores
 
 
 def per_device(
@@ -979,10 +998,13 @@
         after((act_own, act_sib, act_next, act_diag), ffn_grad),
         (dy_own, dy_sib_own, dy_next, dy_diag),
     )
-    ffn_part = lax.psum_scatter(
-        ffn_grad.reshape(4, span, 2 * units), "replica", scatter_dimension=1, tiled=True
-    )
-    dh2_got = after(dh2_got, down_grad)
+    right, left = Ring(1), Ring(-1)
+    rows = span // copies
+    indices = jnp.stack(
+        [jnp.stack([ring.chunk_at(step) for ring in (right, left)]) for step in range(copies)]
+    )
+    unit_sum = RingSum((right, left), indices, [ffn_grad.reshape(4, span, 2 * units)])
+    dh2_got = after(dh2_got, down_grad, *unit_sum.moving)
 
     def chunk_pair(rows):
         parts = rows.reshape(2, span, width)
@@ -996,6 +1018,8 @@
         [F32, BF],
         1,
     )
+    unit_sum.advance(grad_branch)
+    grad_branch = after(grad_branch, *unit_sum.moving)
     grad_branch = grad_branch.reshape(2, span, width)
     branch_even, branch_odd = by_core(grad_branch, swap_core(grad_branch))
     branch_all = jnp.stack([branch_even, branch_odd], 1).reshape(4 * span, width)
@@ -1004,7 +1028,8 @@
     mix_here, mix_there = at_y(mix_grad[:span], mix_grad[span:])
     mix_there = mix_there.astype(BF)
     mix_grad_got = swap_y(mix_there)
-    grad_mixed = after(grad_mixed, mix_there)
+    unit_sum.advance(grad_mixed, mix_there)
+    grad_mixed = after(grad_mixed, mix_there, *unit_sum.moving)
     head_grads = []
     head_gain_part = 0.0
     rows_here = []
@@ -1026,6 +1051,8 @@
             gains,
         )
         head_gain_part = head_gain_part + gain_part
+        unit_sum.advance(grad_heads)
+        grad_heads = after(grad_heads, *unit_sum.moving)
         head_grads.append(grad_heads)
         attn_grad = contract(hidden_one, grad_heads, 0, 0).reshape(2, 2 * span, -1)
         here, there = at_y(attn_grad[0], attn_grad[1])
@@ -1055,11 +1082,6 @@
     own_here, own_there = chunk_pair(out_own)
     next_here, next_there = chunk_pair(out_next)
     out_back = swap_y(jnp.stack([own_there, next_there]).astype(BF))
-    right, left = Ring(1), Ring(-1)
-    rows = span // copies
-    indices = jnp.stack(
-        [jnp.stack([ring.chunk_at(step) for ring in (right, left)]) for step in range(copies)]
-    )
     half = width // 2
     head_sum = jnp.stack(
         [
@@ -1069,7 +1091,10 @@
             mix_here + mix_grad_got.astype(F32),
         ]
     )
-    sums_right, sums_left = sum_over_rings((right, left), indices, (down_grad, head_sum))
+    sums_right, sums_left = RingSum(
+        (right, left), indices, [down_grad[None], head_sum]
+    ).finish()
+    gate_part, up_part = unit_sum.finish()
     down_rows = units // copies
 
     def all_heads(part):
@@ -1079,24 +1104,21 @@
         return jnp.concatenate([part[:down_rows], *both, part[down_rows + 2 * rows :]])
 
     def own_rows(part):
-        parts = part.reshape(2, 2, rows, 2 * units)
+        parts = part.reshape(2, 2, rows, units)
         mine, other = at_core(parts[:, 0], parts[:, 1])
         both_cores = jnp.stack(by_core(mine, swap_core(other)), 1)
         here, there = at_y(both_cores[0], both_cores[1])
         all_units = by_y(here, swap_y(there))
-        blocks = [block[at] for block in all_units for at in range(2)]
-        return [
-            jnp.concatenate([block[:, start : start + units] for block in blocks], 1)
-            for start in (0, units)
-        ]
-
-    w_gate_grad, w_up_grad = gather_over_rings(
+        return jnp.concatenate([block[at] for block in all_units for at in range(2)], 1)
+
+    units_gather = RingGather(
         (right, left),
         indices,
-        own_rows(ffn_part),
+        [own_rows(gate_part), own_rows(up_part)],
         [w_gate.shape, w_up.shape],
         [(side, side, (0, rows), (0, 4 * units), 0) for side in range(2)],
     )
+    sums_right, sums_left = after((sums_right, sums_left), units_gather.advance(copies // 2 - 1))
     targets = []
     for side in range(2):
         targets.append((0, side, (0, down_rows), (0, half), side * half))
@@ -1111,13 +1133,15 @@
             ]
         top = down_rows + 2 * rows
         targets.append((4, side, (top, top + rows), (0, half), side * half))
-    w_down_grad, w_query_grad, w_key_grad, w_value_grad, w_out_grad = gather_over_rings(
+    heads_gather = RingGather(
         (right, left),
         indices,
         [all_heads(sums_right), all_heads(sums_left)],
         [value.shape for value in (w_down, w_query, w_key, w_value, w_out)],
         targets,
     )
+    w_gate_grad, w_up_grad = units_gather.advance(copies)
+    w_down_grad, w_query_grad, w_key_grad, w_value_grad, w_out_grad = heads_gather.advance(copies)
 
     sums = jnp.concatenate([attn_gain_part, ffn_gain_part[0], head_gain_part.T.reshape(-1)])
     sums = after(sums.reshape(-1, 128), sums_right)

time: 473 us -> 444 us (0.939); the launches traced: 471 us -> 435 us
  waiting for transfers between devices: 124 us -> 79.4 us
  starting transfers between devices: 71.3 us -> 87.8 us
  between operations: 15.7 us -> 2.66 us
  Pallas kernels: 191 us -> 202 us
    ppermute x42 -> x56, waiting for transfers between devices: 67.3 us -> 35.9 us  [send(): return lax.ppermute(value, 'replica', self.hops)]
    pallas_call x8 -> x16, Pallas kernels: 15.2 us -> 30 us  [pick_chunks(): pl.pallas_call(functools.partial(pick_kernel, step, len(sources)), out_sh...]
    ppermute x42 -> x56, starting transfers between devices: 43.6 us -> 57.1 us  [send(): return lax.ppermute(value, 'replica', self.hops)]
    pallas_call x1, Pallas kernels: 38.6 us -> 26.8 us  [attention_forward(): pl.pallas_call(forward_kernel, out_shape=[in_hbm(shape, kind) for shape,...]
    pallas_call x2, Pallas kernels: 39 us -> 47.2 us  [feed_forward(): pl.pallas_call(feed_forward_kernel, out_shape=[in_hbm(shape, kind) for sh...]
    ppermute x14 -> x15, waiting for transfers between devices: 26.9 us -> 19.8 us  [swap_y(): return lax.ppermute(value, 'group', Y_SWAP)]
    ppermute x14 -> x15, starting transfers between devices: 14.6 us -> 20.1 us  [swap_y(): return lax.ppermute(value, 'group', Y_SWAP)]
    ppermute x20 -> x21, waiting for transfers between devices: 16.1 us -> 12.7 us  [swap_core(): return lax.ppermute(value, 'group', CORE_SWAP)]
  transfers between devices with their start and end apart: 85 -> 100, of which waited for: 42 -> 43; matrix products, arithmetic and copies ran while one was open for 13% -> 13% of each run, Pallas kernels for 35% -> 39%
where the time goes in v4:
time: 444 us; the launch traced here: 435 us
  Pallas kernels  202 us (45%)
  starting transfers between devices  87.8 us (20%)
  waiting for transfers between devices  79.4 us (18%)
  other arithmetic  37.2 us (8%)
  matrix products  14.7 us (3%)
  local copies, waits for them, and re-layouts  11.7 us (3%)
    ppermute x56, starting transfers between devices, send(): return lax.ppermute(value, 'replica', self.hops)  57.1 us
    pallas_call x2, Pallas kernels, feed_forward(): pl.pallas_call(feed_forward_kernel, out_shape=[in_hbm(shape, kind) for sh...  47.2 us
    ppermute x56, waiting for transfers between devices, send(): return lax.ppermute(value, 'replica', self.hops)  35.9 us
    pallas_call x16, Pallas kernels, pick_chunks(): pl.pallas_call(functools.partial(pick_kernel, step, len(sources)), out_sh...  30 us
    pallas_call x2, Pallas kernels, attention_backward(): pl.pallas_call(functools.partial(backward_kernel, half), grid=(1,), out_s...  27.8 us
    pallas_call x2, Pallas kernels, weight_grad(): pl.pallas_call(functools.partial(weight_grad_kernel, count), grid=(width...  27.6 us
    pallas_call x16, Pallas kernels, place_chunks(): pl.pallas_call(functools.partial(place_kernel, step, targets, len(shapes)...  27 us
    pallas_call x1, Pallas kernels, attention_forward(): pl.pallas_call(forward_kernel, out_shape=[in_hbm(shape, kind) for shape,...  26.8 us
  transfers between devices with their start and end apart: 100, of which 43 were waited for; matrix products, arithmetic and copies ran while one was open for 13% of the time, Pallas kernels for 39%

profile of v4, /device:TPU:0, one launch (start us, length us, event | category | flops | bytes accessed | tf_op | source)
XLA Modules:
  0.0 435.5 jit_solution(6237580517752114697)
XLA Ops:
  0.7 2.1 select_bitcast_fusion.4
  2.7 3.0 collective-permute-start
  8.5 2.2 maximum_select_fusion
  10.6 2.0 collective-permute-start.9
  19.2 2.7 constant_dynamic-slice_fusion.1
  24.0 6.2 %collective-permute-done.9 = bf16[256,1024]{1,0:T(8,128)(2,1)} collective-permute-done((bf16[256,1024]{1,0:T(8,128)(2,1)}, bf16[256,1024]{1,0:T(8,128)(2,1)}, u32[]{:S(2)}, u32[]{:S(2)}) %collective-permute-start.9) | collective-permute-done | bytes 524320 | tf_op jit(solution)/shard_map/ppermute | solution.py:598
  30.2 2.0 collective-permute-start.10
  35.0 7.0 %collective-permute-done.1.piece_0 = bf16[256,1152]{1,0:T(8,128)(2,1)} collective-permute-done((bf16[256,1152]{1,0:T(8,128)(2,1)}, bf16[256,1152]{1,0:T(8,128)(2,1)}, u32[]{:S(2)}, u32[]{:S(2)}) %collective-permute-start.1) | collective-permute-done | bytes 589856 | tf_op jit(solution)/shard_map/ppermute | solution.py:896
  54.8 7.9 %project.1 = (bf16[768,1024]{1,0:T(8,128)(2,1)}, bf16[4,1024,64]{2,1,0:T(8,128)(2,1)}, bf16[1024,256]{1,0:T(8,128)(2,1)}, bf16[256,1024]{1,0:T(8,128)(2,1)}, f32[768,1024]{1,0:T(8,128)}, /*index=5*/f32[16,1024]{1,0:T(8,128)}) custom-call(bf16[1024,1024]{1,0:T(8,128)(2,1)} %fusion.1.hidden_ref, bf16[1024,1024]{1,0:T(8,128)(2,1)} %pad_maximum_fusion.1.weight_ref, ...), custom_call_target="tpu_custom_call" | custom-call | tf_op jit(solution)/shard_map/project/pallas_call | solution.py:285
  63.8 26.8 %attention_forward.1 = (bf16[1024,512]{1,0:T(8,128)(2,1)}, f32[8,1024]{1,0:T(8,128)}, bf16[512,1024]{1,0:T(8,128)(2,1)}, f32[512,1024]{1,0:T(8,128)}, bf16[512,1024]{1,0:T(8,128)(2,1)}) custom-call(bf16[768,1024]{1,0:T(8,128)(2,1)} %get-tuple-element.255.rot_ref.query_ref.key_t_ref, bf16[4,1024,64]{2,1,0:T(8,128)(2,1)} %get-tuple-element.256.key_ref, ...), custom_call_target="tpu_custom_call" | custom-call | tf_op jit(solution)/shard_map/attention_forward/pallas_call | solution.py:306
  93.6 3.1 middle.1
  101.2 19.3 %feed_forward.2 = (bf16[512,1152]{1,0:T(8,128)(2,1)}, bf16[512,1152]{1,0:T(8,128)(2,1)}, bf16[512,2304]{1,0:T(8,128)(2,1)}, bf16[512,2304]{1,0:T(8,128)(2,1)}, f...) custom-call(s32[14]{0:T(128)S(1)} %stack.310.at_ref, ...), custom_call_target="tpu_custom_call" | custom-call | tf_op jit(solution)/shard_map/feed_forward/pallas_call | solution.py:529
  120.7 2.2 collective-permute-done.19.h2_a.refs_2_
  123.7 2.8 collective-permute-done.21.h2_b.refs_3_
  126.5 28.0 %feed_forward.3 = (bf16[512,1152]{1,0:T(8,128)(2,1)}, bf16[512,1152]{1,0:T(8,128)(2,1)}, bf16[512,2304]{1,0:T(8,128)(2,1)}, bf16[512,2304]{1,0:T(8,128)(2,1)}, f...) custom-call(s32[14]{0:T(128)S(1)} %stack.312.at_ref, ...), custom_call_target="tpu_custom_call" | custom-call | tf_op jit(solution)/shard_map/feed_forward/pallas_call | solution.py:529
  154.6 2.7 collective-permute-done.22
  157.4 3.0 add_convert_fusion
  162.0 16.9 %weight_grad.2 = bf16[1024,2304]{1,0:T(8,128)(2,1)} custom-call(bf16[512,1024]{1,0:T(8,128)(2,1)} %get-tuple-element.266.h2_a.refs_0_, bf16[512,1024]{1,0:T(8,128)(2,1)} %copy-done.12, bf16[512,1024]{1,0:T(8,128)(2,1)} %collective-permute-done.19.h2_a.refs_2_, bf16[512,1024]{1,0:T(8,128)(2,1)} %collective-permute-done.21.h2_b.refs_3_, ...), custom_call_target="tpu_custom_call" | custom-call | tf_op jit(solution)/shard_map/weight_grad/pallas_call | solution.py:574
  182.7 10.7 %weight_grad.3 = bf16[1152,1024]{1,0:T(8,128)(2,1)} custom-call(bf16[512,1152]{1,0:T(8,128)(2,1)} %get-tuple-element.328.refs_0_, bf16[512,1152]{1,0:T(8,128)(2,1)} %get-tuple-element.329.refs_1_, bf16[512,1152]{1,0:T(8,128)(2,1)} %get-tuple-element.330.refs_2_, bf16[512,1152]{1,0:T(8,128)(2,1)} %get-tuple-element.331.refs_3_, ...), custom_call_target="tpu_custom_call" | custom-call | tf_op jit(solution)/shard_map/weight_grad/pallas_call | solution.py:574
  193.4 4.6 %middle_grad.1 = (f32[512,1024]{1,0:T(8,128)}, bf16[512,1024]{1,0:T(8,128)(2,1)}, f32[1,1024]{1,0:T(1,128)S(1)}) custom-call(f32[512,1024]{1,0:T(8,128)} %get-tuple-element.275.own_ref, bf16[512,1024]{1,0:T(8,128)(2,1)S(1)} %collective-permute-done.20.sib_ref, bf16[512,1024]{1,0:T(8,128)(2,1)} %collective-permute-done.23.got_ref, ...), custom_call_target="tpu_custom_call" | custom-call | tf_op jit(solution)/shard_map/middle_grad/pallas_call | solution.py:330
  205.4 2.3 convolution_convert_fusion.2.grad_ref
  210.7 1.8 pick_chunks.18
  215.1 13.8 %attention_backward.2 = (bf16[1024,512]{1,0:T(8,128)(2,1)}, f32[64,2]{1,0:T(8,128)S(1)}) custom-call(bf16[1024,512]{1,0:T(8,128)(2,1)} %convolution_convert_fusion.2.grad_ref, bf16[768,1024]{1,0:T(8,128)(2,1)} %get-tuple-element.255.rot_ref.query_ref.key_t_ref, bf16[768,1024]{1,0:T(8,128)(2,1)} %get-tuple-element.255.rot_ref.query_ref.key_t_ref, ...), custom_call_target="tpu_custom_call" | custom-call | tf_op jit(solution)/shard_map/attention_backward/pallas_call | solution.py:372
  228.9 2.1 pick_chunks.19
  236.1 14.0 %attention_backward.3 = (bf16[1024,512]{1,0:T(8,128)(2,1)}, f32[64,2]{1,0:T(8,128)S(1)}) custom-call(bf16[1024,512]{1,0:T(8,128)(2,1)} %convolution_convert_fusion.2.grad_ref, bf16[768,1024]{1,0:T(8,128)(2,1)} %get-tuple-element.255.rot_ref.query_ref.key_t_ref, bf16[768,1024]{1,0:T(8,128)(2,1)} %get-tuple-element.255.rot_ref.query_ref.key_t_ref, ...), custom_call_target="tpu_custom_call" | custom-call | tf_op jit(solution)/shard_map/attention_backward/pallas_call | solution.py:372
  250.4 1.8 pick_chunks.20
  256.3 2.4 fusion.2
  268.3 2.1 pad_maximum_fusion.refs_1_
  270.4 1.8 pick_chunks.21
  280.1 2.2 collective-permute-done.42.refs_3_
  282.3 1.9 pick_chunks.22
  286.9 1.8 pick_chunks.31
  292.3 1.9 pick_chunks.23
  299.5 2.9 collective-permute-done.64
  303.9 3.5 collective-permute-done.62
  309.7 1.9 pick_chunks.24
  315.3 4.5 %collective-permute-done.47.refs_2_ = bf16[240,512]{1,0:T(8,128)(2,1)S(1)} collective-permute-done((bf16[240,512]{1,0:T(8,128)(2,1)S(1)}, bf16[240,512]{1,0:T(8,128)(2,1)S(1)}, u32[]{:S(2)}, u32[]{:S(2)}) %collective-permute-start.47) | collective-permute-done | bytes 245792 | tf_op jit(solution)/shard_map/ppermute | solution.py:632
  321.3 1.9 pick_chunks.25
  329.2 2.9 collective-permute-done.49.refs_2_
  333.8 1.9 pick_chunks.26
  345.1 1.9 pick_chunks.27
  354.3 1.9 pick_chunks.28
  362.4 3.7 collective-permute-done.78.refs_0_
  376.7 5.0 %collective-permute-done.37 = bf16[256,1024]{1,0:T(8,128)(2,1)S(1)} collective-permute-done((bf16[256,1024]{1,0:T(8,128)(2,1)S(1)}, bf16[256,1024]{1,0:T(8,128)(2,1)S(1)}, u32[]{:S(2)}, u32[]{:S(2)}) %collective-permute-start.37) | collective-permute-done | bytes 524320 | tf_op jit(solution)/shard_map/ppermute | solution.py:598
  402.8 4.0 collective-permute-done.74
  409.8 1.8 collective-permute-start.97
  419.6 2.1 collective-permute-start.98
  424.9 2.1 collective-permute-start.90
  (399 shorter events, 185.8 us)
Async XLA Ops:
  2.7 29.5 %collective-permute-start = (bf16[256,1024]{1,0:T(8,128)(2,1)}, bf16[256,1024]{1,0:T(8,128)(2,1)}, u32[]{:S(2)}, u32[]{:S(2)}) collective-permute-start(bf16[256,1024]{1,0:T(8,128)(2,1)} %select_bitcast_fusion.4), channel_id=1, source_target_pairs={{0,2},{2,0},{1,3},{3,1},{4,6},{6,4},{5,7},{7,5},{8,10},{10,8},{9,1... | collective-permute-start | bytes 1572872 | tf_op jit(solution)/shard_map/ppermute | solution.py:598
  8.4 13.7 %collective-permute-start.6 = (f32[6,256]{1,0:T(8,128)S(1)}, f32[6,256]{1,0:T(8,128)S(1)}, u32[]{:S(2)}, u32[]{:S(2)}) collective-permute-start(f32[6,256]{1,0:T(8,128)S(1)} %pad_maximum_fusion.19), channel_id=1, source_target_pairs={{0,2},{2,0},{1,3},{3,1},{4,6},{6,4},{5,7},{7,5},{8,10},{10,8},{9,1... | collective-permute-start | bytes 18440 | tf_op jit(solution)/shard_map/ppermute | solution.py:598
  10.6 19.5 %collective-permute-start.9 = (bf16[256,1024]{1,0:T(8,128)(2,1)}, bf16[256,1024]{1,0:T(8,128)(2,1)}, u32[]{:S(2)}, u32[]{:S(2)}) collective-permute-start(bf16[256,1024]{1,0:T(8,128)(2,1)} %maximum_select_fusion), channel_id=1, source_target_pairs={{0,2},{2,0},{1,3},{3,1},{4,6},{6,4},{5,7},{7,5},{8,10},{10,8},{9,1... | collective-permute-start | bytes 1572872 | tf_op jit(solution)/shard_map/ppermute | solution.py:598
  19.1 14.7 %collective-permute-start.8 = (bf16[256,1024]{1,0:T(8,128)(2,1)}, bf16[256,1024]{1,0:T(8,128)(2,1)}, u32[]{:S(2)}, u32[]{:S(2)}) collective-permute-start(bf16[256,1024]{1,0:T(8,128)(2,1)} %broadcast_select_fusion.8), channel_id=1, source_target_pairs={{0,1},{1,0},{2,3},{3,2},{4,5},{5,4},{6,7},{7,6},{8,9},{9,8},{10,11... | collective-permute-start | bytes 1572872 | tf_op jit(solution)/shard_map/ppermute | solution.py:606
  21.9 20.1 %collective-permute-start.1 = (bf16[256,1152]{1,0:T(8,128)(2,1)}, bf16[256,1152]{1,0:T(8,128)(2,1)}, u32[]{:S(2)}, u32[]{:S(2)}) collective-permute-start(bf16[256,1152]{1,0:T(8,128)(2,1)} %get-tuple-element.474), channel_id=1, source_target_pairs={{0,2},{1,3},{2,0},{3,1},{4,6},{5,7},{6,4},{7,5},{8,11},{9,10},{10,... | collective-permute-start | bytes 1769480 | tf_op jit(solution)/shard_map/ppermute | solution.py:896
  30.2 15.6 %collective-permute-start.10 = (bf16[256,1024]{1,0:T(8,128)(2,1)}, bf16[256,1024]{1,0:T(8,128)(2,1)S(1)}, u32[]{:S(2)}, u32[]{:S(2)}) collective-permute-start(bf16[256,1024]{1,0:T(8,128)(2,1)} %collective-permute-done.9), channel_id=1, source_target_pairs={{0,4},{4,0},{8,12},{12,8},{16,20},{20,16},{24,28},{28,24},{1,5},{5... | collective-permute-start | bytes 1572872 | tf_op jit(solution)/shard_map/ppermute | solution.py:865
  33.8 14.0 %collective-permute-start.5 = (bf16[2,256,1024]{2,1,0:T(8,128)(2,1)S(1)}, bf16[2,256,1024]{2,1,0:T(8,128)(2,1)S(1)}, u32[]{:S(2)}, u32[]{:S(2)}) collective-permute-start(bf16[2,256,1024]{2,1,0:T(8,128)(2,1)S(1)} %pad_maximum_fusion.6), channel_id=1, source_target_pairs={{0,1},{1,0},{2,3},{3,2},{4,5},{5,4},{6,7},{7,6},{8,9},{9,8},{10,11... | collective-permute-start | bytes 3145736 | tf_op jit(solution)/shard_map/ppermute | solution.py:606
  42.0 20.8 %collective-permute-start.4 = (bf16[256,1024]{1,0:T(8,128)(2,1)S(1)}, bf16[256,1024]{1,0:T(8,128)(2,1)S(1)}, u32[]{:S(2)}, u32[]{:S(2)}) collective-permute-start(bf16[256,1024]{1,0:T(8,128)(2,1)S(1)} %copy-done.29), channel_id=1, source_target_pairs={{0,2},{2,0},{1,3},{3,1},{4,6},{6,4},{5,7},{7,5},{8,10},{10,8},{9,1... | collective-permute-start | bytes 1572872 | tf_op jit(solution)/shard_map/ppermute | solution.py:598
  43.7 46.9 %collective-permute-start.13 = (bf16[2,256,1024]{2,1,0:T(8,128)(2,1)}, bf16[2,256,1024]{2,1,0:T(8,128)(2,1)}, u32[]{:S(2)}, u32[]{:S(2)}) collective-permute-start(bf16[2,256,1024]{2,1,0:T(8,128)(2,1)} %dy_a.3), channel_id=1, source_target_pairs={{0,2},{2,0},{1,3},{3,1},{4,6},{6,4},{5,7},{7,5},{8,10},{10,8},{9,1... | collective-permute-start | bytes 3145736 | tf_op jit(solution)/shard_map/ppermute | solution.py:598
  44.0 18.8 %collective-permute-start.2 = (bf16[256,1152]{1,0:T(8,128)(2,1)}, bf16[256,1152]{1,0:T(8,128)(2,1)S(1)}, u32[]{:S(2)}, u32[]{:S(2)}) collective-permute-start(bf16[256,1152]{1,0:T(8,128)(2,1)} %collective-permute-done.1.piece_0), channel_id=1, source_target_pairs={{0,4},{4,0},{8,12},{12,8},{16,20},{20,16},{24,28},{28,24},{1,5},{5... | collective-permute-start | bytes 1769480 | tf_op jit(solution)/shard_map/ppermute | solution.py:865
  45.7 17.1 %collective-permute-start.3 = (bf16[256,1152]{1,0:T(8,128)(2,1)}, bf16[256,1152]{1,0:T(8,128)(2,1)}, u32[]{:S(2)}, u32[]{:S(2)}) collective-permute-start(bf16[256,1152]{1,0:T(8,128)(2,1)} %collective-permute-done.1.piece_0), channel_id=1, source_target_pairs={{0,8},{4,12},{8,0},{12,4},{16,24},{20,28},{24,16},{28,20},{1,9},{5... | collective-permute-start | bytes 1769480 | tf_op jit(solution)/shard_map/ppermute | solution.py:865
  62.8 27.8 %collective-permute-start.12 = (bf16[256,1152]{1,0:T(8,128)(2,1)}, bf16[256,1152]{1,0:T(8,128)(2,1)S(1)}, u32[]{:S(2)}, u32[]{:S(2)}) collective-permute-start(bf16[256,1152]{1,0:T(8,128)(2,1)} %collective-permute-done.3.piece_2), channel_id=1, source_target_pairs={{0,4},{4,0},{8,12},{12,8},{16,20},{20,16},{24,28},{28,24},{1,5},{5... | collective-permute-start | bytes 1769480 | tf_op jit(solution)/shard_map/ppermute | solution.py:865
  97.3 25.6 %collective-permute-start.19 = (bf16[512,1024]{1,0:T(8,128)(2,1)}, bf16[512,1024]{1,0:T(8,128)(2,1)}, u32[]{:S(2)}, u32[]{:S(2)}) collective-permute-start(bf16[512,1024]{1,0:T(8,128)(2,1)} %get-tuple-element.266.h2_a.refs_0_), channel_id=1, source_target_pairs={{0,2},{2,0},{1,3},{3,1},{4,6},{6,4},{5,7},{7,5},{8,10},{10,8},{9,1... | collective-permute-start | bytes 3145736 | tf_op jit(solution)/shard_map/ppermute | solution.py:598
  160.3 33.0 %collective-permute-start.23 = (bf16[512,1024]{1,0:T(8,128)(2,1)}, bf16[512,1024]{1,0:T(8,128)(2,1)}, u32[]{:S(2)}, u32[]{:S(2)}) collective-permute-start(bf16[512,1024]{1,0:T(8,128)(2,1)} %add_convert_fusion), channel_id=1, source_target_pairs={{0,2},{2,0},{1,3},{3,1},{4,6},{6,4},{5,7},{7,5},{8,10},{10,8},{9,1... | collective-permute-start | bytes 3145736 | tf_op jit(solution)/shard_map/ppermute | solution.py:598
  180.6 17.4 %collective-permute-start.24 = (bf16[128,1152]{1,0:T(8,128)(2,1)S(1)}, bf16[128,1152]{1,0:T(8,128)(2,1)S(1)}, u32[]{:S(2)}, u32[]{:S(2)}) collective-permute-start(bf16[128,1152]{1,0:T(8,128)(2,1)S(1)} %get-tuple-element.294), channel_id=1, source_target_pairs={{0,8},{8,16},{16,24},{24,28},{28,20},{20,12},{12,4},{4,0},{1,9},{9... | collective-permute-start | bytes 884744 | tf_op jit(solution)/shard_map/ppermute | solution.py:632
  182.2 15.8 %collective-permute-start.25 = (bf16[128,1152]{1,0:T(8,128)(2,1)S(1)}, bf16[128,1152]{1,0:T(8,128)(2,1)S(1)}, u32[]{:S(2)}, u32[]{:S(2)}) collective-permute-start(bf16[128,1152]{1,0:T(8,128)(2,1)S(1)} %get-tuple-element.295), channel_id=1, source_target_pairs={{4,12},{12,20},{20,28},{28,24},{24,16},{16,8},{8,0},{0,4},{5,13},{... | collective-permute-start | bytes 884744 | tf_op jit(solution)/shard_map/ppermute | solution.py:632
  212.5 16.4 %collective-permute-start.29 = (bf16[128,1152]{1,0:T(8,128)(2,1)S(1)}, bf16[128,1152]{1,0:T(8,128)(2,1)S(1)}, u32[]{:S(2)}, u32[]{:S(2)}) collective-permute-start(bf16[128,1152]{1,0:T(8,128)(2,1)S(1)} %get-tuple-element.306), channel_id=1, source_target_pairs={{0,8},{8,16},{16,24},{24,28},{28,20},{20,12},{12,4},{4,0},{1,9},{9... | collective-permute-start | bytes 884744 | tf_op jit(solution)/shard_map/ppermute | solution.py:632
  214.1 14.8 %collective-permute-start.30 = (bf16[128,1152]{1,0:T(8,128)(2,1)S(1)}, bf16[128,1152]{1,0:T(8,128)(2,1)S(1)}, u32[]{:S(2)}, u32[]{:S(2)}) collective-permute-start(bf16[128,1152]{1,0:T(8,128)(2,1)S(1)} %get-tuple-element.307), channel_id=1, source_target_pairs={{4,12},{12,20},{20,28},{28,24},{24,16},{16,8},{8,0},{0,4},{5,13},{... | collective-permute-start | bytes 884744 | tf_op jit(solution)/shard_map/ppermute | solution.py:632
  214.6 35.5 %collective-permute-start.40 = (bf16[256,1024]{1,0:T(8,128)(2,1)S(1)}, bf16[256,1024]{1,0:T(8,128)(2,1)S(1)}, u32[]{:S(2)}, u32[]{:S(2)}) collective-permute-start(bf16[256,1024]{1,0:T(8,128)(2,1)S(1)} %select_convert_fusion.8), channel_id=1, source_target_pairs={{0,2},{2,0},{1,3},{3,1},{4,6},{6,4},{5,7},{7,5},{8,10},{10,8},{9,1... | collective-permute-start | bytes 1572872 | tf_op jit(solution)/shard_map/ppermute | solution.py:598
  231.1 19.3 %collective-permute-start.31 = (bf16[128,1152]{1,0:T(8,128)(2,1)S(1)}, bf16[128,1152]{1,0:T(8,128)(2,1)S(1)}, u32[]{:S(2)}, u32[]{:S(2)}) collective-permute-start(bf16[128,1152]{1,0:T(8,128)(2,1)S(1)} %get-tuple-element.316), channel_id=1, source_target_pairs={{0,8},{8,16},{16,24},{24,28},{28,20},{20,12},{12,4},{4,0},{1,9},{9... | collective-permute-start | bytes 884744 | tf_op jit(solution)/shard_map/ppermute | solution.py:632
  232.9 17.6 %collective-permute-start.32 = (bf16[128,1152]{1,0:T(8,128)(2,1)S(1)}, bf16[128,1152]{1,0:T(8,128)(2,1)S(1)}, u32[]{:S(2)}, u32[]{:S(2)}) collective-permute-start(bf16[128,1152]{1,0:T(8,128)(2,1)S(1)} %get-tuple-element.317), channel_id=1, source_target_pairs={{4,12},{12,20},{20,28},{28,24},{24,16},{16,8},{8,0},{0,4},{5,13},{... | collective-permute-start | bytes 884744 | tf_op jit(solution)/shard_map/ppermute | solution.py:632
  234.5 28.9 %collective-permute-start.38 = (bf16[512,512]{1,0:T(8,128)(2,1)S(1)}, bf16[512,512]{1,0:T(8,128)(2,1)S(1)}, u32[]{:S(2)}, u32[]{:S(2)}) collective-permute-start(bf16[512,512]{1,0:T(8,128)(2,1)S(1)} %select_convert_fusion.7), channel_id=1, source_target_pairs={{0,2},{2,0},{1,3},{3,1},{4,6},{6,4},{5,7},{7,5},{8,10},{10,8},{9,1... | collective-permute-start | bytes 1572872 | tf_op jit(solution)/shard_map/ppermute | solution.py:598
  252.3 11.5 %collective-permute-start.55 = (bf16[128,1152]{1,0:T(8,128)(2,1)S(1)}, bf16[128,1152]{1,0:T(8,128)(2,1)S(1)}, u32[]{:S(2)}, u32[]{:S(2)}) collective-permute-start(bf16[128,1152]{1,0:T(8,128)(2,1)S(1)} %get-tuple-element.323), channel_id=1, source_target_pairs={{0,8},{8,16},{16,24},{24,28},{28,20},{20,12},{12,4},{4,0},{1,9},{9... | collective-permute-start | bytes 884744 | tf_op jit(solution)/shard_map/ppermute | solution.py:632
  253.9 9.9 %collective-permute-start.56 = (bf16[128,1152]{1,0:T(8,128)(2,1)S(1)}, bf16[128,1152]{1,0:T(8,128)(2,1)S(1)}, u32[]{:S(2)}, u32[]{:S(2)}) collective-permute-start(bf16[128,1152]{1,0:T(8,128)(2,1)S(1)} %get-tuple-element.324), channel_id=1, source_target_pairs={{4,12},{12,20},{20,28},{28,24},{24,16},{16,8},{8,0},{0,4},{5,13},{... | collective-permute-start | bytes 884744 | tf_op jit(solution)/shard_map/ppermute | solution.py:632
  255.7 12.1 %collective-permute-start.39 = (bf16[512,512]{1,0:T(8,128)(2,1)S(1)}, bf16[512,512]{1,0:T(8,128)(2,1)S(1)}, u32[]{:S(2)}, u32[]{:S(2)}) collective-permute-start(bf16[512,512]{1,0:T(8,128)(2,1)S(1)} %select_convert_fusion.3), channel_id=1, source_target_pairs={{0,2},{2,0},{1,3},{3,1},{4,6},{6,4},{5,7},{7,5},{8,10},{10,8},{9,1... | collective-permute-start | bytes 1572872 | tf_op jit(solution)/shard_map/ppermute | solution.py:598
  258.9 89.2 %collective-permute-start.36 = (bf16[512,1024]{1,0:T(8,128)(2,1)S(1)}, bf16[512,1024]{1,0:T(8,128)(2,1)S(1)}, u32[]{:S(2)}, u32[]{:S(2)}) collective-permute-start(bf16[512,1024]{1,0:T(8,128)(2,1)S(1)} %bitcast.357), channel_id=1, source_target_pairs={{0,1},{1,0},{2,3},{3,2},{4,5},{5,4},{6,7},{7,6},{8,9},{9,8},{10,11... | collective-permute-start | bytes 3145736 | tf_op jit(solution)/shard_map/ppermute | solution.py:606
  280.1 16.4 %collective-permute-start.33 = (bf16[512,1024]{1,0:T(8,128)(2,1)S(1)}, bf16[512,1024]{1,0:T(8,128)(2,1)S(1)}, u32[]{:S(2)}, u32[]{:S(2)}) collective-permute-start(bf16[512,1024]{1,0:T(8,128)(2,1)S(1)} %convolution_convert_fusion.1), channel_id=1, source_target_pairs={{0,1},{1,0},{2,3},{3,2},{4,5},{5,4},{6,7},{7,6},{8,9},{9,8},{10,11... | collective-permute-start | bytes 3145736 | tf_op jit(solution)/shard_map/ppermute | solution.py:606
  290.5 22.8 %collective-permute-start.34 = (bf16[512,1024]{1,0:T(8,128)(2,1)S(1)}, bf16[512,1024]{1,0:T(8,128)(2,1)S(1)}, u32[]{:S(2)}, u32[]{:S(2)}) collective-permute-start(bf16[512,1024]{1,0:T(8,128)(2,1)S(1)} %convolution_convert_fusion), channel_id=1, source_target_pairs={{0,1},{1,0},{2,3},{3,2},{4,5},{5,4},{6,7},{7,6},{8,9},{9,8},{10,11... | collective-permute-start | bytes 3145736 | tf_op jit(solution)/shard_map/ppermute | solution.py:606
  294.2 15.1 %collective-permute-start.45 = (bf16[240,512]{1,0:T(8,128)(2,1)S(1)}, bf16[240,512]{1,0:T(8,128)(2,1)S(1)}, u32[]{:S(2)}, u32[]{:S(2)}) collective-permute-start(bf16[240,512]{1,0:T(8,128)(2,1)S(1)} %get-tuple-element.341), channel_id=1, source_target_pairs={{0,8},{8,16},{16,24},{24,28},{28,20},{20,12},{12,4},{4,0},{1,9},{9... | collective-permute-start | bytes 737288 | tf_op jit(solution)/shard_map/ppermute | solution.py:632
  296.0 13.6 %collective-permute-start.46 = (bf16[240,512]{1,0:T(8,128)(2,1)S(1)}, bf16[240,512]{1,0:T(8,128)(2,1)S(1)}, u32[]{:S(2)}, u32[]{:S(2)}) collective-permute-start(bf16[240,512]{1,0:T(8,128)(2,1)S(1)} %get-tuple-element.342), channel_id=1, source_target_pairs={{4,12},{12,20},{20,28},{28,24},{24,16},{16,8},{8,0},{0,4},{5,13},{... | collective-permute-start | bytes 737288 | tf_op jit(solution)/shard_map/ppermute | solution.py:632
  307.6 19.5 %collective-permute-start.65 = (bf16[32,4608]{1,0:T(8,128)(2,1)S(1)}, bf16[32,4608]{1,0:T(8,128)(2,1)S(1)}, u32[]{:S(2)}, u32[]{:S(2)}) collective-permute-start(bf16[32,4608]{1,0:T(8,128)(2,1)S(1)} %pad_maximum_fusion.11.refs_0_), channel_id=1, source_target_pairs={{0,8},{8,16},{16,24},{24,28},{28,20},{20,12},{12,4},{4,0},{1,9},{9... | collective-permute-start | bytes 884744 | tf_op jit(solution)/shard_map/ppermute | solution.py:632
  309.3 17.8 %collective-permute-start.66 = (bf16[32,4608]{1,0:T(8,128)(2,1)S(1)}, bf16[32,4608]{1,0:T(8,128)(2,1)S(1)}, u32[]{:S(2)}, u32[]{:S(2)}) collective-permute-start(bf16[32,4608]{1,0:T(8,128)(2,1)S(1)} %pad_maximum_fusion.12.refs_1_), channel_id=1, source_target_pairs={{4,12},{12,20},{20,28},{28,24},{24,16},{16,8},{8,0},{0,4},{5,13},{... | collective-permute-start | bytes 884744 | tf_op jit(solution)/shard_map/ppermute | solution.py:632
  327.1 13.5 %collective-permute-start.67 = (bf16[32,4608]{1,0:T(8,128)(2,1)S(1)}, bf16[32,4608]{1,0:T(8,128)(2,1)S(1)}, u32[]{:S(2)}, u32[]{:S(2)}) collective-permute-start(bf16[32,4608]{1,0:T(8,128)(2,1)S(1)} %collective-permute-done.65.refs_0_), channel_id=1, source_target_pairs={{0,8},{8,16},{16,24},{24,28},{28,20},{20,12},{12,4},{4,0},{1,9},{9... | collective-permute-start | bytes 884744 | tf_op jit(solution)/shard_map/ppermute | solution.py:632
  328.9 13.4 %collective-permute-start.68 = (bf16[32,4608]{1,0:T(8,128)(2,1)S(1)}, bf16[32,4608]{1,0:T(8,128)(2,1)S(1)}, u32[]{:S(2)}, u32[]{:S(2)}) collective-permute-start(bf16[32,4608]{1,0:T(8,128)(2,1)S(1)} %collective-permute-done.66.refs_1_), channel_id=1, source_target_pairs={{4,12},{12,20},{20,28},{28,24},{24,16},{16,8},{8,0},{0,4},{5,13},{... | collective-permute-start | bytes 884744 | tf_op jit(solution)/shard_map/ppermute | solution.py:632
  340.7 41.8 %collective-permute-start.35 = (bf16[2,256,1024]{2,1,0:T(8,128)(2,1)}, bf16[2,256,1024]{2,1,0:T(8,128)(2,1)}, u32[]{:S(2)}, u32[]{:S(2)}) collective-permute-start(bf16[2,256,1024]{2,1,0:T(8,128)(2,1)} %pad_maximum_fusion.9), channel_id=1, source_target_pairs={{0,2},{2,0},{1,3},{3,1},{4,6},{6,4},{5,7},{7,5},{8,10},{10,8},{9,1... | collective-permute-start | bytes 3145736 | tf_op jit(solution)/shard_map/ppermute | solution.py:598
  369.2 12.6 %collective-permute-start.37 = (bf16[256,1024]{1,0:T(8,128)(2,1)S(1)}, bf16[256,1024]{1,0:T(8,128)(2,1)S(1)}, u32[]{:S(2)}, u32[]{:S(2)}) collective-permute-start(bf16[256,1024]{1,0:T(8,128)(2,1)S(1)} %select_convert_fusion.4), channel_id=1, source_target_pairs={{0,2},{2,0},{1,3},{3,1},{4,6},{6,4},{5,7},{7,5},{8,10},{10,8},{9,1... | collective-permute-start | bytes 1572872 | tf_op jit(solution)/shard_map/ppermute | solution.py:598
  374.5 14.3 %collective-permute-start.82 = (bf16[240,512]{1,0:T(8,128)(2,1)S(1)}, bf16[240,512]{1,0:T(8,128)(2,1)S(1)}, u32[]{:S(2)}, u32[]{:S(2)}) collective-permute-start(bf16[240,512]{1,0:T(8,128)(2,1)S(1)} %collective-permute-done.80.refs_0_), channel_id=1, source_target_pairs={{0,8},{8,16},{16,24},{24,28},{28,20},{20,12},{12,4},{4,0},{1,9},{9... | collective-permute-start | bytes 737288 | tf_op jit(solution)/shard_map/ppermute | solution.py:632
  375.1 13.7 %collective-permute-start.83 = (bf16[240,512]{1,0:T(8,128)(2,1)S(1)}, bf16[240,512]{1,0:T(8,128)(2,1)S(1)}, u32[]{:S(2)}, u32[]{:S(2)}) collective-permute-start(bf16[240,512]{1,0:T(8,128)(2,1)S(1)} %collective-permute-done.81.refs_1_), channel_id=1, source_target_pairs={{4,12},{12,20},{20,28},{28,24},{24,16},{16,8},{8,0},{0,4},{5,13},{... | collective-permute-start | bytes 737288 | tf_op jit(solution)/shard_map/ppermute | solution.py:632
  381.8 10.8 %collective-permute-start.92 = (bf16[32,4608]{1,0:T(8,128)(2,1)S(1)}, bf16[32,4608]{1,0:T(8,128)(2,1)S(1)}, u32[]{:S(2)}, u32[]{:S(2)}) collective-permute-start(bf16[32,4608]{1,0:T(8,128)(2,1)S(1)} %collective-permute-done.69.refs_0_), channel_id=1, source_target_pairs={{0,8},{8,16},{16,24},{24,28},{28,20},{20,12},{12,4},{4,0},{1,9},{9... | collective-permute-start | bytes 884744 | tf_op jit(solution)/shard_map/ppermute | solution.py:632
  382.4 10.2 %collective-permute-start.93 = (bf16[32,4608]{1,0:T(8,128)(2,1)S(1)}, bf16[32,4608]{1,0:T(8,128)(2,1)S(1)}, u32[]{:S(2)}, u32[]{:S(2)}) collective-permute-start(bf16[32,4608]{1,0:T(8,128)(2,1)S(1)} %collective-permute-done.70.refs_1_), channel_id=1, source_target_pairs={{4,12},{12,20},{20,28},{28,24},{24,16},{16,8},{8,0},{0,4},{5,13},{... | collective-permute-start | bytes 884744 | tf_op jit(solution)/shard_map/ppermute | solution.py:632
  392.6 16.9 %collective-permute-start.94 = (bf16[32,4608]{1,0:T(8,128)(2,1)S(1)}, bf16[32,4608]{1,0:T(8,128)(2,1)S(1)}, u32[]{:S(2)}, u32[]{:S(2)}) collective-permute-start(bf16[32,4608]{1,0:T(8,128)(2,1)S(1)} %collective-permute-done.92.refs_0_), channel_id=1, source_target_pairs={{0,8},{8,16},{16,24},{24,28},{28,20},{20,12},{12,4},{4,0},{1,9},{9... | collective-permute-start | bytes 884744 | tf_op jit(solution)/shard_map/ppermute | solution.py:632
  393.7 15.8 %collective-permute-start.95 = (bf16[32,4608]{1,0:T(8,128)(2,1)S(1)}, bf16[32,4608]{1,0:T(8,128)(2,1)S(1)}, u32[]{:S(2)}, u32[]{:S(2)}) collective-permute-start(bf16[32,4608]{1,0:T(8,128)(2,1)S(1)} %collective-permute-done.93.refs_1_), channel_id=1, source_target_pairs={{4,12},{12,20},{20,28},{28,24},{24,16},{16,8},{8,0},{0,4},{5,13},{... | collective-permute-start | bytes 884744 | tf_op jit(solution)/shard_map/ppermute | solution.py:632
  398.3 15.0 %collective-permute-start.86 = (bf16[240,512]{1,0:T(8,128)(2,1)S(1)}, bf16[240,512]{1,0:T(8,128)(2,1)S(1)}, u32[]{:S(2)}, u32[]{:S(2)}) collective-permute-start(bf16[240,512]{1,0:T(8,128)(2,1)S(1)} %collective-permute-done.84.refs_0_), channel_id=1, source_target_pairs={{0,8},{8,16},{16,24},{24,28},{28,20},{20,12},{12,4},{4,0},{1,9},{9... | collective-permute-start | bytes 737288 | tf_op jit(solution)/shard_map/ppermute | solution.py:632
  398.8 14.5 %collective-permute-start.87 = (bf16[240,512]{1,0:T(8,128)(2,1)S(1)}, bf16[240,512]{1,0:T(8,128)(2,1)S(1)}, u32[]{:S(2)}, u32[]{:S(2)}) collective-permute-start(bf16[240,512]{1,0:T(8,128)(2,1)S(1)} %collective-permute-done.85.refs_1_), channel_id=1, source_target_pairs={{4,12},{12,20},{20,28},{28,24},{24,16},{16,8},{8,0},{0,4},{5,13},{... | collective-permute-start | bytes 737288 | tf_op jit(solution)/shard_map/ppermute | solution.py:632
  409.8 9.9 %collective-permute-start.97 = (bf16[32,4608]{1,0:T(8,128)(2,1)S(1)}, bf16[32,4608]{1,0:T(8,128)(2,1)S(1)}, u32[]{:S(2)}, u32[]{:S(2)}) collective-permute-start(bf16[32,4608]{1,0:T(8,128)(2,1)S(1)} %collective-permute-done.95.refs_1_), channel_id=1, source_target_pairs={{4,12},{12,20},{20,28},{28,24},{24,16},{16,8},{8,0},{0,4},{5,13},{... | collective-permute-start | bytes 884744 | tf_op jit(solution)/shard_map/ppermute | solution.py:632
  413.3 11.3 %collective-permute-start.88 = (bf16[240,512]{1,0:T(8,128)(2,1)S(1)}, bf16[240,512]{1,0:T(8,128)(2,1)S(1)}, u32[]{:S(2)}, u32[]{:S(2)}) collective-permute-start(bf16[240,512]{1,0:T(8,128)(2,1)S(1)} %collective-permute-done.86.refs_0_), channel_id=1, source_target_pairs={{0,8},{8,16},{16,24},{24,28},{28,20},{20,12},{12,4},{4,0},{1,9},{9... | collective-permute-start | bytes 737288 | tf_op jit(solution)/shard_map/ppermute | solution.py:632
  413.9 11.0 %collective-permute-start.89 = (bf16[240,512]{1,0:T(8,128)(2,1)S(1)}, bf16[240,512]{1,0:T(8,128)(2,1)S(1)}, u32[]{:S(2)}, u32[]{:S(2)}) collective-permute-start(bf16[240,512]{1,0:T(8,128)(2,1)S(1)} %collective-permute-done.87.refs_1_), channel_id=1, source_target_pairs={{4,12},{12,20},{20,28},{28,24},{24,16},{16,8},{8,0},{0,4},{5,13},{... | collective-permute-start | bytes 737288 | tf_op jit(solution)/shard_map/ppermute | solution.py:632
  419.6 10.2 %collective-permute-start.98 = (bf16[32,4608]{1,0:T(8,128)(2,1)S(1)}, bf16[32,4608]{1,0:T(8,128)(2,1)S(1)}, u32[]{:S(2)}, u32[]{:S(2)}) collective-permute-start(bf16[32,4608]{1,0:T(8,128)(2,1)S(1)} %collective-permute-done.96.refs_0_), channel_id=1, source_target_pairs={{0,8},{8,16},{16,24},{24,28},{28,20},{20,12},{12,4},{4,0},{1,9},{9... | collective-permute-start | bytes 884744 | tf_op jit(solution)/shard_map/ppermute | solution.py:632
  (88 other events, 612.8 us)
